TPU v7x, 256 devices: a whole 4x4x8 slice. The times are simulated.
256 devices in a mesh: rows: 64 (over z, y_lo, x), grp: 4 (over y_hi, core).
Axes of the slice: x: 4, y: 4 (y_hi: 2, y_lo: 2; y = y_hi * 2 + y_lo), z: 8, core: 2. Of those that a mesh axis runs over, the one named last changes fastest.
Arguments:
- tile_values: bfloat16 [8192, 16, 128], P('rows'), may hold values from 0.049804688 to 1
- tile_ids: int32 [8192, 16], P('rows'), may hold values from 0 to 255, as said below
- doc_tiles: int32 [8192], P('rows'), may hold values from 1 to 16
- row_counts: int32 [64], replicated, may hold values from 1 to 128, 4096 in all
Outputs:
- similarity: float32 [4096, 4096], P('rows', 'grp')
Inputs may be any that keep to these rules, and one draw needn't show every extreme that they name: `row_counts`: the entries sum to 4096. `tile_ids`: the 16 entries of a row are distinct.
All inputs are finite; a program needn't handle non-finite values.
Results may differ from a plain program's by a relative error of at most 0.0003.
Values may be sent and summed in bfloat16 or wider, within the bound.
No kernel may reach another device: no remote copies, remote signals or barrier semaphores. Data moves between devices by JAX's collectives and lax.ppermute only.
A program may use at most 64 MiB of HBM per device.

v0:
```python
import jax
import jax.numpy as jnp
from jax import lax
from jax.sharding import PartitionSpec as P

VOCAB = 32768
TILE = 128
LTILES = 16
DOC_DEV = 64


def from_behind(block, axis, distance):
    devices = range(lax.axis_size(axis))
    route = [((i - distance) % len(devices), i) for i in devices]
    return lax.ppermute(block, axis, route)


def densify(values, tile_codes):
    doc_count = values.shape[0]
    tile_count = VOCAB // TILE
    tile_line = jnp.arange(tile_count, dtype=jnp.int32)[None, None, :]
    selector = (tile_codes.astype(jnp.int32)[:, :, None] == tile_line).astype(jnp.bfloat16)
    placed = jnp.einsum("dkt,dki->dti", selector, values, preferred_element_type=jnp.float32)
    return placed.astype(jnp.bfloat16).reshape(doc_count, VOCAB)


def squares(values):
    widened = values.astype(jnp.float32)
    return jnp.sum(widened * widened, axis=(1, 2))


def similar(own_dense, own_norms, values, tile_codes):
    other_dense = densify(values, tile_codes)
    product = lax.dot_general(
        own_dense, other_dense, (((1,), (1,)), ((), ())), preferred_element_type=jnp.float32
    )
    return product / (own_norms[:, None] + squares(values)[None, :] - product)


def forward(values, tile_codes):
    return from_behind((values, tile_codes), "rows", 1)


def deal(tile_values, tile_ids, doc_tiles, row_counts, offsets):
    capacity = tile_values.shape[0]
    rank_count = lax.axis_size("rows")
    here_rank = lax.axis_index("rows")
    slot_count = (capacity + rank_count - 1) // rank_count
    run_ends = jnp.cumsum(row_counts)
    run_starts = run_ends - row_counts
    own_start = run_starts[here_rank]
    own_count = row_counts[here_rank]
    live_mask = jnp.arange(LTILES, dtype=jnp.int32)[None, :] < doc_tiles[:, None]
    masked = jnp.where(live_mask[:, :, None], tile_values, jnp.zeros_like(tile_values))
    target_ids = jnp.arange(rank_count, dtype=jnp.int32)[:, None]
    slot_ids = jnp.arange(slot_count, dtype=jnp.int32)[None, :]
    chosen = (target_ids - own_start) % rank_count + slot_ids * rank_count
    usable = chosen < own_count
    chosen = jnp.where(usable, chosen, 0)
    outgoing = jnp.where(usable[:, :, None, None], masked[chosen], jnp.zeros((), jnp.bfloat16))
    out_codes = tile_ids[chosen].astype(jnp.bfloat16)
    outgoing = jnp.concatenate([jnp.roll(outgoing, offset, axis=0) for offset in offsets], axis=1)
    out_codes = jnp.concatenate([jnp.roll(out_codes, offset, axis=0) for offset in offsets], axis=1)
    incoming, in_codes = (
        lax.all_to_all(outgoing, "rows", split_axis=0, concat_axis=0, tiled=True),
        lax.all_to_all(out_codes, "rows", split_axis=0, concat_axis=0, tiled=True),
    )
    panel_line = jnp.arange(DOC_DEV, dtype=jnp.int32)[:, None]
    panels = []
    for number, offset in enumerate(offsets):
        anchor = (here_rank - offset) % rank_count
        first_row = (anchor - run_starts[:, None]) % rank_count + slot_ids * rank_count
        landed = first_row < row_counts[:, None]
        places = jnp.where(
            landed, (run_starts[:, None] + first_row) // rank_count, DOC_DEV
        ).reshape(-1)
        block_values = incoming[:, number * slot_count : (number + 1) * slot_count].reshape(
            -1, LTILES, TILE
        )
        block_codes = in_codes[:, number * slot_count : (number + 1) * slot_count].reshape(
            -1, LTILES
        )
        placing = (places[None, :] == panel_line).astype(jnp.bfloat16)
        values = jnp.einsum(
            "pn,nki->pki", placing, block_values, preferred_element_type=jnp.float32
        ).astype(jnp.bfloat16)
        codes = jnp.einsum(
            "pn,nk->pk", placing, block_codes, preferred_element_type=jnp.float32
        ).astype(jnp.bfloat16)
        panels.append((values, codes))
    return panels


def on_device(tile_values, tile_ids, doc_tiles, row_counts):
    panel_span = lax.axis_size("rows") // lax.axis_size("grp")
    group_index = lax.axis_index("grp")
    lead_offset = group_index * panel_span
    zero_offset = jnp.zeros((), jnp.int32)
    offsets = [zero_offset, lead_offset]
    panels = deal(tile_values, tile_ids, doc_tiles, row_counts, offsets)
    own_values, own_codes = panels[0]
    own_dense = densify(own_values, own_codes)
    own_norms = squares(own_values)
    output = jnp.zeros((DOC_DEV, panel_span * DOC_DEV), jnp.float32)

    def record(output, column_block, values, codes):
        block = similar(own_dense, own_norms, values, codes)
        return lax.dynamic_update_slice_in_dim(output, block, column_block * DOC_DEV, 1)

    def turn_one(counter, carry):
        output, ahead_values, ahead_codes = carry
        output = record(output, counter, ahead_values, ahead_codes)
        ahead_values, ahead_codes = forward(ahead_values, ahead_codes)
        return (output, ahead_values, ahead_codes)

    start_carry = (output, panels[1][0], panels[1][1])
    output, ahead_values, ahead_codes = lax.fori_loop(0, panel_span - 1, turn_one, start_carry)
    output = record(output, panel_span - 1, ahead_values, ahead_codes)
    return output


def solution(mesh):
    placed = (P("rows", None, None), P("rows", None), P("rows"), P())
    return jax.shard_map(
        on_device, mesh=mesh, in_specs=placed, out_specs=P("rows", "grp"), check_vma=False
    )
```

profile of v0, /device:TPU:16, one launch (start us, length us, event | category | flops | bytes accessed | tf_op | source)
XLA Modules:
  0.0 258.2 jit_solution(4622661325852836392)
XLA Ops:
  7.5 12.7 %all-to-all-start.1 = ((bf16[64,4,16]{2,1,0:T(4,128)(2,1)}), bf16[64,4,16]{2,1,0:T(4,128)(2,1)S(1)}, u32[]{:S(2)}, u32[]{:S(2)}) async-start(bf16[64,4,16]{2,1,0:T(4,128)(2,1)} %pad_maximum_fusion.1), calls=%async_computation.1 | async-start | bytes 131072 | tf_op jit(solution)/shard_map/all_to_all | solution.py:66
  30.7 7.4 %all-to-all-start = ((bf16[64,4,16,128]{3,1,2,0:T(4,128)(2,1)}), bf16[64,4,16,128]{3,1,2,0:T(4,128)(2,1)S(1)}, u32[]{:S(2)}, u32[]{:S(2)}) async-start(bf16[64,4,16,128]{3,1,2,0:T(4,128)(2,1)} %copy.92), calls=%async_computation | async-start | bytes 2097152 | tf_op jit(solution)/shard_map/all_to_all | solution.py:65
  39.9 25.9 %all-to-all-done = bf16[64,4,16,128]{3,1,2,0:T(4,128)(2,1)S(1)} async-done(((bf16[64,4,16,128]{3,1,2,0:T(4,128)(2,1)}), bf16[64,4,16,128]{3,1,2,0:T(4,128)(2,1)S(1)}, u32[]{:S(2)}, u32[]{:S(2)}) %all-to-all-start) | async-done | bytes 1048608 | tf_op jit(solution)/shard_map/all_to_all | solution.py:65
  70.1 4.8 %copy.129 = bf16[8,8,256,128]{3,1,2,0:T(8,128)(2,1)} copy(bf16[8,8,256,128]{3,2,1,0:T(8,128)(2,1)S(1)} %bitcast.57) | data formatting | bytes 8388608
  75.8 172.9 %while.17 = (s32[]{:T(128)}, f32[64,1024]{1,0:T(8,128)S(1)}, bf16[64,16,128]{2,1,0:T(8,128)(2,1)S(1)}, bf16[64,16]{1,0:T(8,128)(2,1)S(1)}, bf16[64,32768]{1,0:T(...) while((s32[]{:T(128)}, f32[64,1024]{1,0:T(8,128)S(1)}, ...), condition=%wide.region_4.9_spmd, body=%wide.region_2.8_spmd.sunk | while | flops 338310080 | bytes 31529984 | solution.py:117
  82.0 4.3 %subtract_divide_fusion.3 = f32[64,64]{1,0:T(8,128)S(1)} fusion(bf16[64,32768]{1,0:T(8,128)(2,1)S(1)} %copy-done.2, bf16[8,8,256,128]{3,2,1,0:T(8,128)(2,1)S(1)} %bitcast.56, f32[64]{0:T(128)S(1)} %multiply_reduce_fusion.4, f32[64]{0:T(128)S(1)} %get-tuple-element.260), kind=kOutput, calls=%fused_computation.10.clone.1 | convolution fusion | flops 268447744 | bytes 8405504 | tf_op jit(solution)/shard_map/while/body/eval_jaxpr/dot_general | solution.py:34
  92.9 4.3 %subtract_divide_fusion.3 = f32[64,64]{1,0:T(8,128)S(1)} fusion(bf16[64,32768]{1,0:T(8,128)(2,1)S(1)} %copy-done.2, bf16[8,8,256,128]{3,2,1,0:T(8,128)(2,1)S(1)} %bitcast.56, f32[64]{0:T(128)S(1)} %multiply_reduce_fusion.4, f32[64]{0:T(128)S(1)} %get-tuple-element.260), kind=kOutput, calls=%fused_computation.10.clone.1 | convolution fusion | flops 268447744 | bytes 8405504 | tf_op jit(solution)/shard_map/while/body/eval_jaxpr/dot_general | solution.py:34
  104.2 4.3 %subtract_divide_fusion.3 = f32[64,64]{1,0:T(8,128)S(1)} fusion(bf16[64,32768]{1,0:T(8,128)(2,1)S(1)} %copy-done.2, bf16[8,8,256,128]{3,2,1,0:T(8,128)(2,1)S(1)} %bitcast.56, f32[64]{0:T(128)S(1)} %multiply_reduce_fusion.4, f32[64]{0:T(128)S(1)} %get-tuple-element.260), kind=kOutput, calls=%fused_computation.10.clone.1 | convolution fusion | flops 268447744 | bytes 8405504 | tf_op jit(solution)/shard_map/while/body/eval_jaxpr/dot_general | solution.py:34
  114.6 4.3 %subtract_divide_fusion.3 = f32[64,64]{1,0:T(8,128)S(1)} fusion(bf16[64,32768]{1,0:T(8,128)(2,1)S(1)} %copy-done.2, bf16[8,8,256,128]{3,2,1,0:T(8,128)(2,1)S(1)} %bitcast.56, f32[64]{0:T(128)S(1)} %multiply_reduce_fusion.4, f32[64]{0:T(128)S(1)} %get-tuple-element.260), kind=kOutput, calls=%fused_computation.10.clone.1 | convolution fusion | flops 268447744 | bytes 8405504 | tf_op jit(solution)/shard_map/while/body/eval_jaxpr/dot_general | solution.py:34
  125.4 4.3 %subtract_divide_fusion.3 = f32[64,64]{1,0:T(8,128)S(1)} fusion(bf16[64,32768]{1,0:T(8,128)(2,1)S(1)} %copy-done.2, bf16[8,8,256,128]{3,2,1,0:T(8,128)(2,1)S(1)} %bitcast.56, f32[64]{0:T(128)S(1)} %multiply_reduce_fusion.4, f32[64]{0:T(128)S(1)} %get-tuple-element.260), kind=kOutput, calls=%fused_computation.10.clone.1 | convolution fusion | flops 268447744 | bytes 8405504 | tf_op jit(solution)/shard_map/while/body/eval_jaxpr/dot_general | solution.py:34
  137.1 4.3 %subtract_divide_fusion.3 = f32[64,64]{1,0:T(8,128)S(1)} fusion(bf16[64,32768]{1,0:T(8,128)(2,1)S(1)} %copy-done.2, bf16[8,8,256,128]{3,2,1,0:T(8,128)(2,1)S(1)} %bitcast.56, f32[64]{0:T(128)S(1)} %multiply_reduce_fusion.4, f32[64]{0:T(128)S(1)} %get-tuple-element.260), kind=kOutput, calls=%fused_computation.10.clone.1 | convolution fusion | flops 268447744 | bytes 8405504 | tf_op jit(solution)/shard_map/while/body/eval_jaxpr/dot_general | solution.py:34
  147.8 4.3 %subtract_divide_fusion.3 = f32[64,64]{1,0:T(8,128)S(1)} fusion(bf16[64,32768]{1,0:T(8,128)(2,1)S(1)} %copy-done.2, bf16[8,8,256,128]{3,2,1,0:T(8,128)(2,1)S(1)} %bitcast.56, f32[64]{0:T(128)S(1)} %multiply_reduce_fusion.4, f32[64]{0:T(128)S(1)} %get-tuple-element.260), kind=kOutput, calls=%fused_computation.10.clone.1 | convolution fusion | flops 268447744 | bytes 8405504 | tf_op jit(solution)/shard_map/while/body/eval_jaxpr/dot_general | solution.py:34
  158.0 4.3 %subtract_divide_fusion.3 = f32[64,64]{1,0:T(8,128)S(1)} fusion(bf16[64,32768]{1,0:T(8,128)(2,1)S(1)} %copy-done.2, bf16[8,8,256,128]{3,2,1,0:T(8,128)(2,1)S(1)} %bitcast.56, f32[64]{0:T(128)S(1)} %multiply_reduce_fusion.4, f32[64]{0:T(128)S(1)} %get-tuple-element.260), kind=kOutput, calls=%fused_computation.10.clone.1 | convolution fusion | flops 268447744 | bytes 8405504 | tf_op jit(solution)/shard_map/while/body/eval_jaxpr/dot_general | solution.py:34
  169.2 4.3 %subtract_divide_fusion.3 = f32[64,64]{1,0:T(8,128)S(1)} fusion(bf16[64,32768]{1,0:T(8,128)(2,1)S(1)} %copy-done.2, bf16[8,8,256,128]{3,2,1,0:T(8,128)(2,1)S(1)} %bitcast.56, f32[64]{0:T(128)S(1)} %multiply_reduce_fusion.4, f32[64]{0:T(128)S(1)} %get-tuple-element.260), kind=kOutput, calls=%fused_computation.10.clone.1 | convolution fusion | flops 268447744 | bytes 8405504 | tf_op jit(solution)/shard_map/while/body/eval_jaxpr/dot_general | solution.py:34
  179.4 4.3 %subtract_divide_fusion.3 = f32[64,64]{1,0:T(8,128)S(1)} fusion(bf16[64,32768]{1,0:T(8,128)(2,1)S(1)} %copy-done.2, bf16[8,8,256,128]{3,2,1,0:T(8,128)(2,1)S(1)} %bitcast.56, f32[64]{0:T(128)S(1)} %multiply_reduce_fusion.4, f32[64]{0:T(128)S(1)} %get-tuple-element.260), kind=kOutput, calls=%fused_computation.10.clone.1 | convolution fusion | flops 268447744 | bytes 8405504 | tf_op jit(solution)/shard_map/while/body/eval_jaxpr/dot_general | solution.py:34
  184.3 4.7 %collective-permute-done.1 = bf16[64,16]{1,0:T(8,128)(2,1)S(1)} collective-permute-done((bf16[64,16]{1,0:T(8,128)(2,1)S(1)}, bf16[64,16]{1,0:T(8,128)(2,1)S(1)}, u32[]{:S(2)}, u32[]{:S(2)}) %collective-permute-start.1) | collective-permute-done | bytes 2080 | tf_op jit(solution)/shard_map/while/body/eval_jaxpr/ppermute | solution.py:15
  192.6 4.3 %subtract_divide_fusion.3 = f32[64,64]{1,0:T(8,128)S(1)} fusion(bf16[64,32768]{1,0:T(8,128)(2,1)S(1)} %copy-done.2, bf16[8,8,256,128]{3,2,1,0:T(8,128)(2,1)S(1)} %bitcast.56, f32[64]{0:T(128)S(1)} %multiply_reduce_fusion.4, f32[64]{0:T(128)S(1)} %get-tuple-element.260), kind=kOutput, calls=%fused_computation.10.clone.1 | convolution fusion | flops 268447744 | bytes 8405504 | tf_op jit(solution)/shard_map/while/body/eval_jaxpr/dot_general | solution.py:34
  197.3 5.2 %collective-permute-done.1 = bf16[64,16]{1,0:T(8,128)(2,1)S(1)} collective-permute-done((bf16[64,16]{1,0:T(8,128)(2,1)S(1)}, bf16[64,16]{1,0:T(8,128)(2,1)S(1)}, u32[]{:S(2)}, u32[]{:S(2)}) %collective-permute-start.1) | collective-permute-done | bytes 2080 | tf_op jit(solution)/shard_map/while/body/eval_jaxpr/ppermute | solution.py:15
  206.0 4.3 %subtract_divide_fusion.3 = f32[64,64]{1,0:T(8,128)S(1)} fusion(bf16[64,32768]{1,0:T(8,128)(2,1)S(1)} %copy-done.2, bf16[8,8,256,128]{3,2,1,0:T(8,128)(2,1)S(1)} %bitcast.56, f32[64]{0:T(128)S(1)} %multiply_reduce_fusion.4, f32[64]{0:T(128)S(1)} %get-tuple-element.260), kind=kOutput, calls=%fused_computation.10.clone.1 | convolution fusion | flops 268447744 | bytes 8405504 | tf_op jit(solution)/shard_map/while/body/eval_jaxpr/dot_general | solution.py:34
  210.9 4.2 %collective-permute-done.1 = bf16[64,16]{1,0:T(8,128)(2,1)S(1)} collective-permute-done((bf16[64,16]{1,0:T(8,128)(2,1)S(1)}, bf16[64,16]{1,0:T(8,128)(2,1)S(1)}, u32[]{:S(2)}, u32[]{:S(2)}) %collective-permute-start.1) | collective-permute-done | bytes 2080 | tf_op jit(solution)/shard_map/while/body/eval_jaxpr/ppermute | solution.py:15
  218.7 4.3 %subtract_divide_fusion.3 = f32[64,64]{1,0:T(8,128)S(1)} fusion(bf16[64,32768]{1,0:T(8,128)(2,1)S(1)} %copy-done.2, bf16[8,8,256,128]{3,2,1,0:T(8,128)(2,1)S(1)} %bitcast.56, f32[64]{0:T(128)S(1)} %multiply_reduce_fusion.4, f32[64]{0:T(128)S(1)} %get-tuple-element.260), kind=kOutput, calls=%fused_computation.10.clone.1 | convolution fusion | flops 268447744 | bytes 8405504 | tf_op jit(solution)/shard_map/while/body/eval_jaxpr/dot_general | solution.py:34
  230.4 4.3 %subtract_divide_fusion.3 = f32[64,64]{1,0:T(8,128)S(1)} fusion(bf16[64,32768]{1,0:T(8,128)(2,1)S(1)} %copy-done.2, bf16[8,8,256,128]{3,2,1,0:T(8,128)(2,1)S(1)} %bitcast.56, f32[64]{0:T(128)S(1)} %multiply_reduce_fusion.4, f32[64]{0:T(128)S(1)} %get-tuple-element.260), kind=kOutput, calls=%fused_computation.10.clone.1 | convolution fusion | flops 268447744 | bytes 8405504 | tf_op jit(solution)/shard_map/while/body/eval_jaxpr/dot_general | solution.py:34
  241.3 4.3 %subtract_divide_fusion.3 = f32[64,64]{1,0:T(8,128)S(1)} fusion(bf16[64,32768]{1,0:T(8,128)(2,1)S(1)} %copy-done.2, bf16[8,8,256,128]{3,2,1,0:T(8,128)(2,1)S(1)} %bitcast.56, f32[64]{0:T(128)S(1)} %multiply_reduce_fusion.4, f32[64]{0:T(128)S(1)} %get-tuple-element.260), kind=kOutput, calls=%fused_computation.10.clone.1 | convolution fusion | flops 268447744 | bytes 8405504 | tf_op jit(solution)/shard_map/while/body/eval_jaxpr/dot_general | solution.py:34
  252.0 4.7 %subtract_divide_fusion.1 = f32[64,64]{1,0:T(8,128)S(1)} fusion(bf16[64,256,128]{2,1,0:T(8,128)(2,1)S(1)} %convolution_convert_fusion.1, bf16[64,256,128]{2,1,0:T(8,128)(2,1)S(1)} %copy-done.1, f32[64]{0:T(128)S(1)} %multiply_reduce_fusion.1, f32[64]{0:T(128)S(1)} %get-tuple-element.271), kind=kOutput, calls=%fused_computation.42 | convolution fusion | flops 268447744 | bytes 8405504 | tf_op jit(solution)/shard_map/dot_general | solution.py:34
  (237 shorter events, 123.1 us)
Async XLA Ops:
  7.5 23.2 %all-to-all-start.1 = ((bf16[64,4,16]{2,1,0:T(4,128)(2,1)}), bf16[64,4,16]{2,1,0:T(4,128)(2,1)S(1)}, u32[]{:S(2)}, u32[]{:S(2)}) async-start(bf16[64,4,16]{2,1,0:T(4,128)(2,1)} %pad_maximum_fusion.1), calls=%async_computation.1 | async-start | bytes 131072 | tf_op jit(solution)/shard_map/all_to_all | solution.py:66
  30.7 35.1 %all-to-all-start = ((bf16[64,4,16,128]{3,1,2,0:T(4,128)(2,1)}), bf16[64,4,16,128]{3,1,2,0:T(4,128)(2,1)S(1)}, u32[]{:S(2)}, u32[]{:S(2)}) async-start(bf16[64,4,16,128]{3,1,2,0:T(4,128)(2,1)} %copy.92), calls=%async_computation | async-start | bytes 2097152 | tf_op jit(solution)/shard_map/all_to_all | solution.py:65
  76.1 10.8 %collective-permute-start = (bf16[64,16,128]{2,1,0:T(8,128)(2,1)S(1)}, bf16[64,16,128]{2,1,0:T(8,128)(2,1)S(1)}, u32[]{:S(2)}, u32[]{:S(2)}) collective-permute-start(bf16[64,16,128]{2,1,0:T(8,128)(2,1)S(1)} %copy.139), channel_id=1, source_target_pairs={{252,0},{0,4},{4,8},{8,12},{12,16},{16,20},{20,24},{24,28},{28,32}... | collective-permute-start | bytes 786440 | tf_op jit(solution)/shard_map/while/body/eval_jaxpr/ppermute | solution.py:15
  86.9 10.8 %collective-permute-start = (bf16[64,16,128]{2,1,0:T(8,128)(2,1)S(1)}, bf16[64,16,128]{2,1,0:T(8,128)(2,1)S(1)}, u32[]{:S(2)}, u32[]{:S(2)}) collective-permute-start(bf16[64,16,128]{2,1,0:T(8,128)(2,1)S(1)} %copy.139), channel_id=1, source_target_pairs={{252,0},{0,4},{4,8},{8,12},{12,16},{16,20},{20,24},{24,28},{28,32}... | collective-permute-start | bytes 786440 | tf_op jit(solution)/shard_map/while/body/eval_jaxpr/ppermute | solution.py:15
  97.8 11.1 %collective-permute-start = (bf16[64,16,128]{2,1,0:T(8,128)(2,1)S(1)}, bf16[64,16,128]{2,1,0:T(8,128)(2,1)S(1)}, u32[]{:S(2)}, u32[]{:S(2)}) collective-permute-start(bf16[64,16,128]{2,1,0:T(8,128)(2,1)S(1)} %copy.139), channel_id=1, source_target_pairs={{252,0},{0,4},{4,8},{8,12},{12,16},{16,20},{20,24},{24,28},{28,32}... | collective-permute-start | bytes 786440 | tf_op jit(solution)/shard_map/while/body/eval_jaxpr/ppermute | solution.py:15
  109.0 10.8 %collective-permute-start = (bf16[64,16,128]{2,1,0:T(8,128)(2,1)S(1)}, bf16[64,16,128]{2,1,0:T(8,128)(2,1)S(1)}, u32[]{:S(2)}, u32[]{:S(2)}) collective-permute-start(bf16[64,16,128]{2,1,0:T(8,128)(2,1)S(1)} %copy.139), channel_id=1, source_target_pairs={{252,0},{0,4},{4,8},{8,12},{12,16},{16,20},{20,24},{24,28},{28,32}... | collective-permute-start | bytes 786440 | tf_op jit(solution)/shard_map/while/body/eval_jaxpr/ppermute | solution.py:15
  119.8 10.8 %collective-permute-start = (bf16[64,16,128]{2,1,0:T(8,128)(2,1)S(1)}, bf16[64,16,128]{2,1,0:T(8,128)(2,1)S(1)}, u32[]{:S(2)}, u32[]{:S(2)}) collective-permute-start(bf16[64,16,128]{2,1,0:T(8,128)(2,1)S(1)} %copy.139), channel_id=1, source_target_pairs={{252,0},{0,4},{4,8},{8,12},{12,16},{16,20},{20,24},{24,28},{28,32}... | collective-permute-start | bytes 786440 | tf_op jit(solution)/shard_map/while/body/eval_jaxpr/ppermute | solution.py:15
  130.7 11.3 %collective-permute-start = (bf16[64,16,128]{2,1,0:T(8,128)(2,1)S(1)}, bf16[64,16,128]{2,1,0:T(8,128)(2,1)S(1)}, u32[]{:S(2)}, u32[]{:S(2)}) collective-permute-start(bf16[64,16,128]{2,1,0:T(8,128)(2,1)S(1)} %copy.139), channel_id=1, source_target_pairs={{252,0},{0,4},{4,8},{8,12},{12,16},{16,20},{20,24},{24,28},{28,32}... | collective-permute-start | bytes 786440 | tf_op jit(solution)/shard_map/while/body/eval_jaxpr/ppermute | solution.py:15
  142.0 10.8 %collective-permute-start = (bf16[64,16,128]{2,1,0:T(8,128)(2,1)S(1)}, bf16[64,16,128]{2,1,0:T(8,128)(2,1)S(1)}, u32[]{:S(2)}, u32[]{:S(2)}) collective-permute-start(bf16[64,16,128]{2,1,0:T(8,128)(2,1)S(1)} %copy.139), channel_id=1, source_target_pairs={{252,0},{0,4},{4,8},{8,12},{12,16},{16,20},{20,24},{24,28},{28,32}... | collective-permute-start | bytes 786440 | tf_op jit(solution)/shard_map/while/body/eval_jaxpr/ppermute | solution.py:15
  152.9 11.1 %collective-permute-start = (bf16[64,16,128]{2,1,0:T(8,128)(2,1)S(1)}, bf16[64,16,128]{2,1,0:T(8,128)(2,1)S(1)}, u32[]{:S(2)}, u32[]{:S(2)}) collective-permute-start(bf16[64,16,128]{2,1,0:T(8,128)(2,1)S(1)} %copy.139), channel_id=1, source_target_pairs={{252,0},{0,4},{4,8},{8,12},{12,16},{16,20},{20,24},{24,28},{28,32}... | collective-permute-start | bytes 786440 | tf_op jit(solution)/shard_map/while/body/eval_jaxpr/ppermute | solution.py:15
  164.0 11.9 %collective-permute-start = (bf16[64,16,128]{2,1,0:T(8,128)(2,1)S(1)}, bf16[64,16,128]{2,1,0:T(8,128)(2,1)S(1)}, u32[]{:S(2)}, u32[]{:S(2)}) collective-permute-start(bf16[64,16,128]{2,1,0:T(8,128)(2,1)S(1)} %copy.139), channel_id=1, source_target_pairs={{252,0},{0,4},{4,8},{8,12},{12,16},{16,20},{20,24},{24,28},{28,32}... | collective-permute-start | bytes 786440 | tf_op jit(solution)/shard_map/while/body/eval_jaxpr/ppermute | solution.py:15
  164.1 11.8 %collective-permute-start.1 = (bf16[64,16]{1,0:T(8,128)(2,1)S(1)}, bf16[64,16]{1,0:T(8,128)(2,1)S(1)}, u32[]{:S(2)}, u32[]{:S(2)}) collective-permute-start(bf16[64,16]{1,0:T(8,128)(2,1)S(1)} %copy.140), channel_id=1, source_target_pairs={{252,0},{0,4},{4,8},{8,12},{12,16},{16,20},{20,24},{24,28},{28,32}... | collective-permute-start | bytes 6152 | tf_op jit(solution)/shard_map/while/body/eval_jaxpr/ppermute | solution.py:15
  175.9 13.1 %collective-permute-start = (bf16[64,16,128]{2,1,0:T(8,128)(2,1)S(1)}, bf16[64,16,128]{2,1,0:T(8,128)(2,1)S(1)}, u32[]{:S(2)}, u32[]{:S(2)}) collective-permute-start(bf16[64,16,128]{2,1,0:T(8,128)(2,1)S(1)} %copy.139), channel_id=1, source_target_pairs={{252,0},{0,4},{4,8},{8,12},{12,16},{16,20},{20,24},{24,28},{28,32}... | collective-permute-start | bytes 786440 | tf_op jit(solution)/shard_map/while/body/eval_jaxpr/ppermute | solution.py:15
  176.0 13.0 %collective-permute-start.1 = (bf16[64,16]{1,0:T(8,128)(2,1)S(1)}, bf16[64,16]{1,0:T(8,128)(2,1)S(1)}, u32[]{:S(2)}, u32[]{:S(2)}) collective-permute-start(bf16[64,16]{1,0:T(8,128)(2,1)S(1)} %copy.140), channel_id=1, source_target_pairs={{252,0},{0,4},{4,8},{8,12},{12,16},{16,20},{20,24},{24,28},{28,32}... | collective-permute-start | bytes 6152 | tf_op jit(solution)/shard_map/while/body/eval_jaxpr/ppermute | solution.py:15
  189.1 13.4 %collective-permute-start = (bf16[64,16,128]{2,1,0:T(8,128)(2,1)S(1)}, bf16[64,16,128]{2,1,0:T(8,128)(2,1)S(1)}, u32[]{:S(2)}, u32[]{:S(2)}) collective-permute-start(bf16[64,16,128]{2,1,0:T(8,128)(2,1)S(1)} %copy.139), channel_id=1, source_target_pairs={{252,0},{0,4},{4,8},{8,12},{12,16},{16,20},{20,24},{24,28},{28,32}... | collective-permute-start | bytes 786440 | tf_op jit(solution)/shard_map/while/body/eval_jaxpr/ppermute | solution.py:15
  189.2 13.3 %collective-permute-start.1 = (bf16[64,16]{1,0:T(8,128)(2,1)S(1)}, bf16[64,16]{1,0:T(8,128)(2,1)S(1)}, u32[]{:S(2)}, u32[]{:S(2)}) collective-permute-start(bf16[64,16]{1,0:T(8,128)(2,1)S(1)} %copy.140), channel_id=1, source_target_pairs={{252,0},{0,4},{4,8},{8,12},{12,16},{16,20},{20,24},{24,28},{28,32}... | collective-permute-start | bytes 6152 | tf_op jit(solution)/shard_map/while/body/eval_jaxpr/ppermute | solution.py:15
  202.5 12.6 %collective-permute-start = (bf16[64,16,128]{2,1,0:T(8,128)(2,1)S(1)}, bf16[64,16,128]{2,1,0:T(8,128)(2,1)S(1)}, u32[]{:S(2)}, u32[]{:S(2)}) collective-permute-start(bf16[64,16,128]{2,1,0:T(8,128)(2,1)S(1)} %copy.139), channel_id=1, source_target_pairs={{252,0},{0,4},{4,8},{8,12},{12,16},{16,20},{20,24},{24,28},{28,32}... | collective-permute-start | bytes 786440 | tf_op jit(solution)/shard_map/while/body/eval_jaxpr/ppermute | solution.py:15
  202.6 12.5 %collective-permute-start.1 = (bf16[64,16]{1,0:T(8,128)(2,1)S(1)}, bf16[64,16]{1,0:T(8,128)(2,1)S(1)}, u32[]{:S(2)}, u32[]{:S(2)}) collective-permute-start(bf16[64,16]{1,0:T(8,128)(2,1)S(1)} %copy.140), channel_id=1, source_target_pairs={{252,0},{0,4},{4,8},{8,12},{12,16},{16,20},{20,24},{24,28},{28,32}... | collective-permute-start | bytes 6152 | tf_op jit(solution)/shard_map/while/body/eval_jaxpr/ppermute | solution.py:15
  215.2 11.7 %collective-permute-start = (bf16[64,16,128]{2,1,0:T(8,128)(2,1)S(1)}, bf16[64,16,128]{2,1,0:T(8,128)(2,1)S(1)}, u32[]{:S(2)}, u32[]{:S(2)}) collective-permute-start(bf16[64,16,128]{2,1,0:T(8,128)(2,1)S(1)} %copy.139), channel_id=1, source_target_pairs={{252,0},{0,4},{4,8},{8,12},{12,16},{16,20},{20,24},{24,28},{28,32}... | collective-permute-start | bytes 786440 | tf_op jit(solution)/shard_map/while/body/eval_jaxpr/ppermute | solution.py:15
  215.3 11.6 %collective-permute-start.1 = (bf16[64,16]{1,0:T(8,128)(2,1)S(1)}, bf16[64,16]{1,0:T(8,128)(2,1)S(1)}, u32[]{:S(2)}, u32[]{:S(2)}) collective-permute-start(bf16[64,16]{1,0:T(8,128)(2,1)S(1)} %copy.140), channel_id=1, source_target_pairs={{252,0},{0,4},{4,8},{8,12},{12,16},{16,20},{20,24},{24,28},{28,32}... | collective-permute-start | bytes 6152 | tf_op jit(solution)/shard_map/while/body/eval_jaxpr/ppermute | solution.py:15
  226.9 10.8 %collective-permute-start = (bf16[64,16,128]{2,1,0:T(8,128)(2,1)S(1)}, bf16[64,16,128]{2,1,0:T(8,128)(2,1)S(1)}, u32[]{:S(2)}, u32[]{:S(2)}) collective-permute-start(bf16[64,16,128]{2,1,0:T(8,128)(2,1)S(1)} %copy.139), channel_id=1, source_target_pairs={{252,0},{0,4},{4,8},{8,12},{12,16},{16,20},{20,24},{24,28},{28,32}... | collective-permute-start | bytes 786440 | tf_op jit(solution)/shard_map/while/body/eval_jaxpr/ppermute | solution.py:15
  227.0 10.7 %collective-permute-start.1 = (bf16[64,16]{1,0:T(8,128)(2,1)S(1)}, bf16[64,16]{1,0:T(8,128)(2,1)S(1)}, u32[]{:S(2)}, u32[]{:S(2)}) collective-permute-start(bf16[64,16]{1,0:T(8,128)(2,1)S(1)} %copy.140), channel_id=1, source_target_pairs={{252,0},{0,4},{4,8},{8,12},{12,16},{16,20},{20,24},{24,28},{28,32}... | collective-permute-start | bytes 6152 | tf_op jit(solution)/shard_map/while/body/eval_jaxpr/ppermute | solution.py:15
  237.8 10.8 %collective-permute-start = (bf16[64,16,128]{2,1,0:T(8,128)(2,1)S(1)}, bf16[64,16,128]{2,1,0:T(8,128)(2,1)S(1)}, u32[]{:S(2)}, u32[]{:S(2)}) collective-permute-start(bf16[64,16,128]{2,1,0:T(8,128)(2,1)S(1)} %copy.139), channel_id=1, source_target_pairs={{252,0},{0,4},{4,8},{8,12},{12,16},{16,20},{20,24},{24,28},{28,32}... | collective-permute-start | bytes 786440 | tf_op jit(solution)/shard_map/while/body/eval_jaxpr/ppermute | solution.py:15
  237.9 10.7 %collective-permute-start.1 = (bf16[64,16]{1,0:T(8,128)(2,1)S(1)}, bf16[64,16]{1,0:T(8,128)(2,1)S(1)}, u32[]{:S(2)}, u32[]{:S(2)}) collective-permute-start(bf16[64,16]{1,0:T(8,128)(2,1)S(1)} %copy.140), channel_id=1, source_target_pairs={{252,0},{0,4},{4,8},{8,12},{12,16},{16,20},{20,24},{24,28},{28,32}... | collective-permute-start | bytes 6152 | tf_op jit(solution)/shard_map/while/body/eval_jaxpr/ppermute | solution.py:15
  (26 other events, 168.1 us)
where the time goes:
time: 259 us; the launch traced here: 258 us
  matrix products  116 us (45%)
  waiting for transfers between devices  57.2 us (22%)
  starting transfers between devices  43.1 us (17%)
  local copies, waits for them, and re-layouts  23.9 us (9%)
  other arithmetic  16.6 us (6%)
    dot_general x16, matrix products, similar(): lax.dot_general(own_dense, other_dense, (((1,), (1,)), ((), ())), preferr...  68.8 us
    dot_general x17, matrix products, densify(): jnp.einsum('dkt,dki->dti', selector, values, preferred_element_type=jnp.f...  46.3 us
    ppermute x30, waiting for transfers between devices, from_behind(): return lax.ppermute(block, axis, route)  27.4 us
    all_to_all x1, waiting for transfers between devices, deal(): lax.all_to_all(outgoing, 'rows', split_axis=0, concat_axis=0, tiled=True)  25.9 us
    ppermute x30, starting transfers between devices, from_behind(): return lax.ppermute(block, axis, route)  23 us
    all_to_all x1, starting transfers between devices, deal(): lax.all_to_all(out_codes, 'rows', split_axis=0, concat_axis=0, tiled=True)  12.7 us
    dynamic_update_slice x16, local copies, waits for them, and re-layouts, record(): lax.dynamic_update_slice_in_dim(output, block, column_block * DOC_DEV, 1)  9.05 us
    reduce_sum x16, other arithmetic, squares(): return jnp.sum(widened * widened, axis=(1, 2))  8.93 us
  transfers between devices with their start and end apart: 32, of which 14 were waited for; matrix products, arithmetic and copies ran while one was open for 50% of the time, Pallas kernels for 0%

commit v1 on v0

v1 whole, which is shorter than its diff:
```python
import jax
import jax.numpy as jnp
from jax import lax
from jax.experimental import pallas as pl
from jax.experimental.pallas import tpu as pltpu
from jax.sharding import Mesh
from jax.sharding import PartitionSpec as P

TILES = 16
LANES = 128
SENT = 24
PIECE = TILES + 1
BF16 = jnp.bfloat16
F32 = jnp.float32
VMEM = pl.BlockSpec(memory_space=pltpu.VMEM)
SMEM = pl.BlockSpec(memory_space=pltpu.SMEM)


def params(mib):
    return pltpu.CompilerParams(vmem_limit_bytes=mib * 2**20)


def pack_kernel(counts, tiles, ids, values, out, source, wide_ids):
    z, yl, x = lax.axis_index("z"), lax.axis_index("yl"), lax.axis_index("x")
    yh, c = lax.axis_index("yh"), lax.axis_index("c")
    here = z * 8 + yl * 4 + x
    base = (yh * 2 + yl) * 64 + z * 8 + c * 4 + x

    def scan(e, carry):
        begin, own_begin = carry
        end = begin + counts[e]
        number = begin + ((base - begin) & 255)

        @pl.when(number < end)
        def _():
            source[number >> 8] = e

        return end, jnp.where(e == here, begin, own_begin)

    _, own_begin = lax.fori_loop(0, 64, scan, (jnp.int32(0), jnp.int32(0)), unroll=8)
    wide_ids[...] = jnp.zeros_like(wide_ids)
    wide_ids[:, 0:TILES] = ids[...].astype(F32)
    tile_line = lax.broadcasted_iota(jnp.int32, (TILES, LANES), 0)

    def fill(t, carry):
        wanted = (yh * 2 + ((t >> 2) & 1)) * 64 + (t >> 3) * 8 + c * 4 + (t & 3)
        slot = jnp.minimum((wanted - own_begin) & 255, 127)
        document = jnp.where(tile_line < tiles[slot], values[slot].astype(F32), 0.0)
        codes = jnp.broadcast_to(wide_ids[pl.ds(slot, 1), :], (SENT - TILES, LANES))
        out[t] = jnp.concatenate([document, codes], axis=0).astype(BF16)
        return carry

    lax.fori_loop(0, 64, fill, 0, unroll=8)


def arrange_kernel(source, arrived, piece, spread, lines):
    for m in range(16):
        lines[pl.ds(m * SENT, SENT), :] = arrived[source[m]].astype(F32)
    total = jnp.zeros((16, LANES), F32)
    parts = []
    for k in range(TILES):
        part = lines[pl.ds(k, 16, stride=SENT), :]
        total = total + part * part
        parts.append(part.astype(BF16))
    norms = jnp.sum(total, axis=1, keepdims=True)
    high = norms.astype(BF16).astype(F32)
    middle = (norms - high).astype(BF16).astype(F32)
    low = norms - high - middle
    lane = lax.broadcasted_iota(jnp.int32, (16, LANES), 1)
    codes = lines[pl.ds(TILES, 16, stride=SENT), :]
    codes = jnp.where(lane == 16, high, codes)
    codes = jnp.where(lane == 17, middle, codes)
    codes = jnp.where(lane == 18, low, codes)
    parts.append(codes.astype(BF16))
    whole = jnp.concatenate([part[None] for part in parts], axis=0)
    piece[...] = whole
    for j in range(16):
        spread[j] = whole


def compare_kernel(rows, own, other, out, columns, column_codes, row_codes, row_norms, acc):
    x, c = lax.axis_index("x"), lax.axis_index("c")
    for u in range(16):
        part = own[u // 2] if u % 2 == 0 else other[((u + 1) // 2 - c) & 7]
        for k in range(TILES):
            columns[k, u * 16 : (u + 1) * 16, :] = part[k]
        column_codes[u * 16 : (u + 1) * 16, :] = part[TILES].astype(F32)
    across = jnp.transpose(column_codes[...], (1, 0))
    column_codes[0:128, :] = across[:, 0:128]
    column_codes[128:256, :] = across[:, 128:256]
    norms_across = across[16:17] + across[17:18] + across[18:19]
    for j in range(16):
        codes = rows[j, TILES].astype(F32)
        for k in range(TILES):
            row_codes[j, k] = jnp.broadcast_to(codes[:, k : k + 1], (16, LANES))
        norms = codes[:, 16:17] + codes[:, 17:18] + codes[:, 18:19]
        row_norms[j] = jnp.broadcast_to(norms, (16, LANES))
    acc[...] = jnp.zeros_like(acc)

    @pl.loop(0, 8)
    def _(pair):
        for b in (2 * pair, 2 * pair + 1):
            weights = jnp.transpose(columns[b], (1, 0))
            codes_b = jnp.concatenate(
                [column_codes[pl.ds(b, 1), :], column_codes[pl.ds(128 + b, 1), :]], axis=1
            )
            for j in range(16):
                left = rows[j, 0:TILES].reshape(256, LANES)
                product = jnp.dot(left, weights, preferred_element_type=F32)
                codes_j = row_codes[j].reshape(256, LANES)
                same = jnp.concatenate([codes_j, codes_j], axis=1) == codes_b
                product = jnp.where(same, product, 0.0).reshape(TILES, 16, 256)
                acc[pl.ds(j * 16, 16), :] += jnp.sum(product, axis=0)

    low_lanes = lax.broadcasted_iota(jnp.int32, (32, LANES), 1) < 64
    for panel in range(4):
        product = acc[pl.ds(panel * 64, 64), :]
        norms = row_norms[pl.ds(panel * 4, 4)].reshape(64, LANES)
        norms = jnp.concatenate([norms, norms], axis=1)
        ratio = product / (norms + norms_across - product)
        ratio = jnp.where(panel < x, pltpu.roll(ratio, 240, 1), ratio)
        for half in range(2):
            first = ratio[0:32, half * 128 : half * 128 + 128]
            second = ratio[32:64, half * 128 : half * 128 + 128]
            out[0, panel, half] = jnp.where(low_lanes, first, pltpu.roll(second, 64, 1))
            out[1, panel, half] = jnp.where(low_lanes, pltpu.roll(first, 64, 1), second)


def place_kernel(arrived, out, tall):
    x = lax.axis_index("x")
    take = lax.broadcasted_iota(jnp.int32, (256, 512), 0)
    give = lax.broadcasted_iota(jnp.int32, (256, 512), 1)
    base = ((take >> 4) & 7) * 64 + (take & 15) * 4 + (take >> 7)
    results = []
    for delta in range(4):
        xs = (x - delta) & 3
        total = jnp.zeros((32, 512), F32)
        for yh in range(2):
            shift = (base + 2 * yh == give).astype(BF16)
            block = jnp.concatenate([arrived[0, xs, yh], arrived[1, xs, yh]], axis=1)
            high = block.astype(BF16)
            rest = block - high.astype(F32)
            middle = rest.astype(BF16)
            low = (rest - middle.astype(F32)).astype(BF16)
            stacked = jnp.concatenate([high, middle, low], axis=0)
            moved = jnp.dot(stacked, shift, preferred_element_type=F32)
            total = total + ((moved[0:32] + moved[32:64]) + moved[64:96])
        results.append(total)
    low_lanes = lax.broadcasted_iota(jnp.int32, (32, LANES), 1) < 64
    for h in range(2):
        for pair in range(2):
            for t in range(4):
                place = h * 256 + (t // 2) * 128
                even = results[2 * pair][:, place : place + 128]
                odd = results[2 * pair + 1][:, place : place + 128]
                if t % 2 == 0:
                    block = jnp.where(low_lanes, even, pltpu.roll(odd, 64, 1))
                else:
                    block = jnp.where(low_lanes, pltpu.roll(even, 64, 1), odd)
                for s in range(2):
                    tall[2 * t + pair, pl.ds(2 * h + s, 16, stride=4), :] = block[s * 16 : s * 16 + 16]
    for group in range(8):
        out[:, group * 128 : group * 128 + 128] = tall[group]


def step(block, axis, distance):
    size = lax.axis_size(axis)
    return lax.ppermute(block, axis, [((i - distance) % size, i) for i in range(size)])


def on_device(tile_values, tile_ids, doc_tiles, row_counts):
    c = lax.axis_index("c")
    sending, source = pl.pallas_call(
        pack_kernel,
        out_shape=(
            jax.ShapeDtypeStruct((64, SENT, LANES), BF16),
            jax.ShapeDtypeStruct((16,), jnp.int32),
        ),
        in_specs=[SMEM, SMEM, VMEM, VMEM],
        out_specs=(VMEM, SMEM),
        scratch_shapes=[pltpu.VMEM((128, LANES), F32)],
        compiler_params=params(16),
    )(row_counts, doc_tiles, tile_ids, tile_values)
    arrived = lax.all_to_all(sending, ("z", "yl", "x"), 0, 0, tiled=True)
    piece, spread = pl.pallas_call(
        arrange_kernel,
        out_shape=(
            jax.ShapeDtypeStruct((PIECE, 16, LANES), BF16),
            jax.ShapeDtypeStruct((16, PIECE, 16, LANES), BF16),
        ),
        in_specs=[SMEM, VMEM],
        out_specs=(VMEM, VMEM),
        scratch_shapes=[pltpu.VMEM((16 * SENT, LANES), F32)],
        compiler_params=params(16),
    )(source, arrived)
    rows = lax.all_to_all(spread, ("x", "yh", "yl"), 0, 0, tiled=True)
    ring = [piece] + [None] * 7
    behind, ahead = piece, piece
    for distance in range(1, 4):
        behind, ahead = step(behind, "z", 1), step(ahead, "z", -1)
        ring[distance], ring[8 - distance] = behind, ahead
    ring[4] = step(behind, "z", 1)
    own = jnp.stack(ring)
    other = step(own, "c", 1)
    blocks = pl.pallas_call(
        compare_kernel,
        out_shape=jax.ShapeDtypeStruct((2, 4, 2, 32, LANES), F32),
        in_specs=[VMEM, VMEM, VMEM],
        out_specs=VMEM,
        scratch_shapes=[
            pltpu.VMEM((TILES, 256, LANES), BF16),
            pltpu.VMEM((256, LANES), F32),
            pltpu.VMEM((16, TILES, 16, LANES), F32),
            pltpu.VMEM((16, 16, LANES), F32),
            pltpu.VMEM((256, 256), F32),
        ],
        compiler_params=params(40),
    )(rows, own, other)
    swapped = step(blocks[1 - c], "c", 1)
    kept = blocks[c]
    results = jnp.where(c == 0, jnp.stack([kept, swapped]), jnp.stack([swapped, kept]))
    results = lax.all_to_all(
        results.reshape(16, 32, LANES), ("yl", "x", "yh"), 0, 0, tiled=True
    ).reshape(2, 4, 2, 32, LANES)
    return pl.pallas_call(
        place_kernel,
        out_shape=jax.ShapeDtypeStruct((64, 1024), F32),
        in_specs=[VMEM],
        out_specs=VMEM,
        scratch_shapes=[pltpu.VMEM((8, 64, LANES), F32)],
        compiler_params=params(16),
    )(results)


def solution(mesh):
    fine = Mesh(mesh.devices.reshape(8, 2, 4, 2, 2), ("z", "yl", "x", "yh", "c"))
    rows, columns = ("z", "yl", "x"), ("yh", "c")
    placed = (P(rows, None, None), P(rows, None), P(rows), P())
    return jax.shard_map(
        on_device, mesh=fine, in_specs=placed, out_specs=P(rows, columns), check_vma=False
    )
```

time: 259 us -> 94.4 us (0.36)
  the two profiles are of different devices: /device:TPU:16 before, /device:TPU:1 now
where the time goes in v1:
time: 94.4 us; the launch traced here: 94 us
  blocking collectives  41.7 us (44%)
  starting transfers between devices  20.7 us (22%)
  Pallas kernels  16.8 us (18%)
  waiting for transfers between devices  11.4 us (12%)
  local copies, waits for them, and re-layouts  3.27 us (3%)
    all_to_all x1, blocking collectives, on_device(): arrived = lax.all_to_all(sending, ('z', 'yl', 'x'), 0, 0, tiled=True)  27 us
    ppermute x9, starting transfers between devices, step(): lax.ppermute(block, axis, [((i - distance) % size, i) for i in range(size)])  15.4 us
    all_to_all x1, blocking collectives, on_device(): lax.all_to_all(results.reshape(16, 32, LANES), ('yl', 'x', 'yh'), 0, 0, t...  14.8 us
    pallas_call x1, Pallas kernels, on_device(): pl.pallas_call(compare_kernel, out_shape=jax.ShapeDtypeStruct((2, 4, 2, 3...  12 us
    ppermute x9, waiting for transfers between devices, step(): lax.ppermute(block, axis, [((i - distance) % size, i) for i in range(size)])  11.4 us
    all_to_all x1, starting transfers between devices, on_device(): rows = lax.all_to_all(spread, ('x', 'yh', 'yl'), 0, 0, tiled=True)  5.3 us
    unnamed x14, local copies, waits for them, and re-layouts  3.23 us
  transfers between devices with their start and end apart: 10, of which 5 were waited for; matrix products, arithmetic and copies ran while one was open for 0% of the time, Pallas kernels for 0%

profile of v1, /device:TPU:1, one launch (start us, length us, event | category | flops | bytes accessed | tf_op | source)
XLA Modules:
  0.0 94.0 jit_solution(9835898843495976813)
XLA Ops:
  0.0 0.8 copy.5.ids
  0.8 1.0 %copy-done = bf16[128,16,128]{2,1,0:T(8,128)(2,1)S(1)} copy-done((bf16[128,16,128]{2,1,0:T(8,128)(2,1)S(1)}, bf16[128,16,128]{2,1,0:T(8,128)(2,1)}, u32[]{:S(2)}) %copy-start) | copy-done | bytes 524312
  1.8 0.7 copy-done.1
  2.5 0.7 copy-done.2
  3.2 1.8 %shard_map.46 = (bf16[64,24,128]{2,1,0:T(8,128)(2,1)S(1)}, s32[16]{0:T(128)S(1)}) custom-call(s32[64]{0:T(128)S(1)} %copy-done.1, s32[128]{0:T(128)S(1)} %copy-done.2, s32[128,16]{1,0:T(8,128)S(1)} %copy.5.ids, bf16[128,16,128]{2,1,0:T(8,128)(2,1)S(1)} %copy-done), custom_call_target="tpu_custom_call" | custom-call | tf_op jit(solution)/shard_map/pallas_call | solution.py:173
  4.9 27.0 %all_to_all.15.arrived = bf16[64,24,128]{2,1,0:T(8,128)(2,1)S(1)} all-to-all(bf16[64,24,128]{2,1,0:T(8,128)(2,1)S(1)} %get-tuple-element.10), channel_id=1, replica_groups=mesh['z'=8,'yl'=2,'x'=4,'yh'=2,'c'=2] {'z','yl','x'}, dimensions={0} | all-to-all | bytes 786432 | tf_op jit(solution)/shard_map/all_to_all | solution.py:184
  31.9 1.7 %shard_map.47 = (bf16[17,16,128]{2,1,0:T(8,128)(2,1)S(1)}, bf16[16,17,16,128]{3,2,1,0:T(8,128)(2,1)}) custom-call(s32[16]{0:T(128)S(1)} %get-tuple-element.9.source, bf16[64,24,128]{2,1,0:T(8,128)(2,1)S(1)} %all_to_all.15.arrived), custom_call_target="tpu_custom_call" | custom-call | tf_op jit(solution)/shard_map/pallas_call | solution.py:185
  33.6 2.7 %collective-permute-start.4 = (bf16[17,16,128]{2,1,0:T(8,128)(2,1)S(1)}, bf16[17,16,128]{2,1,0:T(8,128)(2,1)S(1)}, u32[]{:S(2)}, u32[]{:S(2)}) collective-permute-start(bf16[17,16,128]{2,1,0:T(8,128)(2,1)S(1)} %get-tuple-element.12), channel_id=1, source_target_pairs={{32,0},{64,32},{96,64},{128,96},{160,128},{192,160},{224,192},{0,2... | collective-permute-start | bytes 208904 | tf_op jit(solution)/shard_map/ppermute | solution.py:168
  36.3 5.3 %all-to-all-start.1 = ((bf16[16,17,16,128]{3,2,1,0:T(8,128)(2,1)}), bf16[16,17,16,128]{3,2,1,0:T(8,128)(2,1)S(1)}, u32[]{:S(2)}, u32[]{:S(2)}) async-start(bf16[16,17,16,128]{3,2,1,0:T(8,128)(2,1)} %get-tuple-element.11), calls=%async_computation.1 | async-start | bytes 2228224 | tf_op jit(solution)/shard_map/all_to_all | solution.py:196
  41.6 0.0 collective-permute-done
  41.6 0.1 collective-permute-start.1
  41.7 0.0 collective-permute-done.4
  41.7 2.7 %collective-permute-start.5 = (bf16[17,16,128]{2,1,0:T(8,128)(2,1)S(1)}, bf16[17,16,128]{2,1,0:T(8,128)(2,1)S(1)}, u32[]{:S(2)}, u32[]{:S(2)}) collective-permute-start(bf16[17,16,128]{2,1,0:T(8,128)(2,1)S(1)} %collective-permute-done.4), channel_id=1, source_target_pairs={{32,0},{64,32},{96,64},{128,96},{160,128},{192,160},{224,192},{0,2... | collective-permute-start | bytes 208904 | tf_op jit(solution)/shard_map/ppermute | solution.py:168
  44.4 1.6 %collective-permute-done.1 = bf16[17,16,128]{2,1,0:T(8,128)(2,1)S(1)} collective-permute-done((bf16[17,16,128]{2,1,0:T(8,128)(2,1)S(1)}, bf16[17,16,128]{2,1,0:T(8,128)(2,1)S(1)}, u32[]{:S(2)}, u32[]{:S(2)}) %collective-permute-start.1) | collective-permute-done | bytes 69664 | tf_op jit(solution)/shard_map/ppermute | solution.py:168
  46.1 2.7 %collective-permute-start.6 = (bf16[17,16,128]{2,1,0:T(8,128)(2,1)S(1)}, bf16[17,16,128]{2,1,0:T(8,128)(2,1)S(1)}, u32[]{:S(2)}, u32[]{:S(2)}) collective-permute-start(bf16[17,16,128]{2,1,0:T(8,128)(2,1)S(1)} %collective-permute-done.5), channel_id=1, source_target_pairs={{32,0},{64,32},{96,64},{128,96},{160,128},{192,160},{224,192},{0,2... | collective-permute-start | bytes 208904 | tf_op jit(solution)/shard_map/ppermute | solution.py:168
  48.8 2.5 %collective-permute-done.2 = bf16[17,16,128]{2,1,0:T(8,128)(2,1)S(1)} collective-permute-done((bf16[17,16,128]{2,1,0:T(8,128)(2,1)S(1)}, bf16[17,16,128]{2,1,0:T(8,128)(2,1)S(1)}, u32[]{:S(2)}, u32[]{:S(2)}) %collective-permute-start.2) | collective-permute-done | bytes 69664 | tf_op jit(solution)/shard_map/ppermute | solution.py:168
  51.3 4.7 %collective-permute-done.3 = bf16[17,16,128]{2,1,0:T(8,128)(2,1)S(1)} collective-permute-done((bf16[17,16,128]{2,1,0:T(8,128)(2,1)S(1)}, bf16[17,16,128]{2,1,0:T(8,128)(2,1)S(1)}, u32[]{:S(2)}, u32[]{:S(2)}) %collective-permute-start.3) | collective-permute-done | bytes 69664 | tf_op jit(solution)/shard_map/ppermute | solution.py:168
  56.1 6.6 %collective-permute-start.7 = (bf16[8,17,16,128]{3,2,1,0:T(8,128)(2,1)S(1)}, bf16[8,17,16,128]{3,2,1,0:T(8,128)(2,1)S(1)}, u32[]{:S(2)}, u32[]{:S(2)}) collective-permute-start(bf16[8,17,16,128]{3,2,1,0:T(8,128)(2,1)S(1)} %bitcast_dynamic-update-slice_fusion.own), channel_id=1, source_target_pairs={{1,0},{0,1},{3,2},{2,3},{5,4},{4,5},{7,6},{6,7},{9,8},{8,9},{11,10... | collective-permute-start | bytes 1671176 | tf_op jit(solution)/shard_map/ppermute | solution.py:168
  62.8 1.6 %collective-permute-done.7.other = bf16[8,17,16,128]{3,2,1,0:T(8,128)(2,1)S(1)} collective-permute-done((bf16[8,17,16,128]{3,2,1,0:T(8,128)(2,1)S(1)}, bf16[8,17,16,128]{3,2,1,0:T(8,128)(2,1)S(1)}, u32[]{:S(2)}, u32[]{:S(2)}) %collective-permute-start.7) | collective-permute-done | bytes 557088 | tf_op jit(solution)/shard_map/ppermute | solution.py:168
  64.4 12.0 %shard_map.48 = f32[2,4,2,32,128]{4,3,2,1,0:T(8,128)S(1)} custom-call(bf16[16,17,16,128]{3,2,1,0:T(8,128)(2,1)S(1)} %all-to-all-done.1.rows, bf16[8,17,16,128]{3,2,1,0:T(8,128)(2,1)S(1)} %bitcast_dynamic-update-slice_fusion.own, bf16[8,17,16,128]{3,2,1,0:T(8,128)(2,1)S(1)} %collective-permute-done.7.other), custom_call_target="tpu_custom_call" | custom-call | tf_op jit(solution)/shard_map/pallas_call | solution.py:205
  76.5 0.5 collective-permute-start.8
  76.9 1.0 %collective-permute-done.8 = f32[4,2,32,128]{3,2,1,0:T(8,128)S(1)} collective-permute-done((f32[4,2,32,128]{3,2,1,0:T(8,128)S(1)}, f32[4,2,32,128]{3,2,1,0:T(8,128)S(1)}, u32[]{:S(2)}, u32[]{:S(2)}) %collective-permute-start.8) | collective-permute-done | bytes 131104 | tf_op jit(solution)/shard_map/ppermute | solution.py:168
  77.9 14.8 %all_to_all.16 = f32[16,32,128]{2,1,0:T(8,128)S(1)} all-to-all(f32[16,32,128]{2,1,0:T(8,128)S(1)} %bitcast.22), channel_id=1, replica_groups=mesh['z'=8,'yl'=2,'x'=4,'yh'=2,'c'=2] {'yl','x','yh'}, dimensions={0} | all-to-all | bytes 524288 | tf_op jit(solution)/shard_map/all_to_all | solution.py:222
  92.7 1.3 %shard_map.49 = f32[64,1024]{1,0:T(8,128)} custom-call(f32[2,4,2,32,128]{4,3,2,1,0:T(8,128)S(1)} %bitcast.21), custom_call_target="tpu_custom_call" | custom-call | tf_op jit(solution)/shard_map/pallas_call | solution.py:225
  (19 shorter events, 0.2 us)
Async XLA Ops:
  0.8 1.0 %copy-start = (bf16[128,16,128]{2,1,0:T(8,128)(2,1)S(1)}, bf16[128,16,128]{2,1,0:T(8,128)(2,1)}, u32[]{:S(2)}) copy-start(bf16[128,16,128]{2,1,0:T(8,128)(2,1)} %values.1) | copy-start | bytes 1572868
  1.8 0.7 copy-start.1
  2.5 0.7 copy-start.2
  33.6 8.0 %collective-permute-start = (bf16[17,16,128]{2,1,0:T(8,128)(2,1)S(1)}, bf16[17,16,128]{2,1,0:T(8,128)(2,1)S(1)}, u32[]{:S(2)}, u32[]{:S(2)}) collective-permute-start(bf16[17,16,128]{2,1,0:T(8,128)(2,1)S(1)} %get-tuple-element.12), channel_id=1, source_target_pairs={{224,0},{0,32},{32,64},{64,96},{96,128},{128,160},{160,192},{192,2... | collective-permute-start | bytes 208904 | tf_op jit(solution)/shard_map/ppermute | solution.py:168
  33.6 8.1 %collective-permute-start.4 = (bf16[17,16,128]{2,1,0:T(8,128)(2,1)S(1)}, bf16[17,16,128]{2,1,0:T(8,128)(2,1)S(1)}, u32[]{:S(2)}, u32[]{:S(2)}) collective-permute-start(bf16[17,16,128]{2,1,0:T(8,128)(2,1)S(1)} %get-tuple-element.12), channel_id=1, source_target_pairs={{32,0},{64,32},{96,64},{128,96},{160,128},{192,160},{224,192},{0,2... | collective-permute-start | bytes 208904 | tf_op jit(solution)/shard_map/ppermute | solution.py:168
  36.3 28.1 %all-to-all-start.1 = ((bf16[16,17,16,128]{3,2,1,0:T(8,128)(2,1)}), bf16[16,17,16,128]{3,2,1,0:T(8,128)(2,1)S(1)}, u32[]{:S(2)}, u32[]{:S(2)}) async-start(bf16[16,17,16,128]{3,2,1,0:T(8,128)(2,1)} %get-tuple-element.11), calls=%async_computation.1 | async-start | bytes 2228224 | tf_op jit(solution)/shard_map/all_to_all | solution.py:196
  41.6 4.4 %collective-permute-start.1 = (bf16[17,16,128]{2,1,0:T(8,128)(2,1)S(1)}, bf16[17,16,128]{2,1,0:T(8,128)(2,1)S(1)}, u32[]{:S(2)}, u32[]{:S(2)}) collective-permute-start(bf16[17,16,128]{2,1,0:T(8,128)(2,1)S(1)} %collective-permute-done), channel_id=1, source_target_pairs={{224,0},{0,32},{32,64},{64,96},{96,128},{128,160},{160,192},{192,2... | collective-permute-start | bytes 208904 | tf_op jit(solution)/shard_map/ppermute | solution.py:168
  41.7 4.3 %collective-permute-start.5 = (bf16[17,16,128]{2,1,0:T(8,128)(2,1)S(1)}, bf16[17,16,128]{2,1,0:T(8,128)(2,1)S(1)}, u32[]{:S(2)}, u32[]{:S(2)}) collective-permute-start(bf16[17,16,128]{2,1,0:T(8,128)(2,1)S(1)} %collective-permute-done.4), channel_id=1, source_target_pairs={{32,0},{64,32},{96,64},{128,96},{160,128},{192,160},{224,192},{0,2... | collective-permute-start | bytes 208904 | tf_op jit(solution)/shard_map/ppermute | solution.py:168
  46.0 5.3 %collective-permute-start.2 = (bf16[17,16,128]{2,1,0:T(8,128)(2,1)S(1)}, bf16[17,16,128]{2,1,0:T(8,128)(2,1)S(1)}, u32[]{:S(2)}, u32[]{:S(2)}) collective-permute-start(bf16[17,16,128]{2,1,0:T(8,128)(2,1)S(1)} %collective-permute-done.1), channel_id=1, source_target_pairs={{224,0},{0,32},{32,64},{64,96},{96,128},{128,160},{160,192},{192,2... | collective-permute-start | bytes 208904 | tf_op jit(solution)/shard_map/ppermute | solution.py:168
  46.1 10.0 %collective-permute-start.6 = (bf16[17,16,128]{2,1,0:T(8,128)(2,1)S(1)}, bf16[17,16,128]{2,1,0:T(8,128)(2,1)S(1)}, u32[]{:S(2)}, u32[]{:S(2)}) collective-permute-start(bf16[17,16,128]{2,1,0:T(8,128)(2,1)S(1)} %collective-permute-done.5), channel_id=1, source_target_pairs={{32,0},{64,32},{96,64},{128,96},{160,128},{192,160},{224,192},{0,2... | collective-permute-start | bytes 208904 | tf_op jit(solution)/shard_map/ppermute | solution.py:168
  51.3 4.8 %collective-permute-start.3 = (bf16[17,16,128]{2,1,0:T(8,128)(2,1)S(1)}, bf16[17,16,128]{2,1,0:T(8,128)(2,1)S(1)}, u32[]{:S(2)}, u32[]{:S(2)}) collective-permute-start(bf16[17,16,128]{2,1,0:T(8,128)(2,1)S(1)} %collective-permute-done.2), channel_id=1, source_target_pairs={{224,0},{0,32},{32,64},{64,96},{96,128},{128,160},{160,192},{192,2... | collective-permute-start | bytes 208904 | tf_op jit(solution)/shard_map/ppermute | solution.py:168
  56.1 8.2 %collective-permute-start.7 = (bf16[8,17,16,128]{3,2,1,0:T(8,128)(2,1)S(1)}, bf16[8,17,16,128]{3,2,1,0:T(8,128)(2,1)S(1)}, u32[]{:S(2)}, u32[]{:S(2)}) collective-permute-start(bf16[8,17,16,128]{3,2,1,0:T(8,128)(2,1)S(1)} %bitcast_dynamic-update-slice_fusion.own), channel_id=1, source_target_pairs={{1,0},{0,1},{3,2},{2,3},{5,4},{4,5},{7,6},{6,7},{9,8},{8,9},{11,10... | collective-permute-start | bytes 1671176 | tf_op jit(solution)/shard_map/ppermute | solution.py:168
  76.5 1.5 %collective-permute-start.8 = (f32[4,2,32,128]{3,2,1,0:T(8,128)S(1)}, f32[4,2,32,128]{3,2,1,0:T(8,128)S(1)}, u32[]{:S(2)}, u32[]{:S(2)}) collective-permute-start(f32[4,2,32,128]{3,2,1,0:T(8,128)S(1)} %get-tuple-element.14), channel_id=1, source_target_pairs={{1,0},{0,1},{3,2},{2,3},{5,4},{4,5},{7,6},{6,7},{9,8},{8,9},{11,10... | collective-permute-start | bytes 393224 | tf_op jit(solution)/shard_map/ppermute | solution.py:168

commit v2 on v1

--- a/solution.py
+++ b/solution.py
@@ -8,11 +8,12 @@
 
 TILES = 16
 LANES = 128
-SENT = 24
+SENT = 18
 PIECE = TILES + 1
 BF16 = jnp.bfloat16
 F32 = jnp.float32
 VMEM = pl.BlockSpec(memory_space=pltpu.VMEM)
+ANY = pl.BlockSpec(memory_space=pl.ANY)
 SMEM = pl.BlockSpec(memory_space=pltpu.SMEM)
 
 
@@ -20,14 +21,12 @@
     return pltpu.CompilerParams(vmem_limit_bytes=mib * 2**20)
 
 
-def pack_kernel(counts, tiles, ids, values, out, source, wide_ids):
+def source_kernel(counts, source):
     z, yl, x = lax.axis_index("z"), lax.axis_index("yl"), lax.axis_index("x")
     yh, c = lax.axis_index("yh"), lax.axis_index("c")
-    here = z * 8 + yl * 4 + x
     base = (yh * 2 + yl) * 64 + z * 8 + c * 4 + x
 
-    def scan(e, carry):
-        begin, own_begin = carry
+    def scan(e, begin):
         end = begin + counts[e]
         number = begin + ((base - begin) & 255)
 
@@ -35,11 +34,31 @@
         def _():
             source[number >> 8] = e
 
-        return end, jnp.where(e == here, begin, own_begin)
-
-    _, own_begin = lax.fori_loop(0, 64, scan, (jnp.int32(0), jnp.int32(0)), unroll=8)
-    wide_ids[...] = jnp.zeros_like(wide_ids)
-    wide_ids[:, 0:TILES] = ids[...].astype(F32)
+        return end
+
+    lax.fori_loop(0, 64, scan, jnp.int32(0), unroll=8)
+
+
+def pack_kernel(counts_in, tiles_in, ids_in, values_in, out, counts, tiles, ids, values, wide_ids, sems):
+    moves = [
+        pltpu.make_async_copy(counts_in, counts, sems.at[0]),
+        pltpu.make_async_copy(ids_in, ids, sems.at[1]),
+        pltpu.make_async_copy(tiles_in, tiles, sems.at[2]),
+        pltpu.make_async_copy(values_in, values, sems.at[3]),
+    ]
+    for move in moves:
+        move.start()
+    yh, c = lax.axis_index("yh"), lax.axis_index("c")
+    here = lax.axis_index("z") * 8 + lax.axis_index("yl") * 4 + lax.axis_index("x")
+    moves[0].wait()
+    own_begin = lax.fori_loop(
+        0, 64, lambda e, begin: begin + jnp.where(e < here, counts[e], 0), jnp.int32(0), unroll=16
+    )
+    moves[1].wait()
+    tall_ids = jnp.concatenate([ids[...].astype(F32), jnp.zeros((LANES - TILES, LANES), F32)], axis=0)
+    wide_ids[...] = jnp.transpose(tall_ids, (1, 0))
+    moves[2].wait()
+    moves[3].wait()
     tile_line = lax.broadcasted_iota(jnp.int32, (TILES, LANES), 0)
 
     def fill(t, carry):
@@ -47,7 +66,8 @@
         slot = jnp.minimum((wanted - own_begin) & 255, 127)
         document = jnp.where(tile_line < tiles[slot], values[slot].astype(F32), 0.0)
         codes = jnp.broadcast_to(wide_ids[pl.ds(slot, 1), :], (SENT - TILES, LANES))
-        out[t] = jnp.concatenate([document, codes], axis=0).astype(BF16)
+        whole = jnp.concatenate([document, codes], axis=0).astype(BF16)
+        out[t] = whole.reshape(SENT // 2, 2, LANES)
         return carry
 
     lax.fori_loop(0, 64, fill, 0, unroll=8)
@@ -55,7 +75,7 @@
 
 def arrange_kernel(source, arrived, piece, spread, lines):
     for m in range(16):
-        lines[pl.ds(m * SENT, SENT), :] = arrived[source[m]].astype(F32)
+        lines[pl.ds(m * SENT, SENT), :] = arrived[source[m]].reshape(SENT, LANES).astype(F32)
     total = jnp.zeros((16, LANES), F32)
     parts = []
     for k in range(TILES):
@@ -78,46 +98,53 @@
         spread[j] = whole
 
 
-def compare_kernel(rows, own, other, out, columns, column_codes, row_codes, row_norms, acc):
+def compare(rows, pieces, row_codes, piece_codes, acc):
+    for j in range(16):
+        row_codes[j * 16 : j * 16 + 16, :] = rows[j, TILES].astype(F32)
+    across = jnp.transpose(row_codes[...], (1, 0))
+    row_codes[0:128, :] = across[:, 0:128]
+    row_codes[128:256, :] = across[:, 128:256]
+    piece_norms = []
+    for d in range(8):
+        codes = pieces[d, TILES].astype(F32)
+        for k in range(TILES):
+            piece_codes[d, k] = jnp.broadcast_to(codes[:, k : k + 1], (16, LANES))
+        norms = codes[:, 16:17] + codes[:, 17:18] + codes[:, 18:19]
+        piece_norms.append(jnp.broadcast_to(norms, (16, 256)))
+    acc[...] = jnp.zeros_like(acc)
+
+    for k in range(TILES):
+        weights = jnp.transpose(rows[:, k].reshape(256, LANES), (1, 0))
+        codes_k = jnp.concatenate(
+            [row_codes[pl.ds(k, 1), :], row_codes[pl.ds(128 + k, 1), :]], axis=1
+        )
+        for d in range(8):
+            left = pieces[d, 0:TILES].reshape(256, LANES)
+            product = jnp.dot(left, weights, preferred_element_type=F32)
+            codes_d = piece_codes[d].reshape(256, LANES)
+            same = jnp.concatenate([codes_d, codes_d], axis=1) == codes_k
+            product = jnp.where(same, product, 0.0).reshape(TILES, 16, 256)
+            acc[d] += jnp.sum(product, axis=0)
+
+    norms_across = across[16:17] + across[17:18] + across[18:19]
+    for d in range(8):
+        acc[d] = acc[d] / (piece_norms[d] + norms_across - acc[d])
+
+
+def own_kernel(rows, own, out, row_codes, piece_codes):
+    compare(rows, own, row_codes, piece_codes, out)
+
+
+def other_kernel(rows, other, own_ratio, out, row_codes, piece_codes, acc, tall):
     x, c = lax.axis_index("x"), lax.axis_index("c")
+    compare(rows, other, row_codes, piece_codes, acc)
     for u in range(16):
-        part = own[u // 2] if u % 2 == 0 else other[((u + 1) // 2 - c) & 7]
-        for k in range(TILES):
-            columns[k, u * 16 : (u + 1) * 16, :] = part[k]
-        column_codes[u * 16 : (u + 1) * 16, :] = part[TILES].astype(F32)
-    across = jnp.transpose(column_codes[...], (1, 0))
-    column_codes[0:128, :] = across[:, 0:128]
-    column_codes[128:256, :] = across[:, 128:256]
-    norms_across = across[16:17] + across[17:18] + across[18:19]
-    for j in range(16):
-        codes = rows[j, TILES].astype(F32)
-        for k in range(TILES):
-            row_codes[j, k] = jnp.broadcast_to(codes[:, k : k + 1], (16, LANES))
-        norms = codes[:, 16:17] + codes[:, 17:18] + codes[:, 18:19]
-        row_norms[j] = jnp.broadcast_to(norms, (16, LANES))
-    acc[...] = jnp.zeros_like(acc)
-
-    @pl.loop(0, 8)
-    def _(pair):
-        for b in (2 * pair, 2 * pair + 1):
-            weights = jnp.transpose(columns[b], (1, 0))
-            codes_b = jnp.concatenate(
-                [column_codes[pl.ds(b, 1), :], column_codes[pl.ds(128 + b, 1), :]], axis=1
-            )
-            for j in range(16):
-                left = rows[j, 0:TILES].reshape(256, LANES)
-                product = jnp.dot(left, weights, preferred_element_type=F32)
-                codes_j = row_codes[j].reshape(256, LANES)
-                same = jnp.concatenate([codes_j, codes_j], axis=1) == codes_b
-                product = jnp.where(same, product, 0.0).reshape(TILES, 16, 256)
-                acc[pl.ds(j * 16, 16), :] += jnp.sum(product, axis=0)
-
+        tall[u * 16 : u * 16 + 16, :] = own_ratio[u // 2] if u % 2 == 0 else acc[((u + 1) // 2 - c) & 7]
     low_lanes = lax.broadcasted_iota(jnp.int32, (32, LANES), 1) < 64
     for panel in range(4):
-        product = acc[pl.ds(panel * 64, 64), :]
-        norms = row_norms[pl.ds(panel * 4, 4)].reshape(64, LANES)
-        norms = jnp.concatenate([norms, norms], axis=1)
-        ratio = product / (norms + norms_across - product)
+        if panel % 2 == 0:
+            wide = jnp.transpose(tall[:, panel * 64 : panel * 64 + 128], (1, 0))
+        ratio = wide[(panel % 2) * 64 : (panel % 2) * 64 + 64]
         ratio = jnp.where(panel < x, pltpu.roll(ratio, 240, 1), ratio)
         for half in range(2):
             first = ratio[0:32, half * 128 : half * 128 + 128]
@@ -170,17 +197,29 @@
 
 def on_device(tile_values, tile_ids, doc_tiles, row_counts):
     c = lax.axis_index("c")
-    sending, source = pl.pallas_call(
+    sending = pl.pallas_call(
         pack_kernel,
-        out_shape=(
-            jax.ShapeDtypeStruct((64, SENT, LANES), BF16),
-            jax.ShapeDtypeStruct((16,), jnp.int32),
-        ),
-        in_specs=[SMEM, SMEM, VMEM, VMEM],
-        out_specs=(VMEM, SMEM),
-        scratch_shapes=[pltpu.VMEM((128, LANES), F32)],
-        compiler_params=params(16),
-    )(row_counts, doc_tiles, tile_ids, tile_values)
+        out_shape=jax.ShapeDtypeStruct((64, SENT // 2, 2, LANES), BF16),
+        in_specs=[ANY, ANY, ANY, ANY],
+        out_specs=VMEM,
+        scratch_shapes=[
+            pltpu.SMEM((64,), jnp.int32),
+            pltpu.SMEM((128,), jnp.int32),
+            pltpu.VMEM((TILES, LANES), jnp.int32),
+            pltpu.VMEM((128, TILES, LANES), BF16),
+            pltpu.VMEM((128, LANES), F32),
+            pltpu.SemaphoreType.DMA((4,)),
+        ],
+        compiler_params=params(60),
+    )(row_counts, doc_tiles, tile_ids.T, tile_values)
+    source = pl.pallas_call(
+        source_kernel,
+        out_shape=jax.ShapeDtypeStruct((16,), jnp.int32),
+        in_specs=[SMEM],
+        out_specs=SMEM,
+        compiler_params=params(4),
+        cost_estimate=pl.CostEstimate(flops=2**30, bytes_accessed=2**20, transcendentals=0),
+    )(row_counts)
     arrived = lax.all_to_all(sending, ("z", "yl", "x"), 0, 0, tiled=True)
     piece, spread = pl.pallas_call(
         arrange_kernel,
@@ -195,27 +234,33 @@
     )(source, arrived)
     rows = lax.all_to_all(spread, ("x", "yh", "yl"), 0, 0, tiled=True)
     ring = [piece] + [None] * 7
-    behind, ahead = piece, piece
+    ring[1] = step(piece, "z", 1)
+    ahead, behind = lax.optimization_barrier((piece, ring[1]))
     for distance in range(1, 4):
         behind, ahead = step(behind, "z", 1), step(ahead, "z", -1)
-        ring[distance], ring[8 - distance] = behind, ahead
-    ring[4] = step(behind, "z", 1)
+        ring[distance + 1], ring[8 - distance] = behind, ahead
     own = jnp.stack(ring)
     other = step(own, "c", 1)
+    codes_scratch = [pltpu.VMEM((256, LANES), F32), pltpu.VMEM((8, TILES, 16, LANES), F32)]
+    cost = pl.CostEstimate(flops=2 * 4096 * 2048 * LANES, bytes_accessed=2**21, transcendentals=0)
+    own_ratio = pl.pallas_call(
+        own_kernel,
+        out_shape=jax.ShapeDtypeStruct((8, 16, 256), F32),
+        in_specs=[VMEM, VMEM],
+        out_specs=VMEM,
+        scratch_shapes=codes_scratch,
+        compiler_params=params(32),
+        cost_estimate=cost,
+    )(rows, own)
     blocks = pl.pallas_call(
-        compare_kernel,
+        other_kernel,
         out_shape=jax.ShapeDtypeStruct((2, 4, 2, 32, LANES), F32),
         in_specs=[VMEM, VMEM, VMEM],
         out_specs=VMEM,
-        scratch_shapes=[
-            pltpu.VMEM((TILES, 256, LANES), BF16),
-            pltpu.VMEM((256, LANES), F32),
-            pltpu.VMEM((16, TILES, 16, LANES), F32),
-            pltpu.VMEM((16, 16, LANES), F32),
-            pltpu.VMEM((256, 256), F32),
-        ],
-        compiler_params=params(40),
-    )(rows, own, other)
+        scratch_shapes=codes_scratch + [pltpu.VMEM((8, 16, 256), F32), pltpu.VMEM((256, 256), F32)],
+        compiler_params=params(32),
+        cost_estimate=cost,
+    )(rows, other, own_ratio)
     swapped = step(blocks[1 - c], "c", 1)
     kept = blocks[c]
     results = jnp.where(c == 0, jnp.stack([kept, swapped]), jnp.stack([swapped, kept]))

time: 94.4 us -> 85 us (0.900)
  blocking collectives: 41.7 us -> 14.7 us
  starting transfers between devices: 20.7 us -> 34.6 us
  waiting for transfers between devices: 11.4 us -> 17.8 us
  local copies, waits for them, and re-layouts: 3.27 us -> 0.13 us
    all_to_all x1 -> x0, blocking collectives: 27 us -> none  [on_device(): arrived = lax.all_to_all(sending, ('z', 'yl', 'x'), 0, 0, tiled=True)]
    all_to_all x0 -> x1, starting transfers between devices: none -> 13.5 us  [on_device(): arrived = lax.all_to_all(sending, ('z', 'yl', 'x'), 0, 0, tiled=True)]
    all_to_all x0 -> x1, waiting for transfers between devices: none -> 10.5 us  [on_device(): arrived = lax.all_to_all(sending, ('z', 'yl', 'x'), 0, 0, tiled=True)]
    ppermute x9, waiting for transfers between devices: 11.4 us -> 7.35 us  [step(): lax.ppermute(block, axis, [((i - distance) % size, i) for i in range(size)])]
    unnamed x14 -> x9, local copies, waits for them, and re-layouts: 3.23 us -> 0.09 us
    all_to_all x1, starting transfers between devices: 5.3 us -> 6.37 us  [on_device(): rows = lax.all_to_all(spread, ('x', 'yh', 'yl'), 0, 0, tiled=True)]
    pallas_call x2 -> x4, Pallas kernels: 13.8 us -> 14.2 us  [the longest x1 6.01 us: on_device(): pl.pallas_call(other_kernel, out_shape=jax.ShapeDtypeStruct((2, 4, 2, 32,...]
  transfers between devices with their start and end apart: 10 -> 11, of which waited for: 5 -> 5; matrix products, arithmetic and copies ran while one was open for 0% -> 0% of each run, Pallas kernels for 0% -> 7%
where the time goes in v2:
time: 85 us; the launch traced here: 84.7 us
  starting transfers between devices  34.6 us (41%)
  waiting for transfers between devices  17.8 us (21%)
  Pallas kernels  17.3 us (20%)
  blocking collectives  14.7 us (17%)
    ppermute x9, starting transfers between devices, step(): lax.ppermute(block, axis, [((i - distance) % size, i) for i in range(size)])  14.7 us
    all_to_all x1, blocking collectives, on_device(): lax.all_to_all(results.reshape(16, 32, LANES), ('yl', 'x', 'yh'), 0, 0, t...  14.7 us
    all_to_all x1, starting transfers between devices, on_device(): arrived = lax.all_to_all(sending, ('z', 'yl', 'x'), 0, 0, tiled=True)  13.5 us
    all_to_all x1, waiting for transfers between devices, on_device(): arrived = lax.all_to_all(sending, ('z', 'yl', 'x'), 0, 0, tiled=True)  10.5 us
    ppermute x9, waiting for transfers between devices, step(): lax.ppermute(block, axis, [((i - distance) % size, i) for i in range(size)])  7.35 us
    all_to_all x1, starting transfers between devices, on_device(): rows = lax.all_to_all(spread, ('x', 'yh', 'yl'), 0, 0, tiled=True)  6.37 us
    pallas_call x1, Pallas kernels, on_device(): pl.pallas_call(other_kernel, out_shape=jax.ShapeDtypeStruct((2, 4, 2, 32,...  6.01 us
    pallas_call x1, Pallas kernels, on_device(): pl.pallas_call(own_kernel, out_shape=jax.ShapeDtypeStruct((8, 16, 256), F...  4.63 us
  transfers between devices with their start and end apart: 11, of which 5 were waited for; matrix products, arithmetic and copies ran while one was open for 0% of the time, Pallas kernels for 7%

profile of v2, /device:TPU:1, one launch (start us, length us, event | category | flops | bytes accessed | tf_op | source)
XLA Modules:
  0.0 84.7 jit_solution(6722538162314946342)
XLA Ops:
  0.0 2.2 %shard_map.47 = bf16[64,9,2,128]{3,2,1,0:T(2,128)(2,1)} custom-call(s32[64]{0:T(128)} %counts_in.1, s32[128]{0:T(128)} %tiles_in.1, s32[16,128]{1,0:T(8,128)} %bitcast.25, bf16[128,16,128]{2,1,0:T(8,128)(2,1)} %values_in.1), custom_call_target="tpu_custom_call" | custom-call | tf_op jit(solution)/shard_map/pallas_call | solution.py:200
  2.3 13.5 %all-to-all-start = ((bf16[64,9,2,128]{3,2,1,0:T(2,128)(2,1)}), bf16[64,9,2,128]{3,2,1,0:T(2,128)(2,1)S(1)}, u32[]{:S(2)}, u32[]{:S(2)}) async-start(bf16[64,9,2,128]{3,2,1,0:T(2,128)(2,1)} %shard_map.47), calls=%async_computation | async-start | bytes 589824 | tf_op jit(solution)/shard_map/all_to_all | solution.py:223
  15.8 1.4 %shard_map.46.source = s32[16]{0:T(128)S(1)} custom-call(s32[64]{0:T(128)S(1)} %copy-done), custom_call_target="tpu_custom_call" | custom-call | flops 1073741824 | bytes 1048576 | tf_op jit(solution)/shard_map/pallas_call | solution.py:215
  17.1 10.5 %all-to-all-done.arrived = bf16[64,9,2,128]{3,2,1,0:T(2,128)(2,1)S(1)} async-done(((bf16[64,9,2,128]{3,2,1,0:T(2,128)(2,1)}), bf16[64,9,2,128]{3,2,1,0:T(2,128)(2,1)S(1)}, u32[]{:S(2)}, u32[]{:S(2)}) %all-to-all-start) | async-done | bytes 294944 | tf_op jit(solution)/shard_map/all_to_all | solution.py:223
  27.6 1.7 %shard_map.48 = (bf16[17,16,128]{2,1,0:T(8,128)(2,1)S(1)}, bf16[16,17,16,128]{3,2,1,0:T(8,128)(2,1)}) custom-call(s32[16]{0:T(128)S(1)} %shard_map.46.source, bf16[64,9,2,128]{3,2,1,0:T(2,128)(2,1)S(1)} %all-to-all-done.arrived), custom_call_target="tpu_custom_call" | custom-call | tf_op jit(solution)/shard_map/pallas_call | solution.py:224
  29.3 0.0 collective-permute-start
  29.3 6.4 %all-to-all-start.1 = ((bf16[16,17,16,128]{3,2,1,0:T(8,128)(2,1)}), bf16[16,17,16,128]{3,2,1,0:T(8,128)(2,1)S(1)}, u32[]{:S(2)}, u32[]{:S(2)}) async-start(bf16[16,17,16,128]{3,2,1,0:T(8,128)(2,1)} %get-tuple-element.9), calls=%async_computation.1 | async-start | bytes 2228224 | tf_op jit(solution)/shard_map/all_to_all | solution.py:235
  35.7 0.0 collective-permute-done
  35.7 0.1 collective-permute-start.1
  35.8 2.6 %collective-permute-start.4 = (bf16[17,16,128]{2,1,0:T(8,128)(2,1)S(1)}, bf16[17,16,128]{2,1,0:T(8,128)(2,1)S(1)}, u32[]{:S(2)}, u32[]{:S(2)}) collective-permute-start(bf16[17,16,128]{2,1,0:T(8,128)(2,1)S(1)} %get-tuple-element.12), channel_id=1, source_target_pairs={{32,0},{64,32},{96,64},{128,96},{160,128},{192,160},{224,192},{0,2... | collective-permute-start | bytes 208904 | tf_op jit(solution)/shard_map/ppermute | solution.py:195
  38.5 1.7 %collective-permute-done.1 = bf16[17,16,128]{2,1,0:T(8,128)(2,1)S(1)} collective-permute-done((bf16[17,16,128]{2,1,0:T(8,128)(2,1)S(1)}, bf16[17,16,128]{2,1,0:T(8,128)(2,1)S(1)}, u32[]{:S(2)}, u32[]{:S(2)}) %collective-permute-start.1) | collective-permute-done | bytes 69664 | tf_op jit(solution)/shard_map/ppermute | solution.py:195
  40.1 0.0 collective-permute-start.2
  40.2 0.0 collective-permute-done.4
  40.2 2.7 %collective-permute-start.5 = (bf16[17,16,128]{2,1,0:T(8,128)(2,1)S(1)}, bf16[17,16,128]{2,1,0:T(8,128)(2,1)S(1)}, u32[]{:S(2)}, u32[]{:S(2)}) collective-permute-start(bf16[17,16,128]{2,1,0:T(8,128)(2,1)S(1)} %collective-permute-done.4), channel_id=1, source_target_pairs={{32,0},{64,32},{96,64},{128,96},{160,128},{192,160},{224,192},{0,2... | collective-permute-start | bytes 208904 | tf_op jit(solution)/shard_map/ppermute | solution.py:195
  42.9 1.9 %collective-permute-done.2 = bf16[17,16,128]{2,1,0:T(8,128)(2,1)S(1)} collective-permute-done((bf16[17,16,128]{2,1,0:T(8,128)(2,1)S(1)}, bf16[17,16,128]{2,1,0:T(8,128)(2,1)S(1)}, u32[]{:S(2)}, u32[]{:S(2)}) %collective-permute-start.2) | collective-permute-done | bytes 69664 | tf_op jit(solution)/shard_map/ppermute | solution.py:195
  44.8 2.9 %collective-permute-start.6 = (bf16[17,16,128]{2,1,0:T(8,128)(2,1)S(1)}, bf16[17,16,128]{2,1,0:T(8,128)(2,1)S(1)}, u32[]{:S(2)}, u32[]{:S(2)}) collective-permute-start(bf16[17,16,128]{2,1,0:T(8,128)(2,1)S(1)} %collective-permute-done.5), channel_id=1, source_target_pairs={{32,0},{64,32},{96,64},{128,96},{160,128},{192,160},{224,192},{0,2... | collective-permute-start | bytes 208904 | tf_op jit(solution)/shard_map/ppermute | solution.py:195
  47.7 2.4 %collective-permute-done.3 = bf16[17,16,128]{2,1,0:T(8,128)(2,1)S(1)} collective-permute-done((bf16[17,16,128]{2,1,0:T(8,128)(2,1)S(1)}, bf16[17,16,128]{2,1,0:T(8,128)(2,1)S(1)}, u32[]{:S(2)}, u32[]{:S(2)}) %collective-permute-start.3) | collective-permute-done | bytes 69664 | tf_op jit(solution)/shard_map/ppermute | solution.py:195
  50.2 6.2 %collective-permute-start.7 = (bf16[8,17,16,128]{3,2,1,0:T(8,128)(2,1)S(1)}, bf16[8,17,16,128]{3,2,1,0:T(8,128)(2,1)S(1)}, u32[]{:S(2)}, u32[]{:S(2)}) collective-permute-start(bf16[8,17,16,128]{3,2,1,0:T(8,128)(2,1)S(1)} %bitcast_dynamic-update-slice_fusion.own), channel_id=1, source_target_pairs={{1,0},{0,1},{3,2},{2,3},{5,4},{4,5},{7,6},{6,7},{9,8},{8,9},{11,10... | collective-permute-start | bytes 1671176 | tf_op jit(solution)/shard_map/ppermute | solution.py:195
  56.5 4.6 %shard_map.49.own_ratio = f32[8,16,256]{2,1,0:T(8,128)S(1)} custom-call(bf16[16,17,16,128]{3,2,1,0:T(8,128)(2,1)S(1)} %all-to-all-done.1.rows, bf16[8,17,16,128]{3,2,1,0:T(8,128)(2,1)S(1)} %bitcast_dynamic-update-slice_fusion.own), custom_call_target="tpu_custom_call" | custom-call | flops 2147483648 | bytes 2097152 | tf_op jit(solution)/shard_map/pallas_call | solution.py:246
  61.1 6.0 %shard_map.50 = f32[2,4,2,32,128]{4,3,2,1,0:T(8,128)S(1)} custom-call(bf16[16,17,16,128]{3,2,1,0:T(8,128)(2,1)S(1)} %all-to-all-done.1.rows, bf16[8,17,16,128]{3,2,1,0:T(8,128)(2,1)S(1)} %collective-permute-done.7.other, f32[8,16,256]{2,1,0:T(8,128)S(1)} %shard_map.49.own_ratio), custom_call_target="tpu_custom_call" | custom-call | flops 2147483648 | bytes 2097152 | tf_op jit(solution)/shard_map/pallas_call | solution.py:255
  67.2 0.1 collective-permute-start.8
  67.3 1.3 %collective-permute-done.8 = f32[4,2,32,128]{3,2,1,0:T(8,128)S(1)} collective-permute-done((f32[4,2,32,128]{3,2,1,0:T(8,128)S(1)}, f32[4,2,32,128]{3,2,1,0:T(8,128)S(1)}, u32[]{:S(2)}, u32[]{:S(2)}) %collective-permute-start.8) | collective-permute-done | bytes 131104 | tf_op jit(solution)/shard_map/ppermute | solution.py:195
  68.7 14.7 %all_to_all.15 = f32[16,32,128]{2,1,0:T(8,128)S(1)} all-to-all(f32[16,32,128]{2,1,0:T(8,128)S(1)} %bitcast.23), channel_id=1, replica_groups=mesh['z'=8,'yl'=2,'x'=4,'yh'=2,'c'=2] {'yl','x','yh'}, dimensions={0} | all-to-all | bytes 524288 | tf_op jit(solution)/shard_map/all_to_all | solution.py:267
  83.4 1.3 %shard_map.51 = f32[64,1024]{1,0:T(8,128)} custom-call(f32[2,4,2,32,128]{4,3,2,1,0:T(8,128)S(1)} %bitcast.22), custom_call_target="tpu_custom_call" | custom-call | tf_op jit(solution)/shard_map/pallas_call | solution.py:270
  (17 shorter events, 0.2 us)
Async XLA Ops:
  0.0 15.8 %copy-start = (s32[64]{0:T(128)S(1)}, s32[64]{0:T(128)}, u32[]{:S(2)}) copy-start(s32[64]{0:T(128)} %counts_in.1) | copy-start | bytes 772
  2.3 25.3 %all-to-all-start = ((bf16[64,9,2,128]{3,2,1,0:T(2,128)(2,1)}), bf16[64,9,2,128]{3,2,1,0:T(2,128)(2,1)S(1)}, u32[]{:S(2)}, u32[]{:S(2)}) async-start(bf16[64,9,2,128]{3,2,1,0:T(2,128)(2,1)} %shard_map.47), calls=%async_computation | async-start | bytes 589824 | tf_op jit(solution)/shard_map/all_to_all | solution.py:223
  29.3 6.4 %collective-permute-start = (bf16[17,16,128]{2,1,0:T(8,128)(2,1)S(1)}, bf16[17,16,128]{2,1,0:T(8,128)(2,1)S(1)}, u32[]{:S(2)}, u32[]{:S(2)}) collective-permute-start(bf16[17,16,128]{2,1,0:T(8,128)(2,1)S(1)} %get-tuple-element.12), channel_id=1, source_target_pairs={{224,0},{0,32},{32,64},{64,96},{96,128},{128,160},{160,192},{192,2... | collective-permute-start | bytes 208904 | tf_op jit(solution)/shard_map/ppermute | solution.py:195
  29.3 27.2 %all-to-all-start.1 = ((bf16[16,17,16,128]{3,2,1,0:T(8,128)(2,1)}), bf16[16,17,16,128]{3,2,1,0:T(8,128)(2,1)S(1)}, u32[]{:S(2)}, u32[]{:S(2)}) async-start(bf16[16,17,16,128]{3,2,1,0:T(8,128)(2,1)} %get-tuple-element.9), calls=%async_computation.1 | async-start | bytes 2228224 | tf_op jit(solution)/shard_map/all_to_all | solution.py:235
  35.7 4.4 %collective-permute-start.1 = (bf16[17,16,128]{2,1,0:T(8,128)(2,1)S(1)}, bf16[17,16,128]{2,1,0:T(8,128)(2,1)S(1)}, u32[]{:S(2)}, u32[]{:S(2)}) collective-permute-start(bf16[17,16,128]{2,1,0:T(8,128)(2,1)S(1)} %collective-permute-done), channel_id=1, source_target_pairs={{224,0},{0,32},{32,64},{64,96},{96,128},{128,160},{160,192},{192,2... | collective-permute-start | bytes 208904 | tf_op jit(solution)/shard_map/ppermute | solution.py:195
  35.8 4.3 %collective-permute-start.4 = (bf16[17,16,128]{2,1,0:T(8,128)(2,1)S(1)}, bf16[17,16,128]{2,1,0:T(8,128)(2,1)S(1)}, u32[]{:S(2)}, u32[]{:S(2)}) collective-permute-start(bf16[17,16,128]{2,1,0:T(8,128)(2,1)S(1)} %get-tuple-element.12), channel_id=1, source_target_pairs={{32,0},{64,32},{96,64},{128,96},{160,128},{192,160},{224,192},{0,2... | collective-permute-start | bytes 208904 | tf_op jit(solution)/shard_map/ppermute | solution.py:195
  40.1 4.7 %collective-permute-start.2 = (bf16[17,16,128]{2,1,0:T(8,128)(2,1)S(1)}, bf16[17,16,128]{2,1,0:T(8,128)(2,1)S(1)}, u32[]{:S(2)}, u32[]{:S(2)}) collective-permute-start(bf16[17,16,128]{2,1,0:T(8,128)(2,1)S(1)} %collective-permute-done.1), channel_id=1, source_target_pairs={{224,0},{0,32},{32,64},{64,96},{96,128},{128,160},{160,192},{192,2... | collective-permute-start | bytes 208904 | tf_op jit(solution)/shard_map/ppermute | solution.py:195
  40.2 4.7 %collective-permute-start.5 = (bf16[17,16,128]{2,1,0:T(8,128)(2,1)S(1)}, bf16[17,16,128]{2,1,0:T(8,128)(2,1)S(1)}, u32[]{:S(2)}, u32[]{:S(2)}) collective-permute-start(bf16[17,16,128]{2,1,0:T(8,128)(2,1)S(1)} %collective-permute-done.4), channel_id=1, source_target_pairs={{32,0},{64,32},{96,64},{128,96},{160,128},{192,160},{224,192},{0,2... | collective-permute-start | bytes 208904 | tf_op jit(solution)/shard_map/ppermute | solution.py:195
  44.8 5.4 %collective-permute-start.3 = (bf16[17,16,128]{2,1,0:T(8,128)(2,1)S(1)}, bf16[17,16,128]{2,1,0:T(8,128)(2,1)S(1)}, u32[]{:S(2)}, u32[]{:S(2)}) collective-permute-start(bf16[17,16,128]{2,1,0:T(8,128)(2,1)S(1)} %collective-permute-done.2), channel_id=1, source_target_pairs={{224,0},{0,32},{32,64},{64,96},{96,128},{128,160},{160,192},{192,2... | collective-permute-start | bytes 208904 | tf_op jit(solution)/shard_map/ppermute | solution.py:195
  44.8 5.3 %collective-permute-start.6 = (bf16[17,16,128]{2,1,0:T(8,128)(2,1)S(1)}, bf16[17,16,128]{2,1,0:T(8,128)(2,1)S(1)}, u32[]{:S(2)}, u32[]{:S(2)}) collective-permute-start(bf16[17,16,128]{2,1,0:T(8,128)(2,1)S(1)} %collective-permute-done.5), channel_id=1, source_target_pairs={{32,0},{64,32},{96,64},{128,96},{160,128},{192,160},{224,192},{0,2... | collective-permute-start | bytes 208904 | tf_op jit(solution)/shard_map/ppermute | solution.py:195
  50.2 10.9 %collective-permute-start.7 = (bf16[8,17,16,128]{3,2,1,0:T(8,128)(2,1)S(1)}, bf16[8,17,16,128]{3,2,1,0:T(8,128)(2,1)S(1)}, u32[]{:S(2)}, u32[]{:S(2)}) collective-permute-start(bf16[8,17,16,128]{3,2,1,0:T(8,128)(2,1)S(1)} %bitcast_dynamic-update-slice_fusion.own), channel_id=1, source_target_pairs={{1,0},{0,1},{3,2},{2,3},{5,4},{4,5},{7,6},{6,7},{9,8},{8,9},{11,10... | collective-permute-start | bytes 1671176 | tf_op jit(solution)/shard_map/ppermute | solution.py:195
  67.2 1.4 %collective-permute-start.8 = (f32[4,2,32,128]{3,2,1,0:T(8,128)S(1)}, f32[4,2,32,128]{3,2,1,0:T(8,128)S(1)}, u32[]{:S(2)}, u32[]{:S(2)}) collective-permute-start(f32[4,2,32,128]{3,2,1,0:T(8,128)S(1)} %get-tuple-element.14), channel_id=1, source_target_pairs={{1,0},{0,1},{3,2},{2,3},{5,4},{4,5},{7,6},{6,7},{9,8},{8,9},{11,10... | collective-permute-start | bytes 393224 | tf_op jit(solution)/shard_map/ppermute | solution.py:195

commit v3 on v2

--- a/solution.py
+++ b/solution.py
@@ -1,3 +1,5 @@
+import functools
+
 import jax
 import jax.numpy as jnp
 from jax import lax
@@ -15,6 +17,10 @@
 VMEM = pl.BlockSpec(memory_space=pltpu.VMEM)
 ANY = pl.BlockSpec(memory_space=pl.ANY)
 SMEM = pl.BlockSpec(memory_space=pltpu.SMEM)
+
+
+def cost(pieces):
+    return pl.CostEstimate(flops=2 * 4096 * 256 * pieces * LANES, bytes_accessed=2**21, transcendentals=0)
 
 
 def params(mib):
@@ -98,59 +104,60 @@
         spread[j] = whole
 
 
-def compare(rows, pieces, row_codes, piece_codes, acc):
+def compare(rows, pieces, chosen, row_codes, piece_codes, acc):
     for j in range(16):
         row_codes[j * 16 : j * 16 + 16, :] = rows[j, TILES].astype(F32)
     across = jnp.transpose(row_codes[...], (1, 0))
     row_codes[0:128, :] = across[:, 0:128]
     row_codes[128:256, :] = across[:, 128:256]
     piece_norms = []
-    for d in range(8):
-        codes = pieces[d, TILES].astype(F32)
+    for d, place in enumerate(chosen):
+        codes = pieces[place, TILES].astype(F32)
         for k in range(TILES):
             piece_codes[d, k] = jnp.broadcast_to(codes[:, k : k + 1], (16, LANES))
         norms = codes[:, 16:17] + codes[:, 17:18] + codes[:, 18:19]
         piece_norms.append(jnp.broadcast_to(norms, (16, 256)))
     acc[...] = jnp.zeros_like(acc)
-
     for k in range(TILES):
         weights = jnp.transpose(rows[:, k].reshape(256, LANES), (1, 0))
         codes_k = jnp.concatenate(
             [row_codes[pl.ds(k, 1), :], row_codes[pl.ds(128 + k, 1), :]], axis=1
         )
-        for d in range(8):
-            left = pieces[d, 0:TILES].reshape(256, LANES)
+        for d, place in enumerate(chosen):
+            left = pieces[place, 0:TILES].reshape(256, LANES)
             product = jnp.dot(left, weights, preferred_element_type=F32)
             codes_d = piece_codes[d].reshape(256, LANES)
             same = jnp.concatenate([codes_d, codes_d], axis=1) == codes_k
             product = jnp.where(same, product, 0.0).reshape(TILES, 16, 256)
             acc[d] += jnp.sum(product, axis=0)
-
     norms_across = across[16:17] + across[17:18] + across[18:19]
-    for d in range(8):
+    for d in range(len(chosen)):
         acc[d] = acc[d] / (piece_norms[d] + norms_across - acc[d])
 
 
 def own_kernel(rows, own, out, row_codes, piece_codes):
-    compare(rows, own, row_codes, piece_codes, out)
-
-
-def other_kernel(rows, other, own_ratio, out, row_codes, piece_codes, acc, tall):
+    compare(rows, own, list(range(8)), row_codes, piece_codes, out)
+
+
+def other_kernel(kept, rows, other, own_ratio, out, row_codes, piece_codes, acc, tall):
     x, c = lax.axis_index("x"), lax.axis_index("c")
-    compare(rows, other, row_codes, piece_codes, acc)
-    for u in range(16):
-        tall[u * 16 : u * 16 + 16, :] = own_ratio[u // 2] if u % 2 == 0 else acc[((u + 1) // 2 - c) & 7]
+    core = c if kept else 1 - c
+    odd = [4 * core + 1, 4 * core + 3, 4 * core + 9, 4 * core + 11]
+    chosen = [(((u + 1) >> 1) - c) & 7 for u in odd]
+    compare(rows, other, chosen, row_codes, piece_codes, acc)
     low_lanes = lax.broadcasted_iota(jnp.int32, (32, LANES), 1) < 64
-    for panel in range(4):
-        if panel % 2 == 0:
-            wide = jnp.transpose(tall[:, panel * 64 : panel * 64 + 128], (1, 0))
-        ratio = wide[(panel % 2) * 64 : (panel % 2) * 64 + 64]
-        ratio = jnp.where(panel < x, pltpu.roll(ratio, 240, 1), ratio)
-        for half in range(2):
-            first = ratio[0:32, half * 128 : half * 128 + 128]
-            second = ratio[32:64, half * 128 : half * 128 + 128]
-            out[0, panel, half] = jnp.where(low_lanes, first, pltpu.roll(second, 64, 1))
-            out[1, panel, half] = jnp.where(low_lanes, pltpu.roll(first, 64, 1), second)
+    for half in range(2):
+        for i in range(5):
+            if i % 2 == 0:
+                part = own_ratio[(4 * half + 2 * core + i // 2) & 7]
+            else:
+                part = acc[2 * half + i // 2]
+            tall[half, i * 16 : i * 16 + 16, :] = part
+        wide = jnp.transpose(tall[half], (1, 0))
+        for panel in range(4):
+            ratio = wide[panel * 64 : panel * 64 + 64]
+            ratio = jnp.where(panel < x, pltpu.roll(ratio, 112, 1), ratio)
+            out[panel, half] = jnp.where(low_lanes, ratio[0:32], pltpu.roll(ratio[32:64], 64, 1))
 
 
 def place_kernel(arrived, out, tall):
@@ -241,28 +248,34 @@
         ring[distance + 1], ring[8 - distance] = behind, ahead
     own = jnp.stack(ring)
     other = step(own, "c", 1)
-    codes_scratch = [pltpu.VMEM((256, LANES), F32), pltpu.VMEM((8, TILES, 16, LANES), F32)]
-    cost = pl.CostEstimate(flops=2 * 4096 * 2048 * LANES, bytes_accessed=2**21, transcendentals=0)
     own_ratio = pl.pallas_call(
         own_kernel,
         out_shape=jax.ShapeDtypeStruct((8, 16, 256), F32),
         in_specs=[VMEM, VMEM],
         out_specs=VMEM,
-        scratch_shapes=codes_scratch,
+        scratch_shapes=[pltpu.VMEM((256, LANES), F32), pltpu.VMEM((8, TILES, 16, LANES), F32)],
         compiler_params=params(32),
-        cost_estimate=cost,
+        cost_estimate=cost(8),
     )(rows, own)
-    blocks = pl.pallas_call(
-        other_kernel,
-        out_shape=jax.ShapeDtypeStruct((2, 4, 2, 32, LANES), F32),
-        in_specs=[VMEM, VMEM, VMEM],
-        out_specs=VMEM,
-        scratch_shapes=codes_scratch + [pltpu.VMEM((8, 16, 256), F32), pltpu.VMEM((256, 256), F32)],
-        compiler_params=params(32),
-        cost_estimate=cost,
-    )(rows, other, own_ratio)
-    swapped = step(blocks[1 - c], "c", 1)
-    kept = blocks[c]
+
+    def finish(kept):
+        return pl.pallas_call(
+            functools.partial(other_kernel, kept),
+            out_shape=jax.ShapeDtypeStruct((4, 2, 32, LANES), F32),
+            in_specs=[VMEM, VMEM, VMEM],
+            out_specs=VMEM,
+            scratch_shapes=[
+                pltpu.VMEM((256, LANES), F32),
+                pltpu.VMEM((4, TILES, 16, LANES), F32),
+                pltpu.VMEM((4, 16, 256), F32),
+                pltpu.VMEM((2, LANES, 256), F32),
+            ],
+            compiler_params=params(32),
+            cost_estimate=cost(4),
+        )(rows, other, own_ratio)
+
+    swapped = step(finish(False), "c", 1)
+    kept = finish(True)
     results = jnp.where(c == 0, jnp.stack([kept, swapped]), jnp.stack([swapped, kept]))
     results = lax.all_to_all(
         results.reshape(16, 32, LANES), ("yl", "x", "yh"), 0, 0, tiled=True

time: 85 us -> 83.8 us (0.986)
  waiting for transfers between devices: 17.8 us -> 16.5 us
    ppermute x9, waiting for transfers between devices: 7.35 us -> 6.03 us  [step(): lax.ppermute(block, axis, [((i - distance) % size, i) for i in range(size)])]
    pallas_call x1 -> x2, Pallas kernels: 6.01 us -> 6.31 us  [finish(): pl.pallas_call(functools.partial(other_kernel, kept), out_shape=jax.Shape...]
  transfers between devices with their start and end apart: 11 -> 11, of which waited for: 5 -> 4; matrix products, arithmetic and copies ran while one was open for 0% -> 0% of each run, Pallas kernels for 7% -> 11%
where the time goes in v3:
time: 83.8 us; the launch traced here: 83.5 us
  starting transfers between devices  34.6 us (41%)
  Pallas kernels  17.6 us (21%)
  waiting for transfers between devices  16.5 us (20%)
  blocking collectives  14.5 us (17%)
    ppermute x9, starting transfers between devices, step(): lax.ppermute(block, axis, [((i - distance) % size, i) for i in range(size)])  14.7 us
    all_to_all x1, blocking collectives, on_device(): lax.all_to_all(results.reshape(16, 32, LANES), ('yl', 'x', 'yh'), 0, 0, t...  14.5 us
    all_to_all x1, starting transfers between devices, on_device(): arrived = lax.all_to_all(sending, ('z', 'yl', 'x'), 0, 0, tiled=True)  13.5 us
    all_to_all x1, waiting for transfers between devices, on_device(): arrived = lax.all_to_all(sending, ('z', 'yl', 'x'), 0, 0, tiled=True)  10.5 us
    all_to_all x1, starting transfers between devices, on_device(): rows = lax.all_to_all(spread, ('x', 'yh', 'yl'), 0, 0, tiled=True)  6.37 us
    pallas_call x2, Pallas kernels, finish(): pl.pallas_call(functools.partial(other_kernel, kept), out_shape=jax.Shape...  6.31 us
    ppermute x9, waiting for transfers between devices, step(): lax.ppermute(block, axis, [((i - distance) % size, i) for i in range(size)])  6.03 us
    pallas_call x1, Pallas kernels, on_device(): pl.pallas_call(own_kernel, out_shape=jax.ShapeDtypeStruct((8, 16, 256), F...  4.63 us
  transfers between devices with their start and end apart: 11, of which 4 were waited for; matrix products, arithmetic and copies ran while one was open for 0% of the time, Pallas kernels for 11%

profile of v3, /device:TPU:1, one launch (start us, length us, event | category | flops | bytes accessed | tf_op | source)
XLA Modules:
  0.0 83.5 jit_solution(4951162468599413137)
XLA Ops:
  0.0 2.2 %shard_map.47 = bf16[64,9,2,128]{3,2,1,0:T(2,128)(2,1)} custom-call(s32[64]{0:T(128)} %counts_in.1, s32[128]{0:T(128)} %tiles_in.1, s32[16,128]{1,0:T(8,128)} %bitcast.25, bf16[128,16,128]{2,1,0:T(8,128)(2,1)} %values_in.1), custom_call_target="tpu_custom_call" | custom-call | tf_op jit(solution)/shard_map/pallas_call | solution.py:207
  2.3 13.5 %all-to-all-start = ((bf16[64,9,2,128]{3,2,1,0:T(2,128)(2,1)}), bf16[64,9,2,128]{3,2,1,0:T(2,128)(2,1)S(1)}, u32[]{:S(2)}, u32[]{:S(2)}) async-start(bf16[64,9,2,128]{3,2,1,0:T(2,128)(2,1)} %shard_map.47), calls=%async_computation | async-start | bytes 589824 | tf_op jit(solution)/shard_map/all_to_all | solution.py:230
  15.8 1.4 %shard_map.46.source = s32[16]{0:T(128)S(1)} custom-call(s32[64]{0:T(128)S(1)} %copy-done), custom_call_target="tpu_custom_call" | custom-call | flops 1073741824 | bytes 1048576 | tf_op jit(solution)/shard_map/pallas_call | solution.py:222
  17.1 10.5 %all-to-all-done.arrived = bf16[64,9,2,128]{3,2,1,0:T(2,128)(2,1)S(1)} async-done(((bf16[64,9,2,128]{3,2,1,0:T(2,128)(2,1)}), bf16[64,9,2,128]{3,2,1,0:T(2,128)(2,1)S(1)}, u32[]{:S(2)}, u32[]{:S(2)}) %all-to-all-start) | async-done | bytes 294944 | tf_op jit(solution)/shard_map/all_to_all | solution.py:230
  27.6 1.7 %shard_map.48 = (bf16[17,16,128]{2,1,0:T(8,128)(2,1)S(1)}, bf16[16,17,16,128]{3,2,1,0:T(8,128)(2,1)}) custom-call(s32[16]{0:T(128)S(1)} %shard_map.46.source, bf16[64,9,2,128]{3,2,1,0:T(2,128)(2,1)S(1)} %all-to-all-done.arrived), custom_call_target="tpu_custom_call" | custom-call | tf_op jit(solution)/shard_map/pallas_call | solution.py:231
  29.3 0.0 collective-permute-start
  29.3 6.4 %all-to-all-start.1 = ((bf16[16,17,16,128]{3,2,1,0:T(8,128)(2,1)}), bf16[16,17,16,128]{3,2,1,0:T(8,128)(2,1)S(1)}, u32[]{:S(2)}, u32[]{:S(2)}) async-start(bf16[16,17,16,128]{3,2,1,0:T(8,128)(2,1)} %get-tuple-element.9), calls=%async_computation.1 | async-start | bytes 2228224 | tf_op jit(solution)/shard_map/all_to_all | solution.py:242
  35.7 0.0 collective-permute-done
  35.7 0.1 collective-permute-start.1
  35.8 2.6 %collective-permute-start.4 = (bf16[17,16,128]{2,1,0:T(8,128)(2,1)S(1)}, bf16[17,16,128]{2,1,0:T(8,128)(2,1)S(1)}, u32[]{:S(2)}, u32[]{:S(2)}) collective-permute-start(bf16[17,16,128]{2,1,0:T(8,128)(2,1)S(1)} %get-tuple-element.12), channel_id=1, source_target_pairs={{32,0},{64,32},{96,64},{128,96},{160,128},{192,160},{224,192},{0,2... | collective-permute-start | bytes 208904 | tf_op jit(solution)/shard_map/ppermute | solution.py:202
  38.5 1.7 %collective-permute-done.1 = bf16[17,16,128]{2,1,0:T(8,128)(2,1)S(1)} collective-permute-done((bf16[17,16,128]{2,1,0:T(8,128)(2,1)S(1)}, bf16[17,16,128]{2,1,0:T(8,128)(2,1)S(1)}, u32[]{:S(2)}, u32[]{:S(2)}) %collective-permute-start.1) | collective-permute-done | bytes 69664 | tf_op jit(solution)/shard_map/ppermute | solution.py:202
  40.2 0.0 collective-permute-start.2
  40.2 2.7 %collective-permute-start.5 = (bf16[17,16,128]{2,1,0:T(8,128)(2,1)S(1)}, bf16[17,16,128]{2,1,0:T(8,128)(2,1)S(1)}, u32[]{:S(2)}, u32[]{:S(2)}) collective-permute-start(bf16[17,16,128]{2,1,0:T(8,128)(2,1)S(1)} %collective-permute-done.4), channel_id=1, source_target_pairs={{32,0},{64,32},{96,64},{128,96},{160,128},{192,160},{224,192},{0,2... | collective-permute-start | bytes 208904 | tf_op jit(solution)/shard_map/ppermute | solution.py:202
  42.9 1.9 %collective-permute-done.2 = bf16[17,16,128]{2,1,0:T(8,128)(2,1)S(1)} collective-permute-done((bf16[17,16,128]{2,1,0:T(8,128)(2,1)S(1)}, bf16[17,16,128]{2,1,0:T(8,128)(2,1)S(1)}, u32[]{:S(2)}, u32[]{:S(2)}) %collective-permute-start.2) | collective-permute-done | bytes 69664 | tf_op jit(solution)/shard_map/ppermute | solution.py:202
  44.8 0.0 collective-permute-done.5
  44.8 2.9 %collective-permute-start.6 = (bf16[17,16,128]{2,1,0:T(8,128)(2,1)S(1)}, bf16[17,16,128]{2,1,0:T(8,128)(2,1)S(1)}, u32[]{:S(2)}, u32[]{:S(2)}) collective-permute-start(bf16[17,16,128]{2,1,0:T(8,128)(2,1)S(1)} %collective-permute-done.5), channel_id=1, source_target_pairs={{32,0},{64,32},{96,64},{128,96},{160,128},{192,160},{224,192},{0,2... | collective-permute-start | bytes 208904 | tf_op jit(solution)/shard_map/ppermute | solution.py:202
  47.7 2.4 %collective-permute-done.3 = bf16[17,16,128]{2,1,0:T(8,128)(2,1)S(1)} collective-permute-done((bf16[17,16,128]{2,1,0:T(8,128)(2,1)S(1)}, bf16[17,16,128]{2,1,0:T(8,128)(2,1)S(1)}, u32[]{:S(2)}, u32[]{:S(2)}) %collective-permute-start.3) | collective-permute-done | bytes 69664 | tf_op jit(solution)/shard_map/ppermute | solution.py:202
  50.3 6.2 %collective-permute-start.7 = (bf16[8,17,16,128]{3,2,1,0:T(8,128)(2,1)S(1)}, bf16[8,17,16,128]{3,2,1,0:T(8,128)(2,1)S(1)}, u32[]{:S(2)}, u32[]{:S(2)}) collective-permute-start(bf16[8,17,16,128]{3,2,1,0:T(8,128)(2,1)S(1)} %bitcast_dynamic-update-slice_fusion.own), channel_id=1, source_target_pairs={{1,0},{0,1},{3,2},{2,3},{5,4},{4,5},{7,6},{6,7},{9,8},{8,9},{11,10... | collective-permute-start | bytes 1671176 | tf_op jit(solution)/shard_map/ppermute | solution.py:202
  56.5 4.6 %shard_map.49.own_ratio = f32[8,16,256]{2,1,0:T(8,128)S(1)} custom-call(bf16[16,17,16,128]{3,2,1,0:T(8,128)(2,1)S(1)} %all-to-all-done.1.rows, bf16[8,17,16,128]{3,2,1,0:T(8,128)(2,1)S(1)} %bitcast_dynamic-update-slice_fusion.own), custom_call_target="tpu_custom_call" | custom-call | flops 2147483648 | bytes 2097152 | tf_op jit(solution)/shard_map/pallas_call | solution.py:251
  61.2 3.1 %shard_map.51 = f32[4,2,32,128]{3,2,1,0:T(8,128)S(1)} custom-call(bf16[16,17,16,128]{3,2,1,0:T(8,128)(2,1)S(1)} %all-to-all-done.1.rows, bf16[8,17,16,128]{3,2,1,0:T(8,128)(2,1)S(1)} %collective-permute-done.7.other, f32[8,16,256]{2,1,0:T(8,128)S(1)} %shard_map.49.own_ratio), custom_call_target="tpu_custom_call" | custom-call | flops 1073741824 | bytes 2097152 | tf_op jit(solution)/shard_map/pallas_call | solution.py:262
  64.3 0.1 collective-permute-start.8
  64.4 3.2 %shard_map.50 = f32[4,2,32,128]{3,2,1,0:T(8,128)S(1)} custom-call(bf16[16,17,16,128]{3,2,1,0:T(8,128)(2,1)S(1)} %all-to-all-done.1.rows, bf16[8,17,16,128]{3,2,1,0:T(8,128)(2,1)S(1)} %collective-permute-done.7.other, f32[8,16,256]{2,1,0:T(8,128)S(1)} %shard_map.49.own_ratio), custom_call_target="tpu_custom_call" | custom-call | flops 1073741824 | bytes 2097152 | tf_op jit(solution)/shard_map/pallas_call | solution.py:262
  67.6 14.5 %all_to_all.15 = f32[16,32,128]{2,1,0:T(8,128)S(1)} all-to-all(f32[16,32,128]{2,1,0:T(8,128)S(1)} %bitcast.23), channel_id=1, replica_groups=mesh['z'=8,'yl'=2,'x'=4,'yh'=2,'c'=2] {'yl','x','yh'}, dimensions={0} | all-to-all | bytes 524288 | tf_op jit(solution)/shard_map/all_to_all | solution.py:280
  82.2 1.3 %shard_map.52 = f32[64,1024]{1,0:T(8,128)} custom-call(f32[2,4,2,32,128]{4,3,2,1,0:T(8,128)S(1)} %bitcast.21), custom_call_target="tpu_custom_call" | custom-call | tf_op jit(solution)/shard_map/pallas_call | solution.py:283
  (17 shorter events, 0.1 us)
Async XLA Ops:
  0.0 15.8 %copy-start = (s32[64]{0:T(128)S(1)}, s32[64]{0:T(128)}, u32[]{:S(2)}) copy-start(s32[64]{0:T(128)} %counts_in.1) | copy-start | bytes 772
  2.3 25.3 %all-to-all-start = ((bf16[64,9,2,128]{3,2,1,0:T(2,128)(2,1)}), bf16[64,9,2,128]{3,2,1,0:T(2,128)(2,1)S(1)}, u32[]{:S(2)}, u32[]{:S(2)}) async-start(bf16[64,9,2,128]{3,2,1,0:T(2,128)(2,1)} %shard_map.47), calls=%async_computation | async-start | bytes 589824 | tf_op jit(solution)/shard_map/all_to_all | solution.py:230
  29.3 6.4 %collective-permute-start = (bf16[17,16,128]{2,1,0:T(8,128)(2,1)S(1)}, bf16[17,16,128]{2,1,0:T(8,128)(2,1)S(1)}, u32[]{:S(2)}, u32[]{:S(2)}) collective-permute-start(bf16[17,16,128]{2,1,0:T(8,128)(2,1)S(1)} %get-tuple-element.12), channel_id=1, source_target_pairs={{224,0},{0,32},{32,64},{64,96},{96,128},{128,160},{160,192},{192,2... | collective-permute-start | bytes 208904 | tf_op jit(solution)/shard_map/ppermute | solution.py:202
  29.3 27.2 %all-to-all-start.1 = ((bf16[16,17,16,128]{3,2,1,0:T(8,128)(2,1)}), bf16[16,17,16,128]{3,2,1,0:T(8,128)(2,1)S(1)}, u32[]{:S(2)}, u32[]{:S(2)}) async-start(bf16[16,17,16,128]{3,2,1,0:T(8,128)(2,1)} %get-tuple-element.9), calls=%async_computation.1 | async-start | bytes 2228224 | tf_op jit(solution)/shard_map/all_to_all | solution.py:242
  35.7 4.4 %collective-permute-start.1 = (bf16[17,16,128]{2,1,0:T(8,128)(2,1)S(1)}, bf16[17,16,128]{2,1,0:T(8,128)(2,1)S(1)}, u32[]{:S(2)}, u32[]{:S(2)}) collective-permute-start(bf16[17,16,128]{2,1,0:T(8,128)(2,1)S(1)} %collective-permute-done), channel_id=1, source_target_pairs={{224,0},{0,32},{32,64},{64,96},{96,128},{128,160},{160,192},{192,2... | collective-permute-start | bytes 208904 | tf_op jit(solution)/shard_map/ppermute | solution.py:202
  35.8 4.3 %collective-permute-start.4 = (bf16[17,16,128]{2,1,0:T(8,128)(2,1)S(1)}, bf16[17,16,128]{2,1,0:T(8,128)(2,1)S(1)}, u32[]{:S(2)}, u32[]{:S(2)}) collective-permute-start(bf16[17,16,128]{2,1,0:T(8,128)(2,1)S(1)} %get-tuple-element.12), channel_id=1, source_target_pairs={{32,0},{64,32},{96,64},{128,96},{160,128},{192,160},{224,192},{0,2... | collective-permute-start | bytes 208904 | tf_op jit(solution)/shard_map/ppermute | solution.py:202
  40.2 4.7 %collective-permute-start.2 = (bf16[17,16,128]{2,1,0:T(8,128)(2,1)S(1)}, bf16[17,16,128]{2,1,0:T(8,128)(2,1)S(1)}, u32[]{:S(2)}, u32[]{:S(2)}) collective-permute-start(bf16[17,16,128]{2,1,0:T(8,128)(2,1)S(1)} %collective-permute-done.1), channel_id=1, source_target_pairs={{224,0},{0,32},{32,64},{64,96},{96,128},{128,160},{160,192},{192,2... | collective-permute-start | bytes 208904 | tf_op jit(solution)/shard_map/ppermute | solution.py:202
  40.2 4.7 %collective-permute-start.5 = (bf16[17,16,128]{2,1,0:T(8,128)(2,1)S(1)}, bf16[17,16,128]{2,1,0:T(8,128)(2,1)S(1)}, u32[]{:S(2)}, u32[]{:S(2)}) collective-permute-start(bf16[17,16,128]{2,1,0:T(8,128)(2,1)S(1)} %collective-permute-done.4), channel_id=1, source_target_pairs={{32,0},{64,32},{96,64},{128,96},{160,128},{192,160},{224,192},{0,2... | collective-permute-start | bytes 208904 | tf_op jit(solution)/shard_map/ppermute | solution.py:202
  44.8 5.4 %collective-permute-start.3 = (bf16[17,16,128]{2,1,0:T(8,128)(2,1)S(1)}, bf16[17,16,128]{2,1,0:T(8,128)(2,1)S(1)}, u32[]{:S(2)}, u32[]{:S(2)}) collective-permute-start(bf16[17,16,128]{2,1,0:T(8,128)(2,1)S(1)} %collective-permute-done.2), channel_id=1, source_target_pairs={{224,0},{0,32},{32,64},{64,96},{96,128},{128,160},{160,192},{192,2... | collective-permute-start | bytes 208904 | tf_op jit(solution)/shard_map/ppermute | solution.py:202
  44.8 5.3 %collective-permute-start.6 = (bf16[17,16,128]{2,1,0:T(8,128)(2,1)S(1)}, bf16[17,16,128]{2,1,0:T(8,128)(2,1)S(1)}, u32[]{:S(2)}, u32[]{:S(2)}) collective-permute-start(bf16[17,16,128]{2,1,0:T(8,128)(2,1)S(1)} %collective-permute-done.5), channel_id=1, source_target_pairs={{32,0},{64,32},{96,64},{128,96},{160,128},{192,160},{224,192},{0,2... | collective-permute-start | bytes 208904 | tf_op jit(solution)/shard_map/ppermute | solution.py:202
  50.3 10.9 %collective-permute-start.7 = (bf16[8,17,16,128]{3,2,1,0:T(8,128)(2,1)S(1)}, bf16[8,17,16,128]{3,2,1,0:T(8,128)(2,1)S(1)}, u32[]{:S(2)}, u32[]{:S(2)}) collective-permute-start(bf16[8,17,16,128]{3,2,1,0:T(8,128)(2,1)S(1)} %bitcast_dynamic-update-slice_fusion.own), channel_id=1, source_target_pairs={{1,0},{0,1},{3,2},{2,3},{5,4},{4,5},{7,6},{6,7},{9,8},{8,9},{11,10... | collective-permute-start | bytes 1671176 | tf_op jit(solution)/shard_map/ppermute | solution.py:202
  64.3 3.3 %collective-permute-start.8 = (f32[4,2,32,128]{3,2,1,0:T(8,128)S(1)}, f32[4,2,32,128]{3,2,1,0:T(8,128)S(1)}, u32[]{:S(2)}, u32[]{:S(2)}) collective-permute-start(f32[4,2,32,128]{3,2,1,0:T(8,128)S(1)} %shard_map.51), channel_id=1, source_target_pairs={{1,0},{0,1},{3,2},{2,3},{5,4},{4,5},{7,6},{6,7},{9,8},{8,9},{11,10... | collective-permute-start | bytes 393224 | tf_op jit(solution)/shard_map/ppermute | solution.py:202

commit v4 on v3

--- a/solution.py
+++ b/solution.py
@@ -12,6 +12,7 @@
 LANES = 128
 SENT = 18
 PIECE = TILES + 1
+EARLY, LATE = (0, 1, 2, 3, 6, 7), (4, 5)
 BF16 = jnp.bfloat16
 F32 = jnp.float32
 VMEM = pl.BlockSpec(memory_space=pltpu.VMEM)
@@ -136,15 +137,30 @@
 
 
 def own_kernel(rows, own, out, row_codes, piece_codes):
-    compare(rows, own, list(range(8)), row_codes, piece_codes, out)
-
-
-def other_kernel(kept, rows, other, own_ratio, out, row_codes, piece_codes, acc, tall):
+    compare(rows, own, list(range(own.shape[0])), row_codes, piece_codes, out)
+
+
+def other_kernel(
+    kept, rows, early, late, early_ratio, late_ratio, out, row_codes, piece_codes, acc, tall, picked, own_ratio
+):
     x, c = lax.axis_index("x"), lax.axis_index("c")
     core = c if kept else 1 - c
     odd = [4 * core + 1, 4 * core + 3, 4 * core + 9, 4 * core + 11]
     chosen = [(((u + 1) >> 1) - c) & 7 for u in odd]
-    compare(rows, other, chosen, row_codes, piece_codes, acc)
+    for d, place in enumerate(chosen):
+        is_late = (place >> 1) == 2
+
+        @pl.when(is_late)
+        def _():
+            picked[d] = late[place & 1]
+
+        @pl.when(jnp.logical_not(is_late))
+        def _():
+            picked[d] = early[jnp.where(place > 3, place - 2, place)]
+
+    for d in range(8):
+        own_ratio[d] = late_ratio[d - 4] if d // 2 == 2 else early_ratio[EARLY.index(d)]
+    compare(rows, picked, list(range(4)), row_codes, piece_codes, acc)
     low_lanes = lax.broadcasted_iota(jnp.int32, (32, LANES), 1) < 64
     for half in range(2):
         for i in range(5):
@@ -246,33 +262,43 @@
     for distance in range(1, 4):
         behind, ahead = step(behind, "z", 1), step(ahead, "z", -1)
         ring[distance + 1], ring[8 - distance] = behind, ahead
-    own = jnp.stack(ring)
-    other = step(own, "c", 1)
-    own_ratio = pl.pallas_call(
-        own_kernel,
-        out_shape=jax.ShapeDtypeStruct((8, 16, 256), F32),
-        in_specs=[VMEM, VMEM],
-        out_specs=VMEM,
-        scratch_shapes=[pltpu.VMEM((256, LANES), F32), pltpu.VMEM((8, TILES, 16, LANES), F32)],
-        compiler_params=params(32),
-        cost_estimate=cost(8),
-    )(rows, own)
+    def compare_own(own):
+        count = own.shape[0]
+        return pl.pallas_call(
+            own_kernel,
+            out_shape=jax.ShapeDtypeStruct((count, 16, 256), F32),
+            in_specs=[VMEM, VMEM],
+            out_specs=VMEM,
+            scratch_shapes=[pltpu.VMEM((256, LANES), F32), pltpu.VMEM((count, TILES, 16, LANES), F32)],
+            compiler_params=params(32),
+            cost_estimate=cost(count),
+        )(rows, own)
+
+    early = jnp.stack([ring[d] for d in EARLY])
+    other_early = step(early, "c", 1)
+    early_ratio = compare_own(early)
+    early_ratio, *last = lax.optimization_barrier((early_ratio, *(ring[d] for d in LATE)))
+    late = jnp.stack(last)
+    other_late = step(late, "c", 1)
+    late_ratio = compare_own(late)
 
     def finish(kept):
         return pl.pallas_call(
             functools.partial(other_kernel, kept),
             out_shape=jax.ShapeDtypeStruct((4, 2, 32, LANES), F32),
-            in_specs=[VMEM, VMEM, VMEM],
+            in_specs=[VMEM] * 5,
             out_specs=VMEM,
             scratch_shapes=[
                 pltpu.VMEM((256, LANES), F32),
                 pltpu.VMEM((4, TILES, 16, LANES), F32),
                 pltpu.VMEM((4, 16, 256), F32),
                 pltpu.VMEM((2, LANES, 256), F32),
+                pltpu.VMEM((4, PIECE, 16, LANES), BF16),
+                pltpu.VMEM((8, 16, 256), F32),
             ],
             compiler_params=params(32),
             cost_estimate=cost(4),
-        )(rows, other, own_ratio)
+        )(rows, other_early, other_late, early_ratio, late_ratio)
 
     swapped = step(finish(False), "c", 1)
     kept = finish(True)

time: 83.8 us -> 81.9 us (0.977)
  waiting for transfers between devices: 16.5 us -> 14 us
  starting transfers between devices: 34.6 us -> 35.5 us
    ppermute x9 -> x10, waiting for transfers between devices: 6.03 us -> 3.59 us  [step(): lax.ppermute(block, axis, [((i - distance) % size, i) for i in range(size)])]
    ppermute x9 -> x10, starting transfers between devices: 14.7 us -> 15.6 us  [step(): lax.ppermute(block, axis, [((i - distance) % size, i) for i in range(size)])]
    pallas_call x1 -> x2, Pallas kernels: 4.63 us -> 4.8 us  [compare_own(): pl.pallas_call(own_kernel, out_shape=jax.ShapeDtypeStruct((count, 16, 256...]
  transfers between devices with their start and end apart: 11 -> 12, of which waited for: 4 -> 3; matrix products, arithmetic and copies ran while one was open for 0% -> 0% of each run, Pallas kernels for 11% -> 11%
where the time goes in v4:
time: 81.9 us; the launch traced here: 81.6 us
  starting transfers between devices  35.5 us (43%)
  Pallas kernels  17.9 us (22%)
  waiting for transfers between devices  14 us (17%)
  blocking collectives  13.9 us (17%)
    ppermute x10, starting transfers between devices, step(): lax.ppermute(block, axis, [((i - distance) % size, i) for i in range(size)])  15.6 us
    all_to_all x1, blocking collectives, on_device(): lax.all_to_all(results.reshape(16, 32, LANES), ('yl', 'x', 'yh'), 0, 0, t...  13.9 us
    all_to_all x1, starting transfers between devices, on_device(): arrived = lax.all_to_all(sending, ('z', 'yl', 'x'), 0, 0, tiled=True)  13.5 us
    all_to_all x1, waiting for transfers between devices, on_device(): arrived = lax.all_to_all(sending, ('z', 'yl', 'x'), 0, 0, tiled=True)  10.5 us
    pallas_call x2, Pallas kernels, finish(): pl.pallas_call(functools.partial(other_kernel, kept), out_shape=jax.Shape...  6.42 us
    all_to_all x1, starting transfers between devices, on_device(): rows = lax.all_to_all(spread, ('x', 'yh', 'yl'), 0, 0, tiled=True)  6.37 us
    pallas_call x2, Pallas kernels, compare_own(): pl.pallas_call(own_kernel, out_shape=jax.ShapeDtypeStruct((count, 16, 256...  4.8 us
    ppermute x10, waiting for transfers between devices, step(): lax.ppermute(block, axis, [((i - distance) % size, i) for i in range(size)])  3.59 us
  transfers between devices with their start and end apart: 12, of which 3 were waited for; matrix products, arithmetic and copies ran while one was open for 0% of the time, Pallas kernels for 11%

profile of v4, /device:TPU:1, one launch (start us, length us, event | category | flops | bytes accessed | tf_op | source)
XLA Modules:
  0.0 81.6 jit_solution(295225204329261130)
XLA Ops:
  0.0 2.2 %shard_map.47 = bf16[64,9,2,128]{3,2,1,0:T(2,128)(2,1)} custom-call(s32[64]{0:T(128)} %counts_in.1, s32[128]{0:T(128)} %tiles_in.1, s32[16,128]{1,0:T(8,128)} %bitcast.25, bf16[128,16,128]{2,1,0:T(8,128)(2,1)} %values_in.1), custom_call_target="tpu_custom_call" | custom-call | tf_op jit(solution)/shard_map/pallas_call | solution.py:223
  2.3 13.5 %all-to-all-start = ((bf16[64,9,2,128]{3,2,1,0:T(2,128)(2,1)}), bf16[64,9,2,128]{3,2,1,0:T(2,128)(2,1)S(1)}, u32[]{:S(2)}, u32[]{:S(2)}) async-start(bf16[64,9,2,128]{3,2,1,0:T(2,128)(2,1)} %shard_map.47), calls=%async_computation | async-start | bytes 589824 | tf_op jit(solution)/shard_map/all_to_all | solution.py:246
  15.8 1.4 %shard_map.46.source = s32[16]{0:T(128)S(1)} custom-call(s32[64]{0:T(128)S(1)} %copy-done), custom_call_target="tpu_custom_call" | custom-call | flops 1073741824 | bytes 1048576 | tf_op jit(solution)/shard_map/pallas_call | solution.py:238
  17.1 10.5 %all-to-all-done.arrived = bf16[64,9,2,128]{3,2,1,0:T(2,128)(2,1)S(1)} async-done(((bf16[64,9,2,128]{3,2,1,0:T(2,128)(2,1)}), bf16[64,9,2,128]{3,2,1,0:T(2,128)(2,1)S(1)}, u32[]{:S(2)}, u32[]{:S(2)}) %all-to-all-start) | async-done | bytes 294944 | tf_op jit(solution)/shard_map/all_to_all | solution.py:246
  27.6 1.7 %shard_map.48 = (bf16[17,16,128]{2,1,0:T(8,128)(2,1)S(1)}, bf16[16,17,16,128]{3,2,1,0:T(8,128)(2,1)}) custom-call(s32[16]{0:T(128)S(1)} %shard_map.46.source, bf16[64,9,2,128]{3,2,1,0:T(2,128)(2,1)S(1)} %all-to-all-done.arrived), custom_call_target="tpu_custom_call" | custom-call | tf_op jit(solution)/shard_map/pallas_call | solution.py:247
  29.3 0.0 collective-permute-start
  29.3 6.4 %all-to-all-start.1 = ((bf16[16,17,16,128]{3,2,1,0:T(8,128)(2,1)}), bf16[16,17,16,128]{3,2,1,0:T(8,128)(2,1)S(1)}, u32[]{:S(2)}, u32[]{:S(2)}) async-start(bf16[16,17,16,128]{3,2,1,0:T(8,128)(2,1)} %get-tuple-element.12), calls=%async_computation.1 | async-start | bytes 2228224 | tf_op jit(solution)/shard_map/all_to_all | solution.py:258
  35.7 0.0 collective-permute-done
  35.7 0.1 collective-permute-start.1
  35.8 2.6 %collective-permute-start.3 = (bf16[17,16,128]{2,1,0:T(8,128)(2,1)S(1)}, bf16[17,16,128]{2,1,0:T(8,128)(2,1)S(1)}, u32[]{:S(2)}, u32[]{:S(2)}) collective-permute-start(bf16[17,16,128]{2,1,0:T(8,128)(2,1)S(1)} %get-tuple-element.15), channel_id=1, source_target_pairs={{32,0},{64,32},{96,64},{128,96},{160,128},{192,160},{224,192},{0,2... | collective-permute-start | bytes 208904 | tf_op jit(solution)/shard_map/ppermute | solution.py:218
  38.5 1.7 %collective-permute-done.1 = bf16[17,16,128]{2,1,0:T(8,128)(2,1)S(1)} collective-permute-done((bf16[17,16,128]{2,1,0:T(8,128)(2,1)S(1)}, bf16[17,16,128]{2,1,0:T(8,128)(2,1)S(1)}, u32[]{:S(2)}, u32[]{:S(2)}) %collective-permute-start.1) | collective-permute-done | bytes 69664 | tf_op jit(solution)/shard_map/ppermute | solution.py:218
  40.2 0.0 collective-permute-done.3
  40.2 2.7 %collective-permute-start.4 = (bf16[17,16,128]{2,1,0:T(8,128)(2,1)S(1)}, bf16[17,16,128]{2,1,0:T(8,128)(2,1)S(1)}, u32[]{:S(2)}, u32[]{:S(2)}) collective-permute-start(bf16[17,16,128]{2,1,0:T(8,128)(2,1)S(1)} %collective-permute-done.3), channel_id=1, source_target_pairs={{32,0},{64,32},{96,64},{128,96},{160,128},{192,160},{224,192},{0,2... | collective-permute-start | bytes 208904 | tf_op jit(solution)/shard_map/ppermute | solution.py:218
  42.9 1.9 %collective-permute-done.2 = bf16[17,16,128]{2,1,0:T(8,128)(2,1)S(1)} collective-permute-done((bf16[17,16,128]{2,1,0:T(8,128)(2,1)S(1)}, bf16[17,16,128]{2,1,0:T(8,128)(2,1)S(1)}, u32[]{:S(2)}, u32[]{:S(2)}) %collective-permute-start.2) | collective-permute-done | bytes 69664 | tf_op jit(solution)/shard_map/ppermute | solution.py:218
  44.9 5.2 %collective-permute-start.5 = (bf16[6,17,16,128]{3,2,1,0:T(8,128)(2,1)S(1)}, bf16[6,17,16,128]{3,2,1,0:T(8,128)(2,1)S(1)}, u32[]{:S(2)}, u32[]{:S(2)}) collective-permute-start(bf16[6,17,16,128]{3,2,1,0:T(8,128)(2,1)S(1)} %bitcast_dynamic-update-slice_fusion.own), channel_id=1, source_target_pairs={{1,0},{0,1},{3,2},{2,3},{5,4},{4,5},{7,6},{6,7},{9,8},{8,9},{11,10... | collective-permute-start | bytes 1253384 | tf_op jit(solution)/shard_map/ppermute | solution.py:218
  50.1 3.1 %collective-permute-start.7 = (bf16[17,16,128]{2,1,0:T(8,128)(2,1)S(1)}, bf16[17,16,128]{2,1,0:T(8,128)(2,1)S(1)}, u32[]{:S(2)}, u32[]{:S(2)}) collective-permute-start(bf16[17,16,128]{2,1,0:T(8,128)(2,1)S(1)} %collective-permute-done.4), channel_id=1, source_target_pairs={{32,0},{64,32},{96,64},{128,96},{160,128},{192,160},{224,192},{0,2... | collective-permute-start | bytes 208904 | tf_op jit(solution)/shard_map/ppermute | solution.py:218
  53.2 3.5 %shard_map.49.early_ratio = f32[6,16,256]{2,1,0:T(8,128)S(1)} custom-call(bf16[16,17,16,128]{3,2,1,0:T(8,128)(2,1)S(1)} %all-to-all-done.1.rows, bf16[6,17,16,128]{3,2,1,0:T(8,128)(2,1)S(1)} %bitcast_dynamic-update-slice_fusion.own), custom_call_target="tpu_custom_call" | custom-call | flops 1610612736 | bytes 2097152 | tf_op jit(solution)/shard_map/pallas_call | solution.py:267
  56.8 1.7 %collective-permute-start.8 = (bf16[2,17,16,128]{3,2,1,0:T(8,128)(2,1)S(1)}, bf16[2,17,16,128]{3,2,1,0:T(8,128)(2,1)S(1)}, u32[]{:S(2)}, u32[]{:S(2)}) collective-permute-start(bf16[2,17,16,128]{3,2,1,0:T(8,128)(2,1)S(1)} %pad_maximum_fusion.own), channel_id=1, source_target_pairs={{1,0},{0,1},{3,2},{2,3},{5,4},{4,5},{7,6},{6,7},{9,8},{8,9},{11,10... | collective-permute-start | bytes 417800 | tf_op jit(solution)/shard_map/ppermute | solution.py:218
  58.4 1.3 %shard_map.50.late_ratio = f32[2,16,256]{2,1,0:T(8,128)S(1)} custom-call(bf16[16,17,16,128]{3,2,1,0:T(8,128)(2,1)S(1)} %all-to-all-done.1.rows, bf16[2,17,16,128]{3,2,1,0:T(8,128)(2,1)S(1)} %pad_maximum_fusion.own), custom_call_target="tpu_custom_call" | custom-call | flops 536870912 | bytes 2097152 | tf_op jit(solution)/shard_map/pallas_call | solution.py:267
  59.7 3.2 %shard_map.52 = f32[4,2,32,128]{3,2,1,0:T(8,128)S(1)} custom-call(bf16[16,17,16,128]{3,2,1,0:T(8,128)(2,1)S(1)} %all-to-all-done.1.rows, bf16[6,17,16,128]{3,2,1,0:T(8,128)(2,1)S(1)} %collective-permute-done.5.early, bf16[2,17,16,128]{3,2,1,0:T(8,128)(2,1)S(1)} %collective-permute-done.8.late, f32[6,16,256]{2,1,0:T(8,128)S(1)} %shard_map.49.early_ratio, ...), custom_call_target="tpu_custom_call" | custom-call | flops 1073741824 | bytes 2097152 | tf_op jit(solution)/shard_map/pallas_call | solution.py:286
  63.0 0.1 collective-permute-start.9
  63.1 3.2 %shard_map.51 = f32[4,2,32,128]{3,2,1,0:T(8,128)S(1)} custom-call(bf16[16,17,16,128]{3,2,1,0:T(8,128)(2,1)S(1)} %all-to-all-done.1.rows, bf16[6,17,16,128]{3,2,1,0:T(8,128)(2,1)S(1)} %collective-permute-done.5.early, bf16[2,17,16,128]{3,2,1,0:T(8,128)(2,1)S(1)} %collective-permute-done.8.late, f32[6,16,256]{2,1,0:T(8,128)S(1)} %shard_map.49.early_ratio, ...), custom_call_target="tpu_custom_call" | custom-call | flops 1073741824 | bytes 2097152 | tf_op jit(solution)/shard_map/pallas_call | solution.py:286
  66.3 13.9 %all_to_all.15 = f32[16,32,128]{2,1,0:T(8,128)S(1)} all-to-all(f32[16,32,128]{2,1,0:T(8,128)S(1)} %bitcast.21), channel_id=1, replica_groups=mesh['z'=8,'yl'=2,'x'=4,'yh'=2,'c'=2] {'yl','x','yh'}, dimensions={0} | all-to-all | bytes 524288 | tf_op jit(solution)/shard_map/all_to_all | solution.py:306
  80.3 1.3 %shard_map.53 = f32[64,1024]{1,0:T(8,128)} custom-call(f32[2,4,2,32,128]{4,3,2,1,0:T(8,128)S(1)} %bitcast.19), custom_call_target="tpu_custom_call" | custom-call | tf_op jit(solution)/shard_map/pallas_call | solution.py:309
  (19 shorter events, 0.1 us)
Async XLA Ops:
  0.0 15.8 %copy-start = (s32[64]{0:T(128)S(1)}, s32[64]{0:T(128)}, u32[]{:S(2)}) copy-start(s32[64]{0:T(128)} %counts_in.1) | copy-start | bytes 772
  2.3 25.3 %all-to-all-start = ((bf16[64,9,2,128]{3,2,1,0:T(2,128)(2,1)}), bf16[64,9,2,128]{3,2,1,0:T(2,128)(2,1)S(1)}, u32[]{:S(2)}, u32[]{:S(2)}) async-start(bf16[64,9,2,128]{3,2,1,0:T(2,128)(2,1)} %shard_map.47), calls=%async_computation | async-start | bytes 589824 | tf_op jit(solution)/shard_map/all_to_all | solution.py:246
  29.3 6.4 %collective-permute-start = (bf16[17,16,128]{2,1,0:T(8,128)(2,1)S(1)}, bf16[17,16,128]{2,1,0:T(8,128)(2,1)S(1)}, u32[]{:S(2)}, u32[]{:S(2)}) collective-permute-start(bf16[17,16,128]{2,1,0:T(8,128)(2,1)S(1)} %get-tuple-element.15), channel_id=1, source_target_pairs={{224,0},{0,32},{32,64},{64,96},{96,128},{128,160},{160,192},{192,2... | collective-permute-start | bytes 208904 | tf_op jit(solution)/shard_map/ppermute | solution.py:218
  29.3 23.9 %all-to-all-start.1 = ((bf16[16,17,16,128]{3,2,1,0:T(8,128)(2,1)}), bf16[16,17,16,128]{3,2,1,0:T(8,128)(2,1)S(1)}, u32[]{:S(2)}, u32[]{:S(2)}) async-start(bf16[16,17,16,128]{3,2,1,0:T(8,128)(2,1)} %get-tuple-element.12), calls=%async_computation.1 | async-start | bytes 2228224 | tf_op jit(solution)/shard_map/all_to_all | solution.py:258
  35.7 4.4 %collective-permute-start.1 = (bf16[17,16,128]{2,1,0:T(8,128)(2,1)S(1)}, bf16[17,16,128]{2,1,0:T(8,128)(2,1)S(1)}, u32[]{:S(2)}, u32[]{:S(2)}) collective-permute-start(bf16[17,16,128]{2,1,0:T(8,128)(2,1)S(1)} %collective-permute-done), channel_id=1, source_target_pairs={{224,0},{0,32},{32,64},{64,96},{96,128},{128,160},{160,192},{192,2... | collective-permute-start | bytes 208904 | tf_op jit(solution)/shard_map/ppermute | solution.py:218
  35.8 4.3 %collective-permute-start.3 = (bf16[17,16,128]{2,1,0:T(8,128)(2,1)S(1)}, bf16[17,16,128]{2,1,0:T(8,128)(2,1)S(1)}, u32[]{:S(2)}, u32[]{:S(2)}) collective-permute-start(bf16[17,16,128]{2,1,0:T(8,128)(2,1)S(1)} %get-tuple-element.15), channel_id=1, source_target_pairs={{32,0},{64,32},{96,64},{128,96},{160,128},{192,160},{224,192},{0,2... | collective-permute-start | bytes 208904 | tf_op jit(solution)/shard_map/ppermute | solution.py:218
  40.1 4.7 %collective-permute-start.2 = (bf16[17,16,128]{2,1,0:T(8,128)(2,1)S(1)}, bf16[17,16,128]{2,1,0:T(8,128)(2,1)S(1)}, u32[]{:S(2)}, u32[]{:S(2)}) collective-permute-start(bf16[17,16,128]{2,1,0:T(8,128)(2,1)S(1)} %collective-permute-done.1), channel_id=1, source_target_pairs={{224,0},{0,32},{32,64},{64,96},{96,128},{128,160},{160,192},{192,2... | collective-permute-start | bytes 208904 | tf_op jit(solution)/shard_map/ppermute | solution.py:218
  40.2 4.7 %collective-permute-start.4 = (bf16[17,16,128]{2,1,0:T(8,128)(2,1)S(1)}, bf16[17,16,128]{2,1,0:T(8,128)(2,1)S(1)}, u32[]{:S(2)}, u32[]{:S(2)}) collective-permute-start(bf16[17,16,128]{2,1,0:T(8,128)(2,1)S(1)} %collective-permute-done.3), channel_id=1, source_target_pairs={{32,0},{64,32},{96,64},{128,96},{160,128},{192,160},{224,192},{0,2... | collective-permute-start | bytes 208904 | tf_op jit(solution)/shard_map/ppermute | solution.py:218
  44.9 14.9 %collective-permute-start.5 = (bf16[6,17,16,128]{3,2,1,0:T(8,128)(2,1)S(1)}, bf16[6,17,16,128]{3,2,1,0:T(8,128)(2,1)S(1)}, u32[]{:S(2)}, u32[]{:S(2)}) collective-permute-start(bf16[6,17,16,128]{3,2,1,0:T(8,128)(2,1)S(1)} %bitcast_dynamic-update-slice_fusion.own), channel_id=1, source_target_pairs={{1,0},{0,1},{3,2},{2,3},{5,4},{4,5},{7,6},{6,7},{9,8},{8,9},{11,10... | collective-permute-start | bytes 1253384 | tf_op jit(solution)/shard_map/ppermute | solution.py:218
  50.1 6.6 %collective-permute-start.6 = (bf16[17,16,128]{2,1,0:T(8,128)(2,1)S(1)}, bf16[17,16,128]{2,1,0:T(8,128)(2,1)S(1)}, u32[]{:S(2)}, u32[]{:S(2)}) collective-permute-start(bf16[17,16,128]{2,1,0:T(8,128)(2,1)S(1)} %collective-permute-done.2), channel_id=1, source_target_pairs={{224,0},{0,32},{32,64},{64,96},{96,128},{128,160},{160,192},{192,2... | collective-permute-start | bytes 208904 | tf_op jit(solution)/shard_map/ppermute | solution.py:218
  50.1 6.7 %collective-permute-start.7 = (bf16[17,16,128]{2,1,0:T(8,128)(2,1)S(1)}, bf16[17,16,128]{2,1,0:T(8,128)(2,1)S(1)}, u32[]{:S(2)}, u32[]{:S(2)}) collective-permute-start(bf16[17,16,128]{2,1,0:T(8,128)(2,1)S(1)} %collective-permute-done.4), channel_id=1, source_target_pairs={{32,0},{64,32},{96,64},{128,96},{160,128},{192,160},{224,192},{0,2... | collective-permute-start | bytes 208904 | tf_op jit(solution)/shard_map/ppermute | solution.py:218
  56.8 3.0 %collective-permute-start.8 = (bf16[2,17,16,128]{3,2,1,0:T(8,128)(2,1)S(1)}, bf16[2,17,16,128]{3,2,1,0:T(8,128)(2,1)S(1)}, u32[]{:S(2)}, u32[]{:S(2)}) collective-permute-start(bf16[2,17,16,128]{3,2,1,0:T(8,128)(2,1)S(1)} %pad_maximum_fusion.own), channel_id=1, source_target_pairs={{1,0},{0,1},{3,2},{2,3},{5,4},{4,5},{7,6},{6,7},{9,8},{8,9},{11,10... | collective-permute-start | bytes 417800 | tf_op jit(solution)/shard_map/ppermute | solution.py:218
  63.0 3.3 %collective-permute-start.9 = (f32[4,2,32,128]{3,2,1,0:T(8,128)S(1)}, f32[4,2,32,128]{3,2,1,0:T(8,128)S(1)}, u32[]{:S(2)}, u32[]{:S(2)}) collective-permute-start(f32[4,2,32,128]{3,2,1,0:T(8,128)S(1)} %shard_map.52), channel_id=1, source_target_pairs={{1,0},{0,1},{3,2},{2,3},{5,4},{4,5},{7,6},{6,7},{9,8},{8,9},{11,10... | collective-permute-start | bytes 393224 | tf_op jit(solution)/shard_map/ppermute | solution.py:218

commit v5 on v4

--- a/solution.py
+++ b/solution.py
@@ -39,7 +39,7 @@
 
         @pl.when(number < end)
         def _():
-            source[number >> 8] = e
+            source[number >> 8] = (e & 3) * 16 + (e >> 3) * 2 + ((e >> 2) & 1)
 
         return end
 
@@ -69,7 +69,7 @@
     tile_line = lax.broadcasted_iota(jnp.int32, (TILES, LANES), 0)
 
     def fill(t, carry):
-        wanted = (yh * 2 + ((t >> 2) & 1)) * 64 + (t >> 3) * 8 + c * 4 + (t & 3)
+        wanted = (yh * 2 + (t & 1)) * 64 + ((t >> 1) & 7) * 8 + c * 4 + (t >> 4)
         slot = jnp.minimum((wanted - own_begin) & 255, 127)
         document = jnp.where(tile_line < tiles[slot], values[slot].astype(F32), 0.0)
         codes = jnp.broadcast_to(wide_ids[pl.ds(slot, 1), :], (SENT - TILES, LANES))
@@ -243,7 +243,7 @@
         compiler_params=params(4),
         cost_estimate=pl.CostEstimate(flops=2**30, bytes_accessed=2**20, transcendentals=0),
     )(row_counts)
-    arrived = lax.all_to_all(sending, ("z", "yl", "x"), 0, 0, tiled=True)
+    arrived = lax.all_to_all(sending, ("x", "z", "yl"), 0, 0, tiled=True)
     piece, spread = pl.pallas_call(
         arrange_kernel,
         out_shape=(

time: 81.9 us -> 81.1 us (level)
  starting transfers between devices: 35.5 us -> 36.5 us
  waiting for transfers between devices: 14 us -> 13 us
    all_to_all x1, waiting for transfers between devices: 10.5 us -> 9.44 us  [on_device(): arrived = lax.all_to_all(sending, ('x', 'z', 'yl'), 0, 0, tiled=True)]
    all_to_all x1, blocking collectives: 13.9 us -> 13.1 us  [on_device(): lax.all_to_all(results.reshape(16, 32, LANES), ('yl', 'x', 'yh'), 0, 0, t...]
    ppermute x10, starting transfers between devices: 15.6 us -> 16.4 us  [step(): lax.ppermute(block, axis, [((i - distance) % size, i) for i in range(size)])]
  transfers between devices with their start and end apart: 12 -> 12, of which waited for: 3 -> 3; matrix products, arithmetic and copies ran while one was open for 0% -> 0% of each run, Pallas kernels for 11% -> 12%
where the time goes in v5:
time: 81.1 us; the launch traced here: 80.9 us
  starting transfers between devices  36.5 us (45%)
  Pallas kernels  18 us (22%)
  blocking collectives  13.1 us (16%)
  waiting for transfers between devices  13 us (16%)
    ppermute x10, starting transfers between devices, step(): lax.ppermute(block, axis, [((i - distance) % size, i) for i in range(size)])  16.4 us
    all_to_all x1, starting transfers between devices, on_device(): arrived = lax.all_to_all(sending, ('x', 'z', 'yl'), 0, 0, tiled=True)  13.5 us
    all_to_all x1, blocking collectives, on_device(): lax.all_to_all(results.reshape(16, 32, LANES), ('yl', 'x', 'yh'), 0, 0, t...  13.1 us
    all_to_all x1, waiting for transfers between devices, on_device(): arrived = lax.all_to_all(sending, ('x', 'z', 'yl'), 0, 0, tiled=True)  9.44 us
    all_to_all x1, starting transfers between devices, on_device(): rows = lax.all_to_all(spread, ('x', 'yh', 'yl'), 0, 0, tiled=True)  6.53 us
    pallas_call x2, Pallas kernels, finish(): pl.pallas_call(functools.partial(other_kernel, kept), out_shape=jax.Shape...  6.43 us
    pallas_call x2, Pallas kernels, compare_own(): pl.pallas_call(own_kernel, out_shape=jax.ShapeDtypeStruct((count, 16, 256...  4.79 us
    ppermute x10, waiting for transfers between devices, step(): lax.ppermute(block, axis, [((i - distance) % size, i) for i in range(size)])  3.59 us
  transfers between devices with their start and end apart: 12, of which 3 were waited for; matrix products, arithmetic and copies ran while one was open for 0% of the time, Pallas kernels for 12%

profile of v5, /device:TPU:1, one launch (start us, length us, event | category | flops | bytes accessed | tf_op | source)
XLA Modules:
  0.0 80.9 jit_solution(11010270795011706666)
XLA Ops:
  0.0 2.2 %shard_map.47 = bf16[64,9,2,128]{3,2,1,0:T(2,128)(2,1)} custom-call(s32[64]{0:T(128)} %counts_in.1, s32[128]{0:T(128)} %tiles_in.1, s32[16,128]{1,0:T(8,128)} %bitcast.25, bf16[128,16,128]{2,1,0:T(8,128)(2,1)} %values_in.1), custom_call_target="tpu_custom_call" | custom-call | tf_op jit(solution)/shard_map/pallas_call | solution.py:223
  2.3 13.5 %all-to-all-start = ((bf16[64,9,2,128]{3,2,1,0:T(2,128)(2,1)}), bf16[64,9,2,128]{3,2,1,0:T(2,128)(2,1)S(1)}, u32[]{:S(2)}, u32[]{:S(2)}) async-start(bf16[64,9,2,128]{3,2,1,0:T(2,128)(2,1)} %shard_map.47), calls=%async_computation | async-start | bytes 589824 | tf_op jit(solution)/shard_map/all_to_all | solution.py:246
  15.8 1.5 %shard_map.46.source = s32[16]{0:T(128)S(1)} custom-call(s32[64]{0:T(128)S(1)} %copy-done), custom_call_target="tpu_custom_call" | custom-call | flops 1073741824 | bytes 1048576 | tf_op jit(solution)/shard_map/pallas_call | solution.py:238
  17.3 9.4 %all-to-all-done.arrived = bf16[64,9,2,128]{3,2,1,0:T(2,128)(2,1)S(1)} async-done(((bf16[64,9,2,128]{3,2,1,0:T(2,128)(2,1)}), bf16[64,9,2,128]{3,2,1,0:T(2,128)(2,1)S(1)}, u32[]{:S(2)}, u32[]{:S(2)}) %all-to-all-start) | async-done | bytes 294944 | tf_op jit(solution)/shard_map/all_to_all | solution.py:246
  26.7 1.7 %shard_map.48 = (bf16[17,16,128]{2,1,0:T(8,128)(2,1)S(1)}, bf16[16,17,16,128]{3,2,1,0:T(8,128)(2,1)}) custom-call(s32[16]{0:T(128)S(1)} %shard_map.46.source, bf16[64,9,2,128]{3,2,1,0:T(2,128)(2,1)S(1)} %all-to-all-done.arrived), custom_call_target="tpu_custom_call" | custom-call | tf_op jit(solution)/shard_map/pallas_call | solution.py:247
  28.4 0.9 %collective-permute-start = (bf16[17,16,128]{2,1,0:T(8,128)(2,1)S(1)}, bf16[17,16,128]{2,1,0:T(8,128)(2,1)S(1)}, u32[]{:S(2)}, u32[]{:S(2)}) collective-permute-start(bf16[17,16,128]{2,1,0:T(8,128)(2,1)S(1)} %get-tuple-element.15), channel_id=1, source_target_pairs={{224,0},{0,32},{32,64},{64,96},{96,128},{128,160},{160,192},{192,2... | collective-permute-start | bytes 208904 | tf_op jit(solution)/shard_map/ppermute | solution.py:218
  29.4 6.5 %all-to-all-start.1 = ((bf16[16,17,16,128]{3,2,1,0:T(8,128)(2,1)}), bf16[16,17,16,128]{3,2,1,0:T(8,128)(2,1)S(1)}, u32[]{:S(2)}, u32[]{:S(2)}) async-start(bf16[16,17,16,128]{3,2,1,0:T(8,128)(2,1)} %get-tuple-element.12), calls=%async_computation.1 | async-start | bytes 2228224 | tf_op jit(solution)/shard_map/all_to_all | solution.py:258
  35.9 0.0 collective-permute-done
  35.9 0.6 collective-permute-start.1
  36.5 2.2 %collective-permute-start.3 = (bf16[17,16,128]{2,1,0:T(8,128)(2,1)S(1)}, bf16[17,16,128]{2,1,0:T(8,128)(2,1)S(1)}, u32[]{:S(2)}, u32[]{:S(2)}) collective-permute-start(bf16[17,16,128]{2,1,0:T(8,128)(2,1)S(1)} %get-tuple-element.15), channel_id=1, source_target_pairs={{32,0},{64,32},{96,64},{128,96},{160,128},{192,160},{224,192},{0,2... | collective-permute-start | bytes 208904 | tf_op jit(solution)/shard_map/ppermute | solution.py:218
  38.7 1.7 %collective-permute-done.1 = bf16[17,16,128]{2,1,0:T(8,128)(2,1)S(1)} collective-permute-done((bf16[17,16,128]{2,1,0:T(8,128)(2,1)S(1)}, bf16[17,16,128]{2,1,0:T(8,128)(2,1)S(1)}, u32[]{:S(2)}, u32[]{:S(2)}) %collective-permute-start.1) | collective-permute-done | bytes 69664 | tf_op jit(solution)/shard_map/ppermute | solution.py:218
  40.4 0.0 collective-permute-start.2
  40.4 2.7 %collective-permute-start.4 = (bf16[17,16,128]{2,1,0:T(8,128)(2,1)S(1)}, bf16[17,16,128]{2,1,0:T(8,128)(2,1)S(1)}, u32[]{:S(2)}, u32[]{:S(2)}) collective-permute-start(bf16[17,16,128]{2,1,0:T(8,128)(2,1)S(1)} %collective-permute-done.3), channel_id=1, source_target_pairs={{32,0},{64,32},{96,64},{128,96},{160,128},{192,160},{224,192},{0,2... | collective-permute-start | bytes 208904 | tf_op jit(solution)/shard_map/ppermute | solution.py:218
  43.1 1.9 %collective-permute-done.2 = bf16[17,16,128]{2,1,0:T(8,128)(2,1)S(1)} collective-permute-done((bf16[17,16,128]{2,1,0:T(8,128)(2,1)S(1)}, bf16[17,16,128]{2,1,0:T(8,128)(2,1)S(1)}, u32[]{:S(2)}, u32[]{:S(2)}) %collective-permute-start.2) | collective-permute-done | bytes 69664 | tf_op jit(solution)/shard_map/ppermute | solution.py:218
  45.1 4.6 %collective-permute-start.5 = (bf16[6,17,16,128]{3,2,1,0:T(8,128)(2,1)S(1)}, bf16[6,17,16,128]{3,2,1,0:T(8,128)(2,1)S(1)}, u32[]{:S(2)}, u32[]{:S(2)}) collective-permute-start(bf16[6,17,16,128]{3,2,1,0:T(8,128)(2,1)S(1)} %bitcast_dynamic-update-slice_fusion.own), channel_id=1, source_target_pairs={{1,0},{0,1},{3,2},{2,3},{5,4},{4,5},{7,6},{6,7},{9,8},{8,9},{11,10... | collective-permute-start | bytes 1253384 | tf_op jit(solution)/shard_map/ppermute | solution.py:218
  49.7 3.0 %collective-permute-start.7 = (bf16[17,16,128]{2,1,0:T(8,128)(2,1)S(1)}, bf16[17,16,128]{2,1,0:T(8,128)(2,1)S(1)}, u32[]{:S(2)}, u32[]{:S(2)}) collective-permute-start(bf16[17,16,128]{2,1,0:T(8,128)(2,1)S(1)} %collective-permute-done.4), channel_id=1, source_target_pairs={{32,0},{64,32},{96,64},{128,96},{160,128},{192,160},{224,192},{0,2... | collective-permute-start | bytes 208904 | tf_op jit(solution)/shard_map/ppermute | solution.py:218
  52.7 3.5 %shard_map.49.early_ratio = f32[6,16,256]{2,1,0:T(8,128)S(1)} custom-call(bf16[16,17,16,128]{3,2,1,0:T(8,128)(2,1)S(1)} %all-to-all-done.1.rows, bf16[6,17,16,128]{3,2,1,0:T(8,128)(2,1)S(1)} %bitcast_dynamic-update-slice_fusion.own), custom_call_target="tpu_custom_call" | custom-call | flops 1610612736 | bytes 2097152 | tf_op jit(solution)/shard_map/pallas_call | solution.py:267
  56.3 2.3 %collective-permute-start.8 = (bf16[2,17,16,128]{3,2,1,0:T(8,128)(2,1)S(1)}, bf16[2,17,16,128]{3,2,1,0:T(8,128)(2,1)S(1)}, u32[]{:S(2)}, u32[]{:S(2)}) collective-permute-start(bf16[2,17,16,128]{3,2,1,0:T(8,128)(2,1)S(1)} %pad_maximum_fusion.own), channel_id=1, source_target_pairs={{1,0},{0,1},{3,2},{2,3},{5,4},{4,5},{7,6},{6,7},{9,8},{8,9},{11,10... | collective-permute-start | bytes 417800 | tf_op jit(solution)/shard_map/ppermute | solution.py:218
  58.5 1.3 %shard_map.50.late_ratio = f32[2,16,256]{2,1,0:T(8,128)S(1)} custom-call(bf16[16,17,16,128]{3,2,1,0:T(8,128)(2,1)S(1)} %all-to-all-done.1.rows, bf16[2,17,16,128]{3,2,1,0:T(8,128)(2,1)S(1)} %pad_maximum_fusion.own), custom_call_target="tpu_custom_call" | custom-call | flops 536870912 | bytes 2097152 | tf_op jit(solution)/shard_map/pallas_call | solution.py:267
  59.8 3.2 %shard_map.52 = f32[4,2,32,128]{3,2,1,0:T(8,128)S(1)} custom-call(bf16[16,17,16,128]{3,2,1,0:T(8,128)(2,1)S(1)} %all-to-all-done.1.rows, bf16[6,17,16,128]{3,2,1,0:T(8,128)(2,1)S(1)} %collective-permute-done.5.early, bf16[2,17,16,128]{3,2,1,0:T(8,128)(2,1)S(1)} %collective-permute-done.8.late, f32[6,16,256]{2,1,0:T(8,128)S(1)} %shard_map.49.early_ratio, ...), custom_call_target="tpu_custom_call" | custom-call | flops 1073741824 | bytes 2097152 | tf_op jit(solution)/shard_map/pallas_call | solution.py:286
  63.1 0.1 collective-permute-start.9
  63.2 3.2 %shard_map.51 = f32[4,2,32,128]{3,2,1,0:T(8,128)S(1)} custom-call(bf16[16,17,16,128]{3,2,1,0:T(8,128)(2,1)S(1)} %all-to-all-done.1.rows, bf16[6,17,16,128]{3,2,1,0:T(8,128)(2,1)S(1)} %collective-permute-done.5.early, bf16[2,17,16,128]{3,2,1,0:T(8,128)(2,1)S(1)} %collective-permute-done.8.late, f32[6,16,256]{2,1,0:T(8,128)S(1)} %shard_map.49.early_ratio, ...), custom_call_target="tpu_custom_call" | custom-call | flops 1073741824 | bytes 2097152 | tf_op jit(solution)/shard_map/pallas_call | solution.py:286
  66.4 13.1 %all_to_all.15 = f32[16,32,128]{2,1,0:T(8,128)S(1)} all-to-all(f32[16,32,128]{2,1,0:T(8,128)S(1)} %bitcast.21), channel_id=1, replica_groups=mesh['z'=8,'yl'=2,'x'=4,'yh'=2,'c'=2] {'yl','x','yh'}, dimensions={0} | all-to-all | bytes 524288 | tf_op jit(solution)/shard_map/all_to_all | solution.py:306
  79.5 1.3 %shard_map.53 = f32[64,1024]{1,0:T(8,128)} custom-call(f32[2,4,2,32,128]{4,3,2,1,0:T(8,128)S(1)} %bitcast.19), custom_call_target="tpu_custom_call" | custom-call | tf_op jit(solution)/shard_map/pallas_call | solution.py:309
  (19 shorter events, 0.1 us)
Async XLA Ops:
  0.0 15.8 %copy-start = (s32[64]{0:T(128)S(1)}, s32[64]{0:T(128)}, u32[]{:S(2)}) copy-start(s32[64]{0:T(128)} %counts_in.1) | copy-start | bytes 772
  2.3 24.5 %all-to-all-start = ((bf16[64,9,2,128]{3,2,1,0:T(2,128)(2,1)}), bf16[64,9,2,128]{3,2,1,0:T(2,128)(2,1)S(1)}, u32[]{:S(2)}, u32[]{:S(2)}) async-start(bf16[64,9,2,128]{3,2,1,0:T(2,128)(2,1)} %shard_map.47), calls=%async_computation | async-start | bytes 589824 | tf_op jit(solution)/shard_map/all_to_all | solution.py:246
  28.4 7.5 %collective-permute-start = (bf16[17,16,128]{2,1,0:T(8,128)(2,1)S(1)}, bf16[17,16,128]{2,1,0:T(8,128)(2,1)S(1)}, u32[]{:S(2)}, u32[]{:S(2)}) collective-permute-start(bf16[17,16,128]{2,1,0:T(8,128)(2,1)S(1)} %get-tuple-element.15), channel_id=1, source_target_pairs={{224,0},{0,32},{32,64},{64,96},{96,128},{128,160},{160,192},{192,2... | collective-permute-start | bytes 208904 | tf_op jit(solution)/shard_map/ppermute | solution.py:218
  29.4 23.3 %all-to-all-start.1 = ((bf16[16,17,16,128]{3,2,1,0:T(8,128)(2,1)}), bf16[16,17,16,128]{3,2,1,0:T(8,128)(2,1)S(1)}, u32[]{:S(2)}, u32[]{:S(2)}) async-start(bf16[16,17,16,128]{3,2,1,0:T(8,128)(2,1)} %get-tuple-element.12), calls=%async_computation.1 | async-start | bytes 2228224 | tf_op jit(solution)/shard_map/all_to_all | solution.py:258
  35.9 4.4 %collective-permute-start.1 = (bf16[17,16,128]{2,1,0:T(8,128)(2,1)S(1)}, bf16[17,16,128]{2,1,0:T(8,128)(2,1)S(1)}, u32[]{:S(2)}, u32[]{:S(2)}) collective-permute-start(bf16[17,16,128]{2,1,0:T(8,128)(2,1)S(1)} %collective-permute-done), channel_id=1, source_target_pairs={{224,0},{0,32},{32,64},{64,96},{96,128},{128,160},{160,192},{192,2... | collective-permute-start | bytes 208904 | tf_op jit(solution)/shard_map/ppermute | solution.py:218
  36.5 3.9 %collective-permute-start.3 = (bf16[17,16,128]{2,1,0:T(8,128)(2,1)S(1)}, bf16[17,16,128]{2,1,0:T(8,128)(2,1)S(1)}, u32[]{:S(2)}, u32[]{:S(2)}) collective-permute-start(bf16[17,16,128]{2,1,0:T(8,128)(2,1)S(1)} %get-tuple-element.15), channel_id=1, source_target_pairs={{32,0},{64,32},{96,64},{128,96},{160,128},{192,160},{224,192},{0,2... | collective-permute-start | bytes 208904 | tf_op jit(solution)/shard_map/ppermute | solution.py:218
  40.4 4.7 %collective-permute-start.2 = (bf16[17,16,128]{2,1,0:T(8,128)(2,1)S(1)}, bf16[17,16,128]{2,1,0:T(8,128)(2,1)S(1)}, u32[]{:S(2)}, u32[]{:S(2)}) collective-permute-start(bf16[17,16,128]{2,1,0:T(8,128)(2,1)S(1)} %collective-permute-done.1), channel_id=1, source_target_pairs={{224,0},{0,32},{32,64},{64,96},{96,128},{128,160},{160,192},{192,2... | collective-permute-start | bytes 208904 | tf_op jit(solution)/shard_map/ppermute | solution.py:218
  40.4 4.7 %collective-permute-start.4 = (bf16[17,16,128]{2,1,0:T(8,128)(2,1)S(1)}, bf16[17,16,128]{2,1,0:T(8,128)(2,1)S(1)}, u32[]{:S(2)}, u32[]{:S(2)}) collective-permute-start(bf16[17,16,128]{2,1,0:T(8,128)(2,1)S(1)} %collective-permute-done.3), channel_id=1, source_target_pairs={{32,0},{64,32},{96,64},{128,96},{160,128},{192,160},{224,192},{0,2... | collective-permute-start | bytes 208904 | tf_op jit(solution)/shard_map/ppermute | solution.py:218
  45.1 14.7 %collective-permute-start.5 = (bf16[6,17,16,128]{3,2,1,0:T(8,128)(2,1)S(1)}, bf16[6,17,16,128]{3,2,1,0:T(8,128)(2,1)S(1)}, u32[]{:S(2)}, u32[]{:S(2)}) collective-permute-start(bf16[6,17,16,128]{3,2,1,0:T(8,128)(2,1)S(1)} %bitcast_dynamic-update-slice_fusion.own), channel_id=1, source_target_pairs={{1,0},{0,1},{3,2},{2,3},{5,4},{4,5},{7,6},{6,7},{9,8},{8,9},{11,10... | collective-permute-start | bytes 1253384 | tf_op jit(solution)/shard_map/ppermute | solution.py:218
  49.7 6.6 %collective-permute-start.6 = (bf16[17,16,128]{2,1,0:T(8,128)(2,1)S(1)}, bf16[17,16,128]{2,1,0:T(8,128)(2,1)S(1)}, u32[]{:S(2)}, u32[]{:S(2)}) collective-permute-start(bf16[17,16,128]{2,1,0:T(8,128)(2,1)S(1)} %collective-permute-done.2), channel_id=1, source_target_pairs={{224,0},{0,32},{32,64},{64,96},{96,128},{128,160},{160,192},{192,2... | collective-permute-start | bytes 208904 | tf_op jit(solution)/shard_map/ppermute | solution.py:218
  49.7 6.6 %collective-permute-start.7 = (bf16[17,16,128]{2,1,0:T(8,128)(2,1)S(1)}, bf16[17,16,128]{2,1,0:T(8,128)(2,1)S(1)}, u32[]{:S(2)}, u32[]{:S(2)}) collective-permute-start(bf16[17,16,128]{2,1,0:T(8,128)(2,1)S(1)} %collective-permute-done.4), channel_id=1, source_target_pairs={{32,0},{64,32},{96,64},{128,96},{160,128},{192,160},{224,192},{0,2... | collective-permute-start | bytes 208904 | tf_op jit(solution)/shard_map/ppermute | solution.py:218
  56.3 3.6 %collective-permute-start.8 = (bf16[2,17,16,128]{3,2,1,0:T(8,128)(2,1)S(1)}, bf16[2,17,16,128]{3,2,1,0:T(8,128)(2,1)S(1)}, u32[]{:S(2)}, u32[]{:S(2)}) collective-permute-start(bf16[2,17,16,128]{3,2,1,0:T(8,128)(2,1)S(1)} %pad_maximum_fusion.own), channel_id=1, source_target_pairs={{1,0},{0,1},{3,2},{2,3},{5,4},{4,5},{7,6},{6,7},{9,8},{8,9},{11,10... | collective-permute-start | bytes 417800 | tf_op jit(solution)/shard_map/ppermute | solution.py:218
  63.1 3.3 %collective-permute-start.9 = (f32[4,2,32,128]{3,2,1,0:T(8,128)S(1)}, f32[4,2,32,128]{3,2,1,0:T(8,128)S(1)}, u32[]{:S(2)}, u32[]{:S(2)}) collective-permute-start(f32[4,2,32,128]{3,2,1,0:T(8,128)S(1)} %shard_map.52), channel_id=1, source_target_pairs={{1,0},{0,1},{3,2},{2,3},{5,4},{4,5},{7,6},{6,7},{9,8},{8,9},{11,10... | collective-permute-start | bytes 393224 | tf_op jit(solution)/shard_map/ppermute | solution.py:218

commit v6 on v5

--- a/solution.py
+++ b/solution.py
@@ -106,11 +106,6 @@
 
 
 def compare(rows, pieces, chosen, row_codes, piece_codes, acc):
-    for j in range(16):
-        row_codes[j * 16 : j * 16 + 16, :] = rows[j, TILES].astype(F32)
-    across = jnp.transpose(row_codes[...], (1, 0))
-    row_codes[0:128, :] = across[:, 0:128]
-    row_codes[128:256, :] = across[:, 128:256]
     piece_norms = []
     for d, place in enumerate(chosen):
         codes = pieces[place, TILES].astype(F32)
@@ -131,17 +126,27 @@
             same = jnp.concatenate([codes_d, codes_d], axis=1) == codes_k
             product = jnp.where(same, product, 0.0).reshape(TILES, 16, 256)
             acc[d] += jnp.sum(product, axis=0)
-    norms_across = across[16:17] + across[17:18] + across[18:19]
+    across = jnp.concatenate([row_codes[16:24, :], row_codes[144:152, :]], axis=1)
+    norms_across = across[0:1] + across[1:2] + across[2:3]
     for d in range(len(chosen)):
         acc[d] = acc[d] / (piece_norms[d] + norms_across - acc[d])
 
 
-def own_kernel(rows, own, out, row_codes, piece_codes):
+def early_kernel(rows, own, out, row_codes, piece_codes):
+    for j in range(16):
+        row_codes[j * 16 : j * 16 + 16, :] = rows[j, TILES].astype(F32)
+    across = jnp.transpose(row_codes[...], (1, 0))
+    row_codes[0:128, :] = across[:, 0:128]
+    row_codes[128:256, :] = across[:, 128:256]
     compare(rows, own, list(range(own.shape[0])), row_codes, piece_codes, out)
 
 
+def late_kernel(rows, own, row_codes, out, piece_codes):
+    compare(rows, own, list(range(own.shape[0])), row_codes, piece_codes, out)
+
+
 def other_kernel(
-    kept, rows, early, late, early_ratio, late_ratio, out, row_codes, piece_codes, acc, tall, picked, own_ratio
+    kept, rows, row_codes, early, late, early_ratio, late_ratio, out, piece_codes, acc, tall, picked, own_ratio
 ):
     x, c = lax.axis_index("x"), lax.axis_index("c")
     core = c if kept else 1 - c
@@ -187,7 +192,7 @@
         total = jnp.zeros((32, 512), F32)
         for yh in range(2):
             shift = (base + 2 * yh == give).astype(BF16)
-            block = jnp.concatenate([arrived[0, xs, yh], arrived[1, xs, yh]], axis=1)
+            block = jnp.concatenate([arrived[xs, yh, 0], arrived[xs, yh, 1]], axis=1)
             high = block.astype(BF16)
             rest = block - high.astype(F32)
             middle = rest.astype(BF16)
@@ -262,34 +267,40 @@
     for distance in range(1, 4):
         behind, ahead = step(behind, "z", 1), step(ahead, "z", -1)
         ring[distance + 1], ring[8 - distance] = behind, ahead
-    def compare_own(own):
-        count = own.shape[0]
-        return pl.pallas_call(
-            own_kernel,
-            out_shape=jax.ShapeDtypeStruct((count, 16, 256), F32),
-            in_specs=[VMEM, VMEM],
-            out_specs=VMEM,
-            scratch_shapes=[pltpu.VMEM((256, LANES), F32), pltpu.VMEM((count, TILES, 16, LANES), F32)],
-            compiler_params=params(32),
-            cost_estimate=cost(count),
-        )(rows, own)
-
     early = jnp.stack([ring[d] for d in EARLY])
     other_early = step(early, "c", 1)
-    early_ratio = compare_own(early)
+    early_ratio, row_codes = pl.pallas_call(
+        early_kernel,
+        out_shape=(
+            jax.ShapeDtypeStruct((len(EARLY), 16, 256), F32),
+            jax.ShapeDtypeStruct((256, LANES), F32),
+        ),
+        in_specs=[VMEM, VMEM],
+        out_specs=(VMEM, VMEM),
+        scratch_shapes=[pltpu.VMEM((len(EARLY), TILES, 16, LANES), F32)],
+        compiler_params=params(32),
+        cost_estimate=cost(len(EARLY)),
+    )(rows, early)
     early_ratio, *last = lax.optimization_barrier((early_ratio, *(ring[d] for d in LATE)))
     late = jnp.stack(last)
     other_late = step(late, "c", 1)
-    late_ratio = compare_own(late)
+    late_ratio = pl.pallas_call(
+        late_kernel,
+        out_shape=jax.ShapeDtypeStruct((len(LATE), 16, 256), F32),
+        in_specs=[VMEM, VMEM, VMEM],
+        out_specs=VMEM,
+        scratch_shapes=[pltpu.VMEM((len(LATE), TILES, 16, LANES), F32)],
+        compiler_params=params(32),
+        cost_estimate=cost(len(LATE)),
+    )(rows, late, row_codes)
 
     def finish(kept):
         return pl.pallas_call(
             functools.partial(other_kernel, kept),
             out_shape=jax.ShapeDtypeStruct((4, 2, 32, LANES), F32),
-            in_specs=[VMEM] * 5,
+            in_specs=[VMEM] * 6,
             out_specs=VMEM,
             scratch_shapes=[
-                pltpu.VMEM((256, LANES), F32),
                 pltpu.VMEM((4, TILES, 16, LANES), F32),
                 pltpu.VMEM((4, 16, 256), F32),
                 pltpu.VMEM((2, LANES, 256), F32),
@@ -298,14 +309,14 @@
             ],
             compiler_params=params(32),
             cost_estimate=cost(4),
-        )(rows, other_early, other_late, early_ratio, late_ratio)
+        )(rows, row_codes, other_early, other_late, early_ratio, late_ratio)
 
     swapped = step(finish(False), "c", 1)
     kept = finish(True)
-    results = jnp.where(c == 0, jnp.stack([kept, swapped]), jnp.stack([swapped, kept]))
+    results = jnp.where(c == 0, jnp.stack([kept, swapped], 2), jnp.stack([swapped, kept], 2))
     results = lax.all_to_all(
-        results.reshape(16, 32, LANES), ("yl", "x", "yh"), 0, 0, tiled=True
-    ).reshape(2, 4, 2, 32, LANES)
+        results.reshape(16, 32, LANES), ("x", "yh", "yl"), 0, 0, tiled=True
+    ).reshape(4, 2, 2, 32, LANES)
     return pl.pallas_call(
         place_kernel,
         out_shape=jax.ShapeDtypeStruct((64, 1024), F32),

time: 81.1 us -> 79.8 us (0.984)
  Pallas kernels: 18 us -> 17 us
    pallas_call x2, Pallas kernels: 6.43 us -> 5.46 us  [finish(): pl.pallas_call(functools.partial(other_kernel, kept), out_shape=jax.Shape...]
  transfers between devices with their start and end apart: 12 -> 12, of which waited for: 3 -> 3; matrix products, arithmetic and copies ran while one was open for 0% -> 0% of each run, Pallas kernels for 12% -> 11%
where the time goes in v6:
time: 79.8 us; the launch traced here: 79.5 us
  starting transfers between devices  36.5 us (46%)
  Pallas kernels  17 us (21%)
  waiting for transfers between devices  13 us (16%)
  blocking collectives  12.7 us (16%)
    ppermute x10, starting transfers between devices, step(): lax.ppermute(block, axis, [((i - distance) % size, i) for i in range(size)])  16.4 us
    all_to_all x1, starting transfers between devices, on_device(): arrived = lax.all_to_all(sending, ('x', 'z', 'yl'), 0, 0, tiled=True)  13.5 us
    all_to_all x1, blocking collectives, on_device(): lax.all_to_all(results.reshape(16, 32, LANES), ('x', 'yh', 'yl'), 0, 0, t...  12.7 us
    all_to_all x1, waiting for transfers between devices, on_device(): arrived = lax.all_to_all(sending, ('x', 'z', 'yl'), 0, 0, tiled=True)  9.44 us
    all_to_all x1, starting transfers between devices, on_device(): rows = lax.all_to_all(spread, ('x', 'yh', 'yl'), 0, 0, tiled=True)  6.53 us
    pallas_call x2, Pallas kernels, finish(): pl.pallas_call(functools.partial(other_kernel, kept), out_shape=jax.Shape...  5.46 us
    ppermute x10, waiting for transfers between devices, step(): lax.ppermute(block, axis, [((i - distance) % size, i) for i in range(size)])  3.59 us
    pallas_call x1, Pallas kernels, on_device(): pl.pallas_call(early_kernel, out_shape=(jax.ShapeDtypeStruct((len(EARLY),...  3.48 us
  transfers between devices with their start and end apart: 12, of which 3 were waited for; matrix products, arithmetic and copies ran while one was open for 0% of the time, Pallas kernels for 11%

profile of v6, /device:TPU:1, one launch (start us, length us, event | category | flops | bytes accessed | tf_op | source)
XLA Modules:
  0.0 79.5 jit_solution(9795669332962249672)
XLA Ops:
  0.0 2.3 %shard_map.47 = bf16[64,9,2,128]{3,2,1,0:T(2,128)(2,1)} custom-call(s32[64]{0:T(128)} %counts_in.1, s32[128]{0:T(128)} %tiles_in.1, s32[16,128]{1,0:T(8,128)} %bitcast.25, bf16[128,16,128]{2,1,0:T(8,128)(2,1)} %values_in.1), custom_call_target="tpu_custom_call" | custom-call | tf_op jit(solution)/shard_map/pallas_call | solution.py:228
  2.3 13.5 %all-to-all-start = ((bf16[64,9,2,128]{3,2,1,0:T(2,128)(2,1)}), bf16[64,9,2,128]{3,2,1,0:T(2,128)(2,1)S(1)}, u32[]{:S(2)}, u32[]{:S(2)}) async-start(bf16[64,9,2,128]{3,2,1,0:T(2,128)(2,1)} %shard_map.47), calls=%async_computation | async-start | bytes 589824 | tf_op jit(solution)/shard_map/all_to_all | solution.py:251
  15.8 1.5 %shard_map.46.source = s32[16]{0:T(128)S(1)} custom-call(s32[64]{0:T(128)S(1)} %copy-done), custom_call_target="tpu_custom_call" | custom-call | flops 1073741824 | bytes 1048576 | tf_op jit(solution)/shard_map/pallas_call | solution.py:243
  17.3 9.4 %all-to-all-done.arrived = bf16[64,9,2,128]{3,2,1,0:T(2,128)(2,1)S(1)} async-done(((bf16[64,9,2,128]{3,2,1,0:T(2,128)(2,1)}), bf16[64,9,2,128]{3,2,1,0:T(2,128)(2,1)S(1)}, u32[]{:S(2)}, u32[]{:S(2)}) %all-to-all-start) | async-done | bytes 294944 | tf_op jit(solution)/shard_map/all_to_all | solution.py:251
  26.7 1.7 %shard_map.48 = (bf16[17,16,128]{2,1,0:T(8,128)(2,1)S(1)}, bf16[16,17,16,128]{3,2,1,0:T(8,128)(2,1)}) custom-call(s32[16]{0:T(128)S(1)} %shard_map.46.source, bf16[64,9,2,128]{3,2,1,0:T(2,128)(2,1)S(1)} %all-to-all-done.arrived), custom_call_target="tpu_custom_call" | custom-call | tf_op jit(solution)/shard_map/pallas_call | solution.py:252
  28.4 0.9 %collective-permute-start = (bf16[17,16,128]{2,1,0:T(8,128)(2,1)S(1)}, bf16[17,16,128]{2,1,0:T(8,128)(2,1)S(1)}, u32[]{:S(2)}, u32[]{:S(2)}) collective-permute-start(bf16[17,16,128]{2,1,0:T(8,128)(2,1)S(1)} %get-tuple-element.17), channel_id=1, source_target_pairs={{224,0},{0,32},{32,64},{64,96},{96,128},{128,160},{160,192},{192,2... | collective-permute-start | bytes 208904 | tf_op jit(solution)/shard_map/ppermute | solution.py:223
  29.4 6.5 %all-to-all-start.1 = ((bf16[16,17,16,128]{3,2,1,0:T(8,128)(2,1)}), bf16[16,17,16,128]{3,2,1,0:T(8,128)(2,1)S(1)}, u32[]{:S(2)}, u32[]{:S(2)}) async-start(bf16[16,17,16,128]{3,2,1,0:T(8,128)(2,1)} %get-tuple-element.14), calls=%async_computation.1 | async-start | bytes 2228224 | tf_op jit(solution)/shard_map/all_to_all | solution.py:263
  35.9 0.0 collective-permute-done
  35.9 0.6 collective-permute-start.1
  36.5 2.2 %collective-permute-start.3 = (bf16[17,16,128]{2,1,0:T(8,128)(2,1)S(1)}, bf16[17,16,128]{2,1,0:T(8,128)(2,1)S(1)}, u32[]{:S(2)}, u32[]{:S(2)}) collective-permute-start(bf16[17,16,128]{2,1,0:T(8,128)(2,1)S(1)} %get-tuple-element.17), channel_id=1, source_target_pairs={{32,0},{64,32},{96,64},{128,96},{160,128},{192,160},{224,192},{0,2... | collective-permute-start | bytes 208904 | tf_op jit(solution)/shard_map/ppermute | solution.py:223
  38.7 1.7 %collective-permute-done.1 = bf16[17,16,128]{2,1,0:T(8,128)(2,1)S(1)} collective-permute-done((bf16[17,16,128]{2,1,0:T(8,128)(2,1)S(1)}, bf16[17,16,128]{2,1,0:T(8,128)(2,1)S(1)}, u32[]{:S(2)}, u32[]{:S(2)}) %collective-permute-start.1) | collective-permute-done | bytes 69664 | tf_op jit(solution)/shard_map/ppermute | solution.py:223
  40.4 0.0 collective-permute-start.2
  40.4 2.7 %collective-permute-start.4 = (bf16[17,16,128]{2,1,0:T(8,128)(2,1)S(1)}, bf16[17,16,128]{2,1,0:T(8,128)(2,1)S(1)}, u32[]{:S(2)}, u32[]{:S(2)}) collective-permute-start(bf16[17,16,128]{2,1,0:T(8,128)(2,1)S(1)} %collective-permute-done.3), channel_id=1, source_target_pairs={{32,0},{64,32},{96,64},{128,96},{160,128},{192,160},{224,192},{0,2... | collective-permute-start | bytes 208904 | tf_op jit(solution)/shard_map/ppermute | solution.py:223
  43.2 1.9 %collective-permute-done.2 = bf16[17,16,128]{2,1,0:T(8,128)(2,1)S(1)} collective-permute-done((bf16[17,16,128]{2,1,0:T(8,128)(2,1)S(1)}, bf16[17,16,128]{2,1,0:T(8,128)(2,1)S(1)}, u32[]{:S(2)}, u32[]{:S(2)}) %collective-permute-start.2) | collective-permute-done | bytes 69664 | tf_op jit(solution)/shard_map/ppermute | solution.py:223
  45.1 4.6 %collective-permute-start.5 = (bf16[6,17,16,128]{3,2,1,0:T(8,128)(2,1)S(1)}, bf16[6,17,16,128]{3,2,1,0:T(8,128)(2,1)S(1)}, u32[]{:S(2)}, u32[]{:S(2)}) collective-permute-start(bf16[6,17,16,128]{3,2,1,0:T(8,128)(2,1)S(1)} %bitcast_dynamic-update-slice_fusion.own), channel_id=1, source_target_pairs={{1,0},{0,1},{3,2},{2,3},{5,4},{4,5},{7,6},{6,7},{9,8},{8,9},{11,10... | collective-permute-start | bytes 1253384 | tf_op jit(solution)/shard_map/ppermute | solution.py:223
  49.7 3.0 %collective-permute-start.7 = (bf16[17,16,128]{2,1,0:T(8,128)(2,1)S(1)}, bf16[17,16,128]{2,1,0:T(8,128)(2,1)S(1)}, u32[]{:S(2)}, u32[]{:S(2)}) collective-permute-start(bf16[17,16,128]{2,1,0:T(8,128)(2,1)S(1)} %collective-permute-done.4), channel_id=1, source_target_pairs={{32,0},{64,32},{96,64},{128,96},{160,128},{192,160},{224,192},{0,2... | collective-permute-start | bytes 208904 | tf_op jit(solution)/shard_map/ppermute | solution.py:223
  52.7 3.5 %shard_map.49 = (f32[6,16,256]{2,1,0:T(8,128)S(1)}, f32[256,128]{1,0:T(8,128)S(1)}) custom-call(bf16[16,17,16,128]{3,2,1,0:T(8,128)(2,1)S(1)} %all-to-all-done.1.rows, bf16[6,17,16,128]{3,2,1,0:T(8,128)(2,1)S(1)} %bitcast_dynamic-update-slice_fusion.own), custom_call_target="tpu_custom_call" | custom-call | flops 1610612736 | bytes 2097152 | tf_op jit(solution)/shard_map/pallas_call | solution.py:272
  56.2 2.3 %collective-permute-start.8 = (bf16[2,17,16,128]{3,2,1,0:T(8,128)(2,1)S(1)}, bf16[2,17,16,128]{3,2,1,0:T(8,128)(2,1)S(1)}, u32[]{:S(2)}, u32[]{:S(2)}) collective-permute-start(bf16[2,17,16,128]{3,2,1,0:T(8,128)(2,1)S(1)} %pad_maximum_fusion.own), channel_id=1, source_target_pairs={{1,0},{0,1},{3,2},{2,3},{5,4},{4,5},{7,6},{6,7},{9,8},{8,9},{11,10... | collective-permute-start | bytes 417800 | tf_op jit(solution)/shard_map/ppermute | solution.py:223
  58.5 1.3 %shard_map.50.late_ratio = f32[2,16,256]{2,1,0:T(8,128)S(1)} custom-call(bf16[16,17,16,128]{3,2,1,0:T(8,128)(2,1)S(1)} %all-to-all-done.1.rows, bf16[2,17,16,128]{3,2,1,0:T(8,128)(2,1)S(1)} %pad_maximum_fusion.own, f32[256,128]{1,0:T(8,128)S(1)} %get-tuple-element.18.row_codes), custom_call_target="tpu_custom_call" | custom-call | flops 536870912 | bytes 2097152 | tf_op jit(solution)/shard_map/pallas_call | solution.py:287
  59.8 2.7 %shard_map.52 = f32[4,2,32,128]{3,2,1,0:T(8,128)S(1)} custom-call(bf16[16,17,16,128]{3,2,1,0:T(8,128)(2,1)S(1)} %all-to-all-done.1.rows, f32[256,128]{1,0:T(8,128)S(1)} %get-tuple-element.18.row_codes, bf16[6,17,16,128]{3,2,1,0:T(8,128)(2,1)S(1)} %collective-permute-done.5.early, bf16[2,17,16,128]{3,2,1,0:T(8,128)(2,1)S(1)} %collective-permute-done.8.late, ...), custom_call_target="tpu_custom_call" | custom-call | flops 1073741824 | bytes 2097152 | tf_op jit(solution)/shard_map/pallas_call | solution.py:298
  62.6 0.1 collective-permute-start.9
  62.7 2.7 %shard_map.51 = f32[4,2,32,128]{3,2,1,0:T(8,128)S(1)} custom-call(bf16[16,17,16,128]{3,2,1,0:T(8,128)(2,1)S(1)} %all-to-all-done.1.rows, f32[256,128]{1,0:T(8,128)S(1)} %get-tuple-element.18.row_codes, bf16[6,17,16,128]{3,2,1,0:T(8,128)(2,1)S(1)} %collective-permute-done.5.early, bf16[2,17,16,128]{3,2,1,0:T(8,128)(2,1)S(1)} %collective-permute-done.8.late, ...), custom_call_target="tpu_custom_call" | custom-call | flops 1073741824 | bytes 2097152 | tf_op jit(solution)/shard_map/pallas_call | solution.py:298
  65.5 12.7 %all_to_all.15 = f32[16,32,128]{2,1,0:T(8,128)S(1)} all-to-all(f32[16,32,128]{2,1,0:T(8,128)S(1)} %bitcast.21), channel_id=1, replica_groups=mesh['z'=8,'yl'=2,'x'=4,'yh'=2,'c'=2] {'x','yh','yl'}, dimensions={0} | all-to-all | bytes 524288 | tf_op jit(solution)/shard_map/all_to_all | solution.py:317
  78.2 1.3 %shard_map.53 = f32[64,1024]{1,0:T(8,128)} custom-call(f32[4,2,2,32,128]{4,3,2,1,0:T(8,128)S(1)} %bitcast.19), custom_call_target="tpu_custom_call" | custom-call | tf_op jit(solution)/shard_map/pallas_call | solution.py:320
  (20 shorter events, 0.2 us)
Async XLA Ops:
  0.0 15.8 %copy-start = (s32[64]{0:T(128)S(1)}, s32[64]{0:T(128)}, u32[]{:S(2)}) copy-start(s32[64]{0:T(128)} %counts_in.1) | copy-start | bytes 772
  2.3 24.5 %all-to-all-start = ((bf16[64,9,2,128]{3,2,1,0:T(2,128)(2,1)}), bf16[64,9,2,128]{3,2,1,0:T(2,128)(2,1)S(1)}, u32[]{:S(2)}, u32[]{:S(2)}) async-start(bf16[64,9,2,128]{3,2,1,0:T(2,128)(2,1)} %shard_map.47), calls=%async_computation | async-start | bytes 589824 | tf_op jit(solution)/shard_map/all_to_all | solution.py:251
  28.4 7.5 %collective-permute-start = (bf16[17,16,128]{2,1,0:T(8,128)(2,1)S(1)}, bf16[17,16,128]{2,1,0:T(8,128)(2,1)S(1)}, u32[]{:S(2)}, u32[]{:S(2)}) collective-permute-start(bf16[17,16,128]{2,1,0:T(8,128)(2,1)S(1)} %get-tuple-element.17), channel_id=1, source_target_pairs={{224,0},{0,32},{32,64},{64,96},{96,128},{128,160},{160,192},{192,2... | collective-permute-start | bytes 208904 | tf_op jit(solution)/shard_map/ppermute | solution.py:223
  29.4 23.3 %all-to-all-start.1 = ((bf16[16,17,16,128]{3,2,1,0:T(8,128)(2,1)}), bf16[16,17,16,128]{3,2,1,0:T(8,128)(2,1)S(1)}, u32[]{:S(2)}, u32[]{:S(2)}) async-start(bf16[16,17,16,128]{3,2,1,0:T(8,128)(2,1)} %get-tuple-element.14), calls=%async_computation.1 | async-start | bytes 2228224 | tf_op jit(solution)/shard_map/all_to_all | solution.py:263
  35.9 4.4 %collective-permute-start.1 = (bf16[17,16,128]{2,1,0:T(8,128)(2,1)S(1)}, bf16[17,16,128]{2,1,0:T(8,128)(2,1)S(1)}, u32[]{:S(2)}, u32[]{:S(2)}) collective-permute-start(bf16[17,16,128]{2,1,0:T(8,128)(2,1)S(1)} %collective-permute-done), channel_id=1, source_target_pairs={{224,0},{0,32},{32,64},{64,96},{96,128},{128,160},{160,192},{192,2... | collective-permute-start | bytes 208904 | tf_op jit(solution)/shard_map/ppermute | solution.py:223
  36.5 3.9 %collective-permute-start.3 = (bf16[17,16,128]{2,1,0:T(8,128)(2,1)S(1)}, bf16[17,16,128]{2,1,0:T(8,128)(2,1)S(1)}, u32[]{:S(2)}, u32[]{:S(2)}) collective-permute-start(bf16[17,16,128]{2,1,0:T(8,128)(2,1)S(1)} %get-tuple-element.17), channel_id=1, source_target_pairs={{32,0},{64,32},{96,64},{128,96},{160,128},{192,160},{224,192},{0,2... | collective-permute-start | bytes 208904 | tf_op jit(solution)/shard_map/ppermute | solution.py:223
  40.4 4.7 %collective-permute-start.2 = (bf16[17,16,128]{2,1,0:T(8,128)(2,1)S(1)}, bf16[17,16,128]{2,1,0:T(8,128)(2,1)S(1)}, u32[]{:S(2)}, u32[]{:S(2)}) collective-permute-start(bf16[17,16,128]{2,1,0:T(8,128)(2,1)S(1)} %collective-permute-done.1), channel_id=1, source_target_pairs={{224,0},{0,32},{32,64},{64,96},{96,128},{128,160},{160,192},{192,2... | collective-permute-start | bytes 208904 | tf_op jit(solution)/shard_map/ppermute | solution.py:223
  40.4 4.7 %collective-permute-start.4 = (bf16[17,16,128]{2,1,0:T(8,128)(2,1)S(1)}, bf16[17,16,128]{2,1,0:T(8,128)(2,1)S(1)}, u32[]{:S(2)}, u32[]{:S(2)}) collective-permute-start(bf16[17,16,128]{2,1,0:T(8,128)(2,1)S(1)} %collective-permute-done.3), channel_id=1, source_target_pairs={{32,0},{64,32},{96,64},{128,96},{160,128},{192,160},{224,192},{0,2... | collective-permute-start | bytes 208904 | tf_op jit(solution)/shard_map/ppermute | solution.py:223
  45.1 14.7 %collective-permute-start.5 = (bf16[6,17,16,128]{3,2,1,0:T(8,128)(2,1)S(1)}, bf16[6,17,16,128]{3,2,1,0:T(8,128)(2,1)S(1)}, u32[]{:S(2)}, u32[]{:S(2)}) collective-permute-start(bf16[6,17,16,128]{3,2,1,0:T(8,128)(2,1)S(1)} %bitcast_dynamic-update-slice_fusion.own), channel_id=1, source_target_pairs={{1,0},{0,1},{3,2},{2,3},{5,4},{4,5},{7,6},{6,7},{9,8},{8,9},{11,10... | collective-permute-start | bytes 1253384 | tf_op jit(solution)/shard_map/ppermute | solution.py:223
  49.7 6.5 %collective-permute-start.6 = (bf16[17,16,128]{2,1,0:T(8,128)(2,1)S(1)}, bf16[17,16,128]{2,1,0:T(8,128)(2,1)S(1)}, u32[]{:S(2)}, u32[]{:S(2)}) collective-permute-start(bf16[17,16,128]{2,1,0:T(8,128)(2,1)S(1)} %collective-permute-done.2), channel_id=1, source_target_pairs={{224,0},{0,32},{32,64},{64,96},{96,128},{128,160},{160,192},{192,2... | collective-permute-start | bytes 208904 | tf_op jit(solution)/shard_map/ppermute | solution.py:223
  49.7 6.5 %collective-permute-start.7 = (bf16[17,16,128]{2,1,0:T(8,128)(2,1)S(1)}, bf16[17,16,128]{2,1,0:T(8,128)(2,1)S(1)}, u32[]{:S(2)}, u32[]{:S(2)}) collective-permute-start(bf16[17,16,128]{2,1,0:T(8,128)(2,1)S(1)} %collective-permute-done.4), channel_id=1, source_target_pairs={{32,0},{64,32},{96,64},{128,96},{160,128},{192,160},{224,192},{0,2... | collective-permute-start | bytes 208904 | tf_op jit(solution)/shard_map/ppermute | solution.py:223
  56.2 3.6 %collective-permute-start.8 = (bf16[2,17,16,128]{3,2,1,0:T(8,128)(2,1)S(1)}, bf16[2,17,16,128]{3,2,1,0:T(8,128)(2,1)S(1)}, u32[]{:S(2)}, u32[]{:S(2)}) collective-permute-start(bf16[2,17,16,128]{3,2,1,0:T(8,128)(2,1)S(1)} %pad_maximum_fusion.own), channel_id=1, source_target_pairs={{1,0},{0,1},{3,2},{2,3},{5,4},{4,5},{7,6},{6,7},{9,8},{8,9},{11,10... | collective-permute-start | bytes 417800 | tf_op jit(solution)/shard_map/ppermute | solution.py:223
  62.6 2.9 %collective-permute-start.9 = (f32[4,2,32,128]{3,2,1,0:T(8,128)S(1)}, f32[4,2,32,128]{3,2,1,0:T(8,128)S(1)}, u32[]{:S(2)}, u32[]{:S(2)}) collective-permute-start(f32[4,2,32,128]{3,2,1,0:T(8,128)S(1)} %shard_map.52), channel_id=1, source_target_pairs={{1,0},{0,1},{3,2},{2,3},{5,4},{4,5},{7,6},{6,7},{9,8},{8,9},{11,10... | collective-permute-start | bytes 393224 | tf_op jit(solution)/shard_map/ppermute | solution.py:223
